TPU v7x, 32 devices: a whole 2x2x4 slice. The times are simulated.
32 devices in a mesh: dp: 8 (over z, core), tensor: 4 (over y, x).
Axes of the slice: x: 2, y: 2, z: 4, core: 2. Of those that a mesh axis runs over, the one named last changes fastest.
Arguments:
- inputs: bfloat16 [16384, 2048], P(('dp', 'tensor')), may hold values from -6 to 6
- input_projection_weight: float32 [2048, 8, 512], P('dp', 'tensor'), may hold values from -0.125 to 0.125
- input_first_moment: float32 [2048, 8, 512], P('dp', 'tensor'), may hold values from -320 to 320
- input_second_moment: float32 [2048, 8, 512], P('dp', 'tensor'), may hold values from 1064.96 to 16384
- out_weight: float32 [2048, 2048], P('tensor', 'dp'), may hold values from -0.375 to 0.375
- out_mean: float32 [2048, 2048], P('tensor', 'dp'), may hold values from -320 to 320
- out_square: float32 [2048, 2048], P('tensor', 'dp'), may hold values from 1064.96 to 16384
- swiglu_weight: float32 [2048, 2, 6144], P('dp', None, 'tensor'), may hold values from -0.125 to 0.125
- swiglu_mean: float32 [2048, 2, 6144], P('dp', None, 'tensor'), may hold values from -320 to 320
- swiglu_square: float32 [2048, 2, 6144], P('dp', None, 'tensor'), may hold values from 1064.96 to 16384
- down_weight: float32 [6144, 2048], P('tensor', 'dp'), may hold values from -0.078125 to 0.078125
- down_mean: float32 [6144, 2048], P('tensor', 'dp'), may hold values from -448 to 448
- down_square: float32 [6144, 2048], P('tensor', 'dp'), may hold values from 2457.6 to 39321.6
- norm_gains: float32 [2, 2048], replicated, may hold values from 0.5 to 1.5
- norm_mean: float32 [2, 2048], replicated, may hold values from -512 to 512
- norm_square: float32 [2, 2048], replicated, may hold values from 3276.8 to 52428.8
- qknorm_gains: float32 [2, 128], replicated, may hold values from 0.5 to 1.5
- qknorm_mean: float32 [2, 128], replicated, may hold values from -896 to 896
- qknorm_square: float32 [2, 128], replicated, may hold values from 9699.328 to 157286.4
- cotangent: bfloat16 [16384, 2048], P(('dp', 'tensor')), may hold values from -8 to 8
Outputs:
- outputs: bfloat16 [16384, 2048], P(('dp', 'tensor'))
- input_grad: bfloat16 [16384, 2048], P(('dp', 'tensor'))
- in_grad: float32 [2048, 8, 512], P('dp', 'tensor')
- in_new: float32 [2048, 8, 512], P('dp', 'tensor')
- in_second: float32 [2048, 8, 512], P('dp', 'tensor')
- out_grad: float32 [2048, 2048], P('tensor', 'dp')
- out_new: float32 [2048, 2048], P('tensor', 'dp')
- out_second: float32 [2048, 2048], P('tensor', 'dp')
- swiglu_grad: float32 [2048, 2, 6144], P('dp', None, 'tensor')
- swiglu_new: float32 [2048, 2, 6144], P('dp', None, 'tensor')
- swiglu_second: float32 [2048, 2, 6144], P('dp', None, 'tensor')
- down_grad: float32 [6144, 2048], P('tensor', 'dp')
- down_new: float32 [6144, 2048], P('tensor', 'dp')
- down_second: float32 [6144, 2048], P('tensor', 'dp')
- norm_grad: float32 [2, 2048], replicated
- norm_new: float32 [2, 2048], replicated
- norm_second: float32 [2, 2048], replicated
- qknorm_grad: float32 [2, 128], replicated
- qknorm_new: float32 [2, 128], replicated
- qknorm_second: float32 [2, 128], replicated
All inputs are finite; a program needn't handle non-finite values.
Results may differ from a plain program's by a relative error of at most 0.015.
Values may be sent and summed in bfloat16 or wider, within the bound.
No kernel may reach another device: no remote copies, remote signals or barrier semaphores. Data moves between devices by JAX's collectives and lax.ppermute only.
A program may use at most 320 MiB of HBM per device.

v0:
```python
import jax
import jax.numpy as jnp
from jax import lax
from jax.sharding import PartitionSpec as P

MODEL_WIDTH = 2048
HQ = 16
HEAD_WIDTH = 128
FF = 6144
QUERY_PER_KEY = 2
SEQUENCE_TOKENS = 2048


norm_eps = 1e-06
rope_base = 1000000.0
beta_one = 0.5
beta_two = 0.55
step_count = 5.0
adam_eps = 1e-08
decay_rate = 0.1
gain_rate = 0.3
masked_score = -1e30


def rms_gain(values, gain_row):
    return (
        values * lax.rsqrt(jnp.mean(values * values, axis=-1, keepdims=True) + norm_eps) * gain_row
    )


def rotary_tables(row_total, length, width):
    positions = (jnp.arange(row_total, dtype=jnp.int32) % length).astype(jnp.float32)
    frequency = rope_base ** (
        -2.0 * jnp.arange(width // 2, dtype=jnp.int32).astype(jnp.float32) / width
    )
    angles = positions[:, None] * frequency[None, :]
    return (jnp.cos(angles), jnp.sin(angles))


def rotate(values, cos_table, sin_table):
    half_width = values.shape[-1] // 2
    table_shape = (cos_table.shape[0],) + (1,) * (values.ndim - 2) + (half_width,)
    cos_rows = cos_table.reshape(table_shape)
    sin_rows = sin_table.reshape(table_shape)
    first_half = values[..., :half_width]
    second_half = values[..., half_width:]
    return jnp.concatenate(
        [
            first_half * cos_rows - second_half * sin_rows,
            second_half * cos_rows + first_half * sin_rows,
        ],
        axis=-1,
    )


def masked_scores(query_block, key_block, offset, score_scale):
    scores = (
        jnp.einsum("qhgd,khd->hgqk", query_block, key_block, preferred_element_type=jnp.float32)
        * score_scale
    )
    query_pos = offset + jnp.arange(query_block.shape[0], dtype=jnp.int32)
    key_pos = jnp.arange(key_block.shape[0], dtype=jnp.int32)
    return jnp.where(key_pos[None, :] <= query_pos[:, None], scores, masked_score)


def add_rows(totals, addend):
    return totals + addend


def contract_rows(left, right):
    return lax.dot_general(
        left, right, (((0,), (0,)), ((), ())), preferred_element_type=jnp.float32
    )


def contract_cols(left, right):
    return lax.dot_general(
        left, right, (((1,), (1,)), ((), ())), preferred_element_type=jnp.float32
    )


def adamw(weight, gradient, mean_old, square_old, rate):
    mean_new = beta_one * mean_old + (1.0 - beta_one) * gradient
    square_new = beta_two * square_old + (1.0 - beta_two) * gradient * gradient
    mean_hat = mean_new / (1.0 - beta_one**step_count)
    square_hat = square_new / (1.0 - beta_two**step_count)
    weight_new = weight - rate * (
        mean_hat / (jnp.sqrt(square_hat) + adam_eps) + decay_rate * weight
    )
    return (weight_new, square_new)


def local(
    inputs,
    input_projection_weight,
    input_first_moment,
    input_second_moment,
    out_weight,
    out_mean,
    out_square,
    swiglu_weight,
    swiglu_mean,
    swiglu_square,
    down_weight,
    down_mean,
    down_square,
    norm_gains,
    norm_mean,
    norm_square,
    qknorm_gains,
    qknorm_mean,
    qknorm_square,
    cotangent,
):
    local_rows = inputs.shape[0]
    group_rows = local_rows * lax.axis_size("tensor")
    local_kv = input_projection_weight.shape[1]
    local_heads = local_kv * QUERY_PER_KEY
    local_ff = swiglu_weight.shape[2]
    block_rows = min(512, SEQUENCE_TOKENS)
    block_count = group_rows // block_rows
    per_sequence = SEQUENCE_TOKENS // block_rows
    score_scale = HEAD_WIDTH ** (-0.5)
    in_low = input_projection_weight.astype(jnp.bfloat16)
    out_low = out_weight.astype(jnp.bfloat16)
    swiglu_low = swiglu_weight.astype(jnp.bfloat16)
    down_low = down_weight.astype(jnp.bfloat16)
    in_full, out_full = (
        lax.all_gather(in_low, "dp", axis=0, tiled=True),
        lax.all_gather(out_low, "dp", axis=1, tiled=True),
    )
    in_matrix = in_full.reshape(MODEL_WIDTH, local_kv * (QUERY_PER_KEY + 2) * HEAD_WIDTH)
    inputs_f = inputs.astype(jnp.float32)
    normed_f, norm_one_back = jax.vjp(rms_gain, inputs_f, norm_gains[0])
    normalized_rows = normed_f.astype(jnp.bfloat16)
    normed_all = lax.all_gather(normalized_rows, "tensor", axis=0, tiled=True)
    mixed_precision = jnp.dot(normed_all, in_matrix, preferred_element_type=jnp.float32).reshape(
        group_rows, local_kv, QUERY_PER_KEY + 2, HEAD_WIDTH
    )
    cos_table, sin_table = rotary_tables(group_rows, SEQUENCE_TOKENS, HEAD_WIDTH)

    def rotate_both(query_in, key_in, gains_in):
        return (
            rotate(rms_gain(query_in, gains_in[0]), cos_table, sin_table),
            rotate(rms_gain(key_in, gains_in[1]), cos_table, sin_table),
        )

    (query_rot, key_rot), rotate_back = jax.vjp(
        rotate_both,
        mixed_precision[:, :, :QUERY_PER_KEY],
        mixed_precision[:, :, QUERY_PER_KEY],
        qknorm_gains,
    )
    query_rows = query_rot.astype(jnp.bfloat16)
    key_rows = key_rot.astype(jnp.bfloat16)
    value_rows = mixed_precision[:, :, QUERY_PER_KEY + 1].astype(jnp.bfloat16)

    def attend(block_index):
        key_start = block_index // per_sequence * SEQUENCE_TOKENS
        row_start = block_index * block_rows
        query_block = lax.dynamic_slice_in_dim(query_rows, row_start, block_rows, 0)
        scores = masked_scores(query_block, key_rows, row_start - key_start, score_scale)
        row_max = jnp.max(scores, axis=-1, keepdims=True)
        shifted = jnp.exp(scores - row_max)
        denom_sum = jnp.sum(shifted, axis=-1, keepdims=True)
        attention = (shifted / denom_sum).astype(jnp.bfloat16)
        context_block = jnp.einsum(
            "hgqk,khd->qhgd", attention, value_rows, preferred_element_type=jnp.float32
        )
        return (context_block.astype(jnp.bfloat16), row_max + jnp.log(denom_sum))

    contexts, log_sums = lax.map(attend, jnp.arange(block_count, dtype=jnp.int32))
    context = contexts.reshape(group_rows, local_heads * HEAD_WIDTH)
    row_slice = context
    attended = lax.psum_scatter(
        jnp.dot(row_slice, out_full, preferred_element_type=jnp.float32),
        "tensor",
        scatter_dimension=0,
        tiled=True,
    )
    hidden = inputs_f + attended
    normed_two_f, norm_two_back = jax.vjp(rms_gain, hidden, norm_gains[1])
    normed_two = normed_two_f.astype(jnp.bfloat16)
    swiglu_full, down_full = (
        lax.all_gather(swiglu_low, "dp", axis=0, tiled=True),
        lax.all_gather(down_low, "dp", axis=1, tiled=True),
    )
    swiglu_matrix = swiglu_full.reshape(MODEL_WIDTH, 2 * local_ff)
    normed_two_all = lax.all_gather(normed_two, "tensor", axis=0, tiled=True)
    gate_up = jnp.dot(normed_two_all, swiglu_matrix, preferred_element_type=jnp.float32)
    gate_part = gate_up[:, :local_ff]
    up_part = gate_up[:, local_ff:]
    activated = (jax.nn.silu(gate_part) * up_part).astype(jnp.bfloat16)
    row_slice = activated
    projected = lax.psum_scatter(
        jnp.dot(row_slice, down_full, preferred_element_type=jnp.float32),
        "tensor",
        scatter_dimension=0,
        tiled=True,
    )
    outputs = (hidden + projected).astype(jnp.bfloat16)
    in_back, out_back, swiglu_back, down_back = (
        lax.all_gather(in_low, "dp", axis=0, tiled=True),
        lax.all_gather(out_low, "dp", axis=1, tiled=True),
        lax.all_gather(swiglu_low, "dp", axis=0, tiled=True),
        lax.all_gather(down_low, "dp", axis=1, tiled=True),
    )
    in_matrix_back = in_back.reshape(MODEL_WIDTH, local_kv * (QUERY_PER_KEY + 2) * HEAD_WIDTH)
    swiglu_matrix_back = swiglu_back.reshape(MODEL_WIDTH, 2 * local_ff)
    cot_all = lax.all_gather(cotangent, "tensor", axis=0, tiled=True)
    down_grad_full = contract_rows(activated, cot_all)
    activated_grad = contract_cols(cot_all, down_back)
    sigmoid_gate = jax.nn.sigmoid(gate_part)
    gate_grad = activated_grad * up_part * sigmoid_gate * (1.0 + gate_part * (1.0 - sigmoid_gate))
    up_grad = activated_grad * gate_part * sigmoid_gate
    gate_up_grad = jnp.concatenate([gate_grad, up_grad], axis=1).astype(jnp.bfloat16)
    swiglu_grad_full = contract_rows(normed_two_all, gate_up_grad).reshape(MODEL_WIDTH, 2, local_ff)
    row_slice = gate_up_grad
    normed_two_grad = lax.psum_scatter(
        contract_cols(row_slice, swiglu_matrix_back), "tensor", scatter_dimension=0, tiled=True
    )
    hidden_norm_grad, mlp_gain_grad = norm_two_back(normed_two_grad)
    hidden_grad = cotangent.astype(jnp.float32) + hidden_norm_grad
    swiglu_grad, down_grad = (swiglu_grad_full, down_grad_full)
    attended_grad = hidden_grad.astype(jnp.bfloat16)
    attended_all = lax.all_gather(attended_grad, "tensor", axis=0, tiled=True)
    out_grad_full = contract_rows(context, attended_all)
    context_grad = (
        contract_cols(attended_all, out_back)
        .astype(jnp.bfloat16)
        .reshape(group_rows, local_kv, QUERY_PER_KEY, HEAD_WIDTH)
    )

    def attend_back(totals, block_index):
        key_grads, value_grads = totals
        key_start = block_index // per_sequence * SEQUENCE_TOKENS
        row_start = block_index * block_rows
        query_block = lax.dynamic_slice_in_dim(query_rows, row_start, block_rows, 0)
        grad_block = lax.dynamic_slice_in_dim(context_grad, row_start, block_rows, 0)
        scores = masked_scores(query_block, key_rows, row_start - key_start, score_scale)
        attention = jnp.exp(scores - log_sums[block_index])
        prob_grad = jnp.einsum(
            "qhgd,khd->hgqk", grad_block, value_rows, preferred_element_type=jnp.float32
        )
        value_part = jnp.einsum(
            "hgqk,qhgd->khd",
            attention.astype(jnp.bfloat16),
            grad_block,
            preferred_element_type=jnp.float32,
        )
        row_dot = jnp.sum(attention * prob_grad, axis=-1, keepdims=True)
        score_grad = (attention * (prob_grad - row_dot)).astype(jnp.bfloat16)
        query_grad = (
            jnp.einsum("hgqk,khd->qhgd", score_grad, key_rows, preferred_element_type=jnp.float32)
            * score_scale
        )
        key_part = (
            jnp.einsum(
                "hgqk,qhgd->khd", score_grad, query_block, preferred_element_type=jnp.float32
            )
            * score_scale
        )
        return ((add_rows(key_grads, key_part), add_rows(value_grads, value_part)), query_grad)

    start_totals = (
        jnp.zeros((group_rows, local_kv, HEAD_WIDTH), jnp.float32),
        jnp.zeros((group_rows, local_kv, HEAD_WIDTH), jnp.float32),
    )
    (key_grads, value_grads), query_grads = lax.scan(
        attend_back, start_totals, jnp.arange(block_count, dtype=jnp.int32)
    )
    query_grads = query_grads.reshape(group_rows, local_kv, QUERY_PER_KEY, HEAD_WIDTH)
    query_pre_grad, key_pre_grad, qknorm_part = rotate_back((query_grads, key_grads))
    mixed_grad = jnp.concatenate(
        [query_pre_grad, key_pre_grad[:, :, None], value_grads[:, :, None]], axis=2
    )
    mixed_grad = mixed_grad.astype(jnp.bfloat16).reshape(
        group_rows, local_kv * (QUERY_PER_KEY + 2) * HEAD_WIDTH
    )
    in_grad_full = contract_rows(normed_all, mixed_grad).reshape(
        MODEL_WIDTH, local_kv, (QUERY_PER_KEY + 2) * HEAD_WIDTH
    )
    row_slice = mixed_grad
    normed_grad = lax.psum_scatter(
        contract_cols(row_slice, in_matrix_back), "tensor", scatter_dimension=0, tiled=True
    )
    input_norm_grad, attn_gain_grad = norm_one_back(normed_grad)
    input_grad = (hidden_grad + input_norm_grad).astype(jnp.bfloat16)
    norm_grad, qknorm_grad = lax.psum(
        (jnp.stack([attn_gain_grad, mlp_gain_grad]), qknorm_part), ("dp", "tensor")
    )
    in_grad, out_grad, swiglu_grad, down_grad = (
        lax.psum_scatter(in_grad_full, "dp", scatter_dimension=0, tiled=True),
        lax.psum_scatter(out_grad_full, "dp", scatter_dimension=1, tiled=True),
        lax.psum_scatter(swiglu_grad, "dp", scatter_dimension=0, tiled=True),
        lax.psum_scatter(down_grad, "dp", scatter_dimension=1, tiled=True),
    )
    in_new, in_second = adamw(
        input_projection_weight,
        in_grad,
        input_first_moment,
        input_second_moment,
        MODEL_WIDTH ** (-0.5),
    )
    out_new, out_second = adamw(
        out_weight, out_grad, out_mean, out_square, (HQ * HEAD_WIDTH / 8.0) ** (-0.5)
    )
    swiglu_new, swiglu_second = adamw(
        swiglu_weight, swiglu_grad, swiglu_mean, swiglu_square, MODEL_WIDTH ** (-0.5)
    )
    down_new, down_second = adamw(down_weight, down_grad, down_mean, down_square, FF ** (-0.5))
    norm_new, norm_second = adamw(norm_gains, norm_grad, norm_mean, norm_square, gain_rate)
    qknorm_new, qknorm_second = adamw(
        qknorm_gains, qknorm_grad, qknorm_mean, qknorm_square, gain_rate
    )
    return (
        outputs,
        input_grad,
        in_grad,
        in_new,
        in_second,
        out_grad,
        out_new,
        out_second,
        swiglu_grad,
        swiglu_new,
        swiglu_second,
        down_grad,
        down_new,
        down_second,
        norm_grad,
        norm_new,
        norm_second,
        qknorm_grad,
        qknorm_new,
        qknorm_second,
    )


def solution(mesh):
    return jax.shard_map(
        local,
        mesh=mesh,
        in_specs=(
            P(("dp", "tensor"), None),
            P("dp", "tensor", None),
            P("dp", "tensor", None),
            P("dp", "tensor", None),
            P("tensor", "dp"),
            P("tensor", "dp"),
            P("tensor", "dp"),
            P("dp", None, "tensor"),
            P("dp", None, "tensor"),
            P("dp", None, "tensor"),
            P("tensor", "dp"),
            P("tensor", "dp"),
            P("tensor", "dp"),
            P(),
            P(),
            P(),
            P(),
            P(),
            P(),
            P(("dp", "tensor"), None),
        ),
        out_specs=(
            P(("dp", "tensor"), None),
            P(("dp", "tensor"), None),
            P("dp", "tensor", None),
            P("dp", "tensor", None),
            P("dp", "tensor", None),
            P("tensor", "dp"),
            P("tensor", "dp"),
            P("tensor", "dp"),
            P("dp", None, "tensor"),
            P("dp", None, "tensor"),
            P("dp", None, "tensor"),
            P("tensor", "dp"),
            P("tensor", "dp"),
            P("tensor", "dp"),
            P(),
            P(),
            P(),
            P(),
            P(),
            P(),
        ),
        check_vma=False,
    )
```

profile of v0, /device:TPU:0, one launch (start us, length us, event | category | flops | bytes accessed | tf_op | source)
XLA Modules:
  0.0 2209.1 jit_solution(10189911346163746460)
XLA Ops:
  18.0 42.2 %all-gather.11.cloned.1.call-done = bf16[2048,2,512]{2,1,0:T(2,128)(2,1)} async-done(((bf16[256,2,512]{2,1,0:T(2,128)(2,1)}), bf16[2048,2,512]{2,1,0:T(2,128)(2,1)}) %all-gather.11.cloned.1.call-update) | async-done | bytes 4194320 | tf_op jit(solution)/shard_map/all_gather | solution.py:129
  72.1 76.7 %all-gather.9.cloned.1.call-done = bf16[2048,2048]{1,0:T(8,128)(2,1)} async-done(((bf16[512,2048]{1,0:T(8,128)(2,1)}), bf16[2048,2048]{1,0:T(8,128)(2,1)}) %all-gather.9.cloned.1.call-update) | async-done | bytes 8388624 | tf_op jit(solution)/shard_map/all_gather | solution.py:136
  179.7 85.5 %while.31 = (s32[]{:T(128)}, bf16[4,512,2,2,128]{4,3,2,1,0:T(2,128)(2,1)}, f32[4,2,2,512,1]{3,2,1,4,0:T(2,128)}, s32[4]{0:T(128)S(1)}, bf16[2048,2,2,128]{3,0,2,...) while((s32[]{:T(128)}, ...), condition=%wide.region_6.7_spmd, body=%wide.region_3.6_spmd.sunk | while | flops 2199124480 | bytes 58790276 | solution.py:172
  287.1 149.2 %reduce-scatter.8.cloned.1.call-done = f32[512,2048]{1,0:T(8,128)} async-done(((f32[2048,2048]{1,0:T(8,128)}), f32[512,2048]{1,0:T(8,128)}) %reduce-scatter.8.cloned.1.call-update) | async-done | bytes 4194320 | tf_op jit(solution)/shard_map/reduce_scatter | solution.py:175
  444.7 110.4 %all-gather.17.cloned.1.call-done = bf16[2048,2,1536]{2,1,0:T(2,128)(2,1)} async-done(((bf16[256,2,1536]{2,1,0:T(2,128)(2,1)}), bf16[2048,2,1536]{2,1,0:T(2,128)(2,1)}) %all-gather.17.cloned.1.call-update) | async-done | bytes 12582928 | tf_op jit(solution)/shard_map/all_gather | solution.py:185
  568.1 75.2 %all-gather.15.cloned.1.call-done = bf16[2048,2048]{1,0:T(8,128)(2,1)} async-done(((bf16[512,2048]{1,0:T(8,128)(2,1)}), bf16[2048,2048]{1,0:T(8,128)(2,1)}) %all-gather.15.cloned.1.call-update) | async-done | bytes 8388624 | tf_op jit(solution)/shard_map/all_gather | solution.py:189
  643.3 34.0 %fusion.91 = f32[2048,3072]{1,0:T(8,128)} fusion(bf16[2048,2048]{1,0:T(8,128)(2,1)} %all-gather.15.cloned.1.call-done, bf16[2048,3072]{1,0:T(8,128)(2,1)} %bitcast.226), kind=kOutput, calls=%fused_computation.171 | convolution fusion | flops 25769803776 | bytes 46137344 | tf_op jit(solution)/shard_map/dot_general | solution.py:190
  677.2 33.4 %all-gather.19.cloned.1.call-done = bf16[1536,2048]{1,0:T(8,128)(2,1)} async-done(((bf16[1536,256]{1,0:T(8,128)(2,1)}), bf16[1536,2048]{1,0:T(8,128)(2,1)}) %all-gather.19.cloned.1.call-update) | async-done | bytes 6291472 | tf_op jit(solution)/shard_map/all_gather | solution.py:186
  710.6 87.7 %all-gather.21.cloned.1.call-done = bf16[2048,2048]{1,0:T(8,128)(2,1)} async-done(((bf16[512,2048]{1,0:T(8,128)(2,1)}), bf16[2048,2048]{1,0:T(8,128)(2,1)}) %all-gather.21.cloned.1.call-update) | async-done | bytes 8388624 | tf_op jit(solution)/shard_map/all_gather | solution.py:210
  798.3 30.2 %multiply_convert_fusion.1 = (bf16[2048,1536]{1,0:T(8,128)(2,1)}, bf16[2048,1536]{1,0:T(8,128)(2,1)}, bf16[2048,1536]{1,0:T(8,128)(2,1)}) fusion(f32[2048,3072]{1,0:T(8,128)} %fusion.91, bf16[2048,2048]{1,0:T(8,128)(2,1)} %all-gather.21.cloned.1.call-done, bf16[1536,2048]{1,0:T(8,128)(2,1)} %all-gather.19.cloned.1.call-done), kind=kOutput, calls=%fused_computation.58 | convolution fusion | flops 12935233536 | bytes 58720256 | tf_op jit(solution)/shard_map/dot_general | solution.py:77
  828.5 34.3 %fusion.50 = f32[2048,2048]{1,0:T(8,128)} fusion(bf16[2048,3072]{1,0:T(8,128)(2,1)} %bitcast.227, bf16[2048,1536]{1,0:T(8,128)(2,1)} %get-tuple-element.450, bf16[2048,1536]{1,0:T(8,128)(2,1)} %get-tuple-element.449), kind=kOutput, calls=%fused_computation.72 | convolution fusion | flops 25794969600 | bytes 41943040 | tf_op jit(solution)/shard_map/dot_general | solution.py:77
  863.3 153.5 %reduce-scatter.12.cloned.1.call-done = f32[512,2048]{1,0:T(8,128)} async-done(((f32[2048,2048]{1,0:T(8,128)}), f32[512,2048]{1,0:T(8,128)}) %reduce-scatter.12.cloned.1.call-update) | async-done | bytes 4194320 | tf_op jit(solution)/shard_map/reduce_scatter | solution.py:219
  1025.4 34.0 %fusion.49 = f32[2048,3072]{1,0:T(8,128)} fusion(bf16[2048,2048]{1,0:T(8,128)(2,1)} %all-gather.15.cloned.1.call-done, bf16[2048,1536]{1,0:T(8,128)(2,1)} %get-tuple-element.450, bf16[2048,1536]{1,0:T(8,128)(2,1)} %get-tuple-element.449), kind=kOutput, calls=%fused_computation.71 | convolution fusion | flops 25794969600 | bytes 46137344 | tf_op jit(solution)/shard_map/dot_general | solution.py:71
  1059.4 32.5 %reshape.316 = f32[2048,2,1536]{2,1,0:T(2,128)} reshape(f32[2048,3072]{1,0:T(8,128)} %fusion.49) | data formatting | bytes 50331648 | tf_op jit(solution)/shard_map/reshape | solution.py:217
  1133.4 323.3 %while.32 = (s32[]{:T(128)}, f32[2048,2,128]{0,2,1:T(8,128)}, f32[2048,2,128]{0,2,1:T(8,128)}, f32[4,512,2,2,128]{1,0,4,3,2:T(4,128)}, s32[4]{0:T(128)S(1)}, /*i...) while((s32[]{:T(128)}, f32[2048,2,128]{0,2,1:T(8,128)}, ...), condition=%wide.region_14.15_spmd.clone, body=%wide.region_12.14_spmd.clone.sunk | while | flops 5435554304 | bytes 232845856 | solution.py:269
  1354.3 21.3 dynamic_update_slice.29
  1435.1 21.2 dynamic_update_slice.29
  1524.9 81.3 %all-reduce.10.cloned.1.call-done = f32[2048,2,1536]{2,1,0:T(2,128)} async-done(((f32[2048,2,1536]{2,1,0:T(2,128)}), f32[2048,2,1536]{2,1,0:T(2,128)}) %all-reduce.10.cloned.1.call-update) | async-done | bytes 25165840
  1621.5 116.9 %reduce-scatter.20.cloned.1.call-done = f32[1536,256]{1,0:T(8,128)} async-done(((f32[1536,2048]{1,0:T(8,128)}), f32[1536,256]{1,0:T(8,128)}) %reduce-scatter.20.cloned.1.call-update) | async-done | bytes 1572880 | tf_op jit(solution)/shard_map/reduce_scatter | solution.py:296
  1743.9 45.7 %reduce-scatter.18.cloned.1.call-done = f32[512,256]{1,0:T(8,128)} async-done(((f32[512,2048]{1,0:T(8,128)}), f32[512,256]{1,0:T(8,128)}) %reduce-scatter.18.cloned.1.call-update) | async-done | bytes 524304 | tf_op jit(solution)/shard_map/reduce_scatter | solution.py:294
  1792.1 87.4 %reduce-scatter.16.cloned.1.call-done = f32[256,2,512]{2,0,1:T(8,128)} async-done(((f32[2048,2,512]{2,0,1:T(8,128)}), f32[256,2,512]{2,0,1:T(8,128)}) %reduce-scatter.16.cloned.1.call-update) | async-done | bytes 1048592 | tf_op jit(solution)/shard_map/reduce_scatter | solution.py:293
  1887.6 147.1 %reduce-scatter.14.cloned.1.call-done = f32[512,2048]{1,0:T(8,128)} async-done(((f32[2048,2048]{1,0:T(8,128)}), f32[512,2048]{1,0:T(8,128)}) %reduce-scatter.14.cloned.1.call-update) | async-done | bytes 4194320 | tf_op jit(solution)/shard_map/reduce_scatter | solution.py:284
  2038.3 40.0 %all-reduce.7 = (f32[2,2048]{1,0:T(2,128)S(1)}, f32[2,128]{1,0:T(2,128)S(1)}) all-reduce(f32[2,2048]{1,0:T(2,128)S(1)} %pad_maximum_fusion.5, f32[2,128]{1,0:T(2,128)S(1)} %pad_add_fusion.2), channel_id=1, replica_groups=mesh['dp'=8,'tensor'=4] {'dp','tensor'}, use_global_device_ids=true, to_apply=%region_25.26 | all-reduce | flops 4352 | bytes 34816 | tf_op jit(solution)/shard_map/psum | solution.py:289
  2079.6 113.0 %reduce-scatter.10.cloned.1.call-done = f32[512,2048]{1,0:T(8,128)} async-done(((f32[2048,2048]{1,0:T(8,128)}), f32[512,2048]{1,0:T(8,128)}) %reduce-scatter.10.cloned.1.call-update) | async-done | bytes 4194320 | tf_op jit(solution)/shard_map/reduce_scatter | solution.py:195
  (360 shorter events, 593.9 us)
Async XLA Ops:
  7.2 52.9 %all-gather.11.cloned.1.call-start = ((), (), s32[]{:S(2)}) async-start(), calls=%async_computation.8 | async-start | bytes 4718592 | tf_op jit(solution)/shard_map/all_gather | solution.py:129
  9.8 139.0 %all-gather.9.cloned.1.call-start = ((), (), s32[]{:S(2)}) async-start(), calls=%async_computation.7 | async-start | bytes 10485760 | tf_op jit(solution)/shard_map/all_gather | solution.py:136
  15.1 254.6 %all-gather.13.cloned.1.call-start = ((), (), s32[]{:S(2)}) async-start(), calls=%async_computation.9 | async-start | bytes 2359296 | tf_op jit(solution)/shard_map/all_gather | solution.py:130
  15.9 420.3 %reduce-scatter.8.cloned.1.call-start = ((), (), s32[]{:S(2)}) async-start(), calls=%async_computation.10 | async-start | bytes 20971520 | tf_op jit(solution)/shard_map/reduce_scatter | solution.py:175
  282.3 272.8 %all-gather.17.cloned.1.call-start = ((), (), s32[]{:S(2)}) async-start(), calls=%async_computation.12 | async-start | bytes 14155776 | tf_op jit(solution)/shard_map/all_gather | solution.py:185
  286.6 356.6 %all-gather.15.cloned.1.call-start = ((), (), s32[]{:S(2)}) async-start(), calls=%async_computation.11 | async-start | bytes 10485760 | tf_op jit(solution)/shard_map/all_gather | solution.py:189
  442.9 267.7 %all-gather.19.cloned.1.call-start = ((), (), s32[]{:S(2)}) async-start(), calls=%async_computation.13 | async-start | bytes 7077888 | tf_op jit(solution)/shard_map/all_gather | solution.py:186
  443.9 354.3 %all-gather.21.cloned.1.call-start = ((), (), s32[]{:S(2)}) async-start(), calls=%async_computation.15 | async-start | bytes 10485760 | tf_op jit(solution)/shard_map/all_gather | solution.py:210
  444.7 572.2 %reduce-scatter.12.cloned.1.call-start = ((), (), s32[]{:S(2)}) async-start(), calls=%async_computation.16 | async-start | bytes 20971520 | tf_op jit(solution)/shard_map/reduce_scatter | solution.py:219
  862.9 250.3 %all-gather.23.cloned.1.call-start = ((), (), s32[]{:S(2)}) async-start(), calls=%async_computation.17 | async-start | bytes 10485760 | tf_op jit(solution)/shard_map/all_gather | solution.py:226
  1025.4 580.8 %all-reduce.10.cloned.1.call-start = ((), (), s32[]{:S(2)}) async-start(), calls=%async_computation.22 | async-start | bytes 50331648
  1092.0 646.4 %reduce-scatter.20.cloned.1.call-start = ((), (), s32[]{:S(2)}) async-start(), calls=%async_computation.21 | async-start | bytes 14155776 | tf_op jit(solution)/shard_map/reduce_scatter | solution.py:296
  1111.2 678.4 %reduce-scatter.18.cloned.1.call-start = ((), (), s32[]{:S(2)}) async-start(), calls=%async_computation.20 | async-start | bytes 4718592 | tf_op jit(solution)/shard_map/reduce_scatter | solution.py:294
  1122.7 756.8 %reduce-scatter.16.cloned.1.call-start = ((), (), s32[]{:S(2)}) async-start(), calls=%async_computation.19 | async-start | bytes 9437184 | tf_op jit(solution)/shard_map/reduce_scatter | solution.py:293
  1487.6 547.1 %reduce-scatter.14.cloned.1.call-start = ((), (), s32[]{:S(2)}) async-start(), calls=%async_computation.18 | async-start | bytes 20971520 | tf_op jit(solution)/shard_map/reduce_scatter | solution.py:284
  1503.3 689.2 %reduce-scatter.10.cloned.1.call-start = ((), (), s32[]{:S(2)}) async-start(), calls=%async_computation.14 | async-start | bytes 20971520 | tf_op jit(solution)/shard_map/reduce_scatter | solution.py:195
  1621.4 258.1 %copy-start.23 = (f32[256,2,512]{2,1,0:T(2,128)S(1)}, f32[256,2,512]{2,1,0:T(2,128)}, u32[]{:S(2)}) copy-start(f32[256,2,512]{2,1,0:T(2,128)} %param.25) | copy-start | bytes 3145732
  1621.5 258.1 %copy-start.29 = (f32[256,2,512]{2,1,0:T(2,128)S(1)}, f32[256,2,512]{2,1,0:T(2,128)}, u32[]{:S(2)}) copy-start(f32[256,2,512]{2,1,0:T(2,128)} %param.27) | copy-start | bytes 3145732
  1885.7 193.1 %copy-start.45 = (f32[2,2048]{1,0:T(2,128)S(1)}, f32[2,2048]{1,0:T(2,128)}, u32[]{:S(2)}) copy-start(f32[2,2048]{1,0:T(2,128)} %param.37) | copy-start | bytes 49156
  1885.7 193.1 %copy-start.58 = (f32[2,2048]{1,0:T(2,128)S(1)}, f32[2,2048]{1,0:T(2,128)}, u32[]{:S(2)}) copy-start(f32[2,2048]{1,0:T(2,128)} %param.38) | copy-start | bytes 49156
  1885.8 193.1 %copy-start.59 = (f32[2,2048]{1,0:T(2,128)S(1)}, f32[2,2048]{1,0:T(2,128)}, u32[]{:S(2)}) copy-start(f32[2,2048]{1,0:T(2,128)} %param.39) | copy-start | bytes 49156
  1885.8 306.8 %copy-start.39 = (f32[1,2048]{1,0:T(1,128)S(1)}, f32[1,2048]{1,0:T(1,128)}, u32[]{:S(2)}) copy-start(f32[1,2048]{1,0:T(1,128)} %get-tuple-element.464) | copy-start | bytes 24580
  1885.8 306.7 %copy-start.48 = (f32[512]{0:T(512)S(1)}, f32[512]{0:T(512)}, u32[]{:S(2)}) copy-start(f32[512]{0:T(512)} %copy-done.46) | copy-start | bytes 6148
  1885.8 306.7 %copy-start.53 = (f32[512]{0:T(512)S(1)}, f32[512]{0:T(512)}, u32[]{:S(2)}) copy-start(f32[512]{0:T(512)} %copy-done.52) | copy-start | bytes 6148
  (77 other events, 3904.8 us)
Sparse Core Ops, SparseCore 0:
  10.2 49.8 all-gather.10
  62.6 86.1 all-gather.8
  151.0 30.8 all-gather.12
  282.4 153.8 reduce-scatter.7
  438.4 116.7 all-gather.16
  557.4 85.8 all-gather.14
  645.4 65.1 all-gather.18
  712.5 85.7 all-gather.20
  863.0 153.8 reduce-scatter.11
  1025.5 87.5 all-gather.22
  1115.6 490.4 all-reduce.9
  1608.9 129.3 reduce-scatter.19
  1741.2 48.3 reduce-scatter.17
  1791.7 87.7 reduce-scatter.15
  1882.5 152.2 reduce-scatter.13
  2037.6 154.8 reduce-scatter.9
where the time goes:
time: 2220 us; the launch traced here: 2210 us
  waiting for transfers between devices  1320 us (59%)
  matrix products  408 us (18%)
  local copies, waits for them, and re-layouts  230 us (10%)
  other arithmetic  160 us (7%)
  blocking collectives  40 us (2%)
  loops' own time  32.4 us (1%)
    reduce_scatter x1, waiting for transfers between devices, local(): lax.psum_scatter(contract_cols(row_slice, swiglu_matrix_back), 'tensor',...  154 us
    reduce_scatter x1, waiting for transfers between devices, local(): lax.psum_scatter(jnp.dot(row_slice, out_full, preferred_element_type=jnp....  149 us
    reduce_scatter x1, waiting for transfers between devices, local(): lax.psum_scatter(contract_cols(row_slice, in_matrix_back), 'tensor', scat...  147 us
    reduce_scatter x1, waiting for transfers between devices, local(): lax.psum_scatter(down_grad, 'dp', scatter_dimension=1, tiled=True)  117 us
    reduce_scatter x1, waiting for transfers between devices, local(): lax.psum_scatter(jnp.dot(row_slice, down_full, preferred_element_type=jnp...  113 us
    all_gather x1, waiting for transfers between devices, local(): lax.all_gather(swiglu_low, 'dp', axis=0, tiled=True)  110 us
    dynamic_update_slice x8, local copies, waits for them, and re-layouts, local(): lax.scan(attend_back, start_totals, jnp.arange(block_count, dtype=jnp.int...  99.9 us
    dot_general x4, matrix products, contract_cols(): lax.dot_general(left, right, (((1,), (1,)), ((), ())), preferred_element_...  89.3 us
  transfers between devices with their start and end apart: 16, of which 15 were waited for; matrix products, arithmetic and copies ran while one was open for 30% of the time, Pallas kernels for 0%

commit v1 on v0

v1 whole, which is shorter than its diff:
```python
import jax
import jax.numpy as jnp
from jax import lax
from jax.experimental import pallas as pl
from jax.experimental.pallas import tpu as pltpu
from jax.sharding import PartitionSpec as P

MODEL_WIDTH = 2048
HQ = 16
HEAD_WIDTH = 128
FF = 6144
QUERY_PER_KEY = 2
SEQUENCE_TOKENS = 2048


norm_eps = 1e-06
rope_base = 1000000.0
beta_one = 0.5
beta_two = 0.55
step_count = 5.0
adam_eps = 1e-08
decay_rate = 0.1
gain_rate = 0.3
masked_score = -1e30
log2_e = 1.4426950408889634


def rms_gain(values, gain_row):
    return (
        values * lax.rsqrt(jnp.mean(values * values, axis=-1, keepdims=True) + norm_eps) * gain_row
    )


def rotary_tables(row_total, length, width):
    positions = (jnp.arange(row_total, dtype=jnp.int32) % length).astype(jnp.float32)
    frequency = rope_base ** (
        -2.0 * jnp.arange(width // 2, dtype=jnp.int32).astype(jnp.float32) / width
    )
    angles = positions[:, None] * frequency[None, :]
    return (jnp.cos(angles), jnp.sin(angles))


def rotate(values, cos_table, sin_table):
    half_width = values.shape[-1] // 2
    table_shape = (cos_table.shape[0],) + (1,) * (values.ndim - 2) + (half_width,)
    cos_rows = cos_table.reshape(table_shape)
    sin_rows = sin_table.reshape(table_shape)
    first_half = values[..., :half_width]
    second_half = values[..., half_width:]
    return jnp.concatenate(
        [
            first_half * cos_rows - second_half * sin_rows,
            second_half * cos_rows + first_half * sin_rows,
        ],
        axis=-1,
    )


def contract_rows(left, right):
    return lax.dot_general(
        left, right, (((0,), (0,)), ((), ())), preferred_element_type=jnp.float32
    )


def contract_cols(left, right):
    return lax.dot_general(
        left, right, (((1,), (1,)), ((), ())), preferred_element_type=jnp.float32
    )


def product(left, right):
    return jnp.dot(left, right, preferred_element_type=jnp.float32)


def adamw(weight, gradient, mean_old, square_old, rate):
    mean_new = beta_one * mean_old + (1.0 - beta_one) * gradient
    square_new = beta_two * square_old + (1.0 - beta_two) * gradient * gradient
    mean_hat = mean_new / (1.0 - beta_one**step_count)
    square_hat = square_new / (1.0 - beta_two**step_count)
    weight_new = weight - rate * (
        mean_hat / (jnp.sqrt(square_hat) + adam_eps) + decay_rate * weight
    )
    return (weight_new, square_new)


def ring_place(index, size):
    return jnp.where(index < size // 2, index, size // 2 + size - 1 - index)


def ring_pairs(size):
    half = size // 2
    order = list(range(half)) + list(range(size - 1, half - 1, -1))
    ahead = [(order[r], order[(r + 1) % size]) for r in range(size)]
    return ahead, [(b, a) for a, b in ahead]


def ring_offsets(size):
    offsets = [0]
    for step in range(1, size // 2):
        offsets += [step, -step]
    return offsets + [size // 2]


def ring_gather(rows, size):
    ahead, back = ring_pairs(size)
    half = rows.shape[0] // 2
    slots = [rows]
    from_left = from_right = rows
    for _ in range(1, size // 2):
        from_left, from_right = (
            lax.ppermute(from_left, "tensor", ahead),
            lax.ppermute(from_right, "tensor", back),
        )
        slots += [from_right, from_left]
    low = lax.ppermute(from_left[:half], "tensor", ahead)
    high = lax.ppermute(from_right[half:], "tensor", back)
    return slots + [jnp.concatenate([low, high], axis=0)]


def ring_scatter(parts, size):
    ahead, back = ring_pairs(size)
    far = parts[-1]
    half = far.shape[0] // 2
    going_ahead = lax.ppermute(far[:half], "tensor", ahead)
    going_back = lax.ppermute(far[half:], "tensor", back)
    for step in range(size // 2 - 1, 0, -1):
        to_right, to_left = parts[2 * step - 1], parts[2 * step]
        if step == size // 2 - 1:
            to_right = jnp.concatenate(
                [(to_right[:half] + going_ahead.astype(jnp.float32)), to_right[half:]], axis=0
            )
            to_left = jnp.concatenate(
                [to_left[:half], to_left[half:] + going_back.astype(jnp.float32)], axis=0
            )
        else:
            to_right = to_right + going_ahead.astype(jnp.float32)
            to_left = to_left + going_back.astype(jnp.float32)
        going_ahead = lax.ppermute(to_right.astype(jnp.bfloat16), "tensor", ahead)
        going_back = lax.ppermute(to_left.astype(jnp.bfloat16), "tensor", back)
    if size == 2:
        return parts[0] + jnp.concatenate([going_ahead, going_back], axis=0).astype(jnp.float32)
    return parts[0] + going_ahead.astype(jnp.float32) + going_back.astype(jnp.float32)


def narrow_far(parts):
    return parts[:-1] + [parts[-1].astype(jnp.bfloat16)]


def attend_kernel(scale, query_ref, key_ref, value_ref, out_ref, log_ref):
    block = query_ref.shape[0]
    width = key_ref.shape[1]
    group = query_ref.shape[1] // width
    step = pl.program_id(2)
    below = lax.broadcasted_iota(jnp.int32, (block, block), 0) <= lax.broadcasted_iota(
        jnp.int32, (block, block), 1
    )
    queries = [query_ref[:, g * width : (g + 1) * width] for g in range(group)]

    def visit(start, carry, masked):
        keys = key_ref[pl.ds(start, block), :]
        values = value_ref[pl.ds(start, block), :]
        new = []
        for g in range(group):
            total, acc = carry[g]
            weights = jnp.exp2(contract_cols(keys, queries[g]) * (scale * log2_e))
            if masked:
                weights = jnp.where(below, weights, 0.0)
            total = total + jnp.sum(weights, axis=0, keepdims=True)
            acc = acc + contract_rows(values, weights.astype(jnp.bfloat16))
            new.append((total, acc))
        return tuple(new)

    start_carry = tuple(
        (jnp.zeros((1, block), jnp.float32), jnp.zeros((width, block), jnp.float32))
        for _ in range(group)
    )
    carry = lax.fori_loop(
        0, step, lambda j, c: visit(pl.multiple_of(j * block, block), c, False), start_carry
    )
    carry = visit(pl.multiple_of(step * block, block), carry, True)
    for g in range(group):
        total, acc = carry[g]
        out_ref[:, g * width : (g + 1) * width] = jnp.transpose(acc / total).astype(jnp.bfloat16)
        log_ref[0, 0, g : g + 1, :] = jnp.log2(total)


def attention_forward(query, key, value, block):
    rows = query.shape[0]
    heads = key.shape[1] // HEAD_WIDTH
    steps = SEQUENCE_TOKENS // block
    wide = QUERY_PER_KEY * HEAD_WIDTH
    sequences = rows // SEQUENCE_TOKENS
    area = heads * QUERY_PER_KEY * rows * SEQUENCE_TOKENS // 2
    kernel = lambda *refs: attend_kernel(HEAD_WIDTH ** (-0.5), *refs)
    return pl.pallas_call(
        kernel,
        grid=(heads, sequences, steps),
        in_specs=[
            pl.BlockSpec((block, wide), lambda h, s, i: (s * steps + i, h)),
            pl.BlockSpec((SEQUENCE_TOKENS, HEAD_WIDTH), lambda h, s, i: (s, h)),
            pl.BlockSpec((SEQUENCE_TOKENS, HEAD_WIDTH), lambda h, s, i: (s, h)),
        ],
        out_specs=[
            pl.BlockSpec((block, wide), lambda h, s, i: (s * steps + i, h)),
            pl.BlockSpec(
                (1, 1, QUERY_PER_KEY, block), lambda h, s, i: (h, s * steps + i, 0, 0)
            ),
        ],
        out_shape=[
            jax.ShapeDtypeStruct(query.shape, jnp.bfloat16),
            jax.ShapeDtypeStruct((heads, rows // block, QUERY_PER_KEY, block), jnp.float32),
        ],
        compiler_params=pltpu.CompilerParams(vmem_limit_bytes=48 * 1024 * 1024),
        cost_estimate=pl.CostEstimate(
            flops=8 * area * HEAD_WIDTH, bytes_accessed=8 * rows * wide * heads, transcendentals=area
        ),
        name="attend",
    )(query, key, value)


def attend_back_kernel(
    scale,
    query_ref,
    key_ref,
    value_ref,
    grad_ref,
    context_ref,
    log_ref,
    query_out,
    key_out,
    value_out,
):
    block = query_ref.shape[0]
    width = key_ref.shape[1]
    group = query_ref.shape[1] // width
    step = pl.program_id(2)
    below = lax.broadcasted_iota(jnp.int32, (block, block), 0) <= lax.broadcasted_iota(
        jnp.int32, (block, block), 1
    )

    @pl.when(step == 0)
    def _():
        key_out[...] = jnp.zeros_like(key_out)
        value_out[...] = jnp.zeros_like(value_out)

    queries, grads, logs, dots = [], [], [], []
    for g in range(group):
        cols = slice(g * width, (g + 1) * width)
        queries.append(query_ref[:, cols])
        grads.append(grad_ref[:, cols])
        logs.append(log_ref[0, 0, g : g + 1, :])
        both = grads[g].astype(jnp.float32) * context_ref[:, cols].astype(jnp.float32)
        dots.append(jnp.sum(jnp.transpose(both), axis=0, keepdims=True))

    def visit(start, carry, masked):
        rows = pl.ds(start, block)
        keys = key_ref[rows, :]
        values = value_ref[rows, :]
        new = []
        key_part = value_part = None
        for g in range(group):
            weights = jnp.exp2(contract_cols(keys, queries[g]) * (scale * log2_e) - logs[g])
            if masked:
                weights = jnp.where(below, weights, 0.0)
            slope = contract_cols(values, grads[g])
            score = (weights * (slope - dots[g])).astype(jnp.bfloat16)
            value_g = product(weights.astype(jnp.bfloat16), grads[g])
            key_g = product(score, queries[g])
            key_part = key_g if key_part is None else key_part + key_g
            value_part = value_g if value_part is None else value_part + value_g
            new.append(carry[g] + contract_rows(keys, score))
        key_out[rows, :] += key_part * scale
        value_out[rows, :] += value_part
        return tuple(new)

    carry = tuple(jnp.zeros((width, block), jnp.float32) for _ in range(group))
    carry = lax.fori_loop(
        0, step, lambda j, c: visit(pl.multiple_of(j * block, block), c, False), carry
    )
    carry = visit(pl.multiple_of(step * block, block), carry, True)
    for g in range(group):
        query_out[:, g * width : (g + 1) * width] = jnp.transpose(carry[g]) * scale


def attention_backward(query, key, value, grad, context, logs):
    rows = query.shape[0]
    block = logs.shape[-1]
    heads = key.shape[1] // HEAD_WIDTH
    steps = SEQUENCE_TOKENS // block
    wide = QUERY_PER_KEY * HEAD_WIDTH
    sequences = rows // SEQUENCE_TOKENS
    area = heads * QUERY_PER_KEY * rows * SEQUENCE_TOKENS // 2
    kernel = lambda *refs: attend_back_kernel(HEAD_WIDTH ** (-0.5), *refs)
    query_spec = pl.BlockSpec((block, wide), lambda h, s, i: (s * steps + i, h))
    key_spec = pl.BlockSpec((SEQUENCE_TOKENS, HEAD_WIDTH), lambda h, s, i: (s, h))
    return pl.pallas_call(
        kernel,
        grid=(heads, sequences, steps),
        in_specs=[
            query_spec,
            key_spec,
            key_spec,
            query_spec,
            query_spec,
            pl.BlockSpec((1, 1, QUERY_PER_KEY, block), lambda h, s, i: (h, s * steps + i, 0, 0)),
        ],
        out_specs=[query_spec, key_spec, key_spec],
        out_shape=[
            jax.ShapeDtypeStruct(query.shape, jnp.float32),
            jax.ShapeDtypeStruct(key.shape, jnp.float32),
            jax.ShapeDtypeStruct(key.shape, jnp.float32),
        ],
        compiler_params=pltpu.CompilerParams(vmem_limit_bytes=48 * 1024 * 1024),
        cost_estimate=pl.CostEstimate(
            flops=20 * area * HEAD_WIDTH,
            bytes_accessed=16 * rows * wide * heads,
            transcendentals=area,
        ),
        name="attend_back",
    )(query, key, value, grad, context, logs)


def pick(rows, place, block):
    return lax.dynamic_slice_in_dim(rows, place * block, block, 0)


def local(
    inputs,
    input_projection_weight,
    input_first_moment,
    input_second_moment,
    out_weight,
    out_mean,
    out_square,
    swiglu_weight,
    swiglu_mean,
    swiglu_square,
    down_weight,
    down_mean,
    down_square,
    norm_gains,
    norm_mean,
    norm_square,
    qknorm_gains,
    qknorm_mean,
    qknorm_square,
    cotangent,
):
    size = lax.axis_size("tensor")
    rows = inputs.shape[0]
    group_rows = rows * size
    dp_rows = input_projection_weight.shape[0]
    local_kv = input_projection_weight.shape[1]
    local_ff = swiglu_weight.shape[2]
    wide = QUERY_PER_KEY * HEAD_WIDTH
    offsets = ring_offsets(size)
    me = ring_place(lax.axis_index("tensor"), size)
    places = [ring_place((me + d + size) % size, size) for d in offsets]
    barrier = lax.optimization_barrier

    in_low = input_projection_weight.astype(jnp.bfloat16).reshape(dp_rows, -1)
    out_low = out_weight.astype(jnp.bfloat16)
    swiglu_low = swiglu_weight.astype(jnp.bfloat16).reshape(dp_rows, 2 * local_ff)
    down_low = down_weight.astype(jnp.bfloat16)
    in_matrix = lax.all_gather(in_low, "dp", axis=0, tiled=True)
    out_full = lax.all_gather(out_low, "dp", axis=1, tiled=True)
    swiglu_matrix = lax.all_gather(swiglu_low, "dp", axis=0, tiled=True)
    down_full = lax.all_gather(down_low, "dp", axis=1, tiled=True)

    inputs_f = inputs.astype(jnp.float32)
    normed_f, norm_one_back = jax.vjp(rms_gain, inputs_f, norm_gains[0])
    normed_slots = ring_gather(normed_f.astype(jnp.bfloat16), size)
    cotangent_sent, _ = barrier((cotangent, normed_slots[-1]))
    cot_slots = ring_gather(cotangent_sent, size)

    mixed = jnp.zeros((group_rows, in_matrix.shape[1]), jnp.float32)
    for place, slot in zip(places, normed_slots):
        mixed = lax.dynamic_update_slice_in_dim(
            mixed, product(slot, in_matrix), place * rows, 0
        )
    mixed = mixed.reshape(group_rows, local_kv, QUERY_PER_KEY + 2, HEAD_WIDTH)
    cos_table, sin_table = rotary_tables(group_rows, SEQUENCE_TOKENS, HEAD_WIDTH)

    def rotate_both(query_in, key_in, gains_in):
        return (
            rotate(rms_gain(query_in, gains_in[0]), cos_table, sin_table),
            rotate(rms_gain(key_in, gains_in[1]), cos_table, sin_table),
        )

    (query_rot, key_rot), rotate_back = jax.vjp(
        rotate_both, mixed[:, :, :QUERY_PER_KEY], mixed[:, :, QUERY_PER_KEY], qknorm_gains
    )
    query = query_rot.astype(jnp.bfloat16).reshape(group_rows, local_kv * wide)
    key = key_rot.astype(jnp.bfloat16).reshape(group_rows, local_kv * HEAD_WIDTH)
    value = mixed[:, :, QUERY_PER_KEY + 1].astype(jnp.bfloat16)
    value = value.reshape(group_rows, local_kv * HEAD_WIDTH)
    context, logs = attention_forward(query, key, value, 512)

    attended = ring_scatter(
        narrow_far([product(pick(context, place, rows), out_full) for place in places]), size
    )
    hidden = inputs_f + attended
    normed_two_f, norm_two_back = jax.vjp(rms_gain, hidden, norm_gains[1])
    two_slots = ring_gather(normed_two_f.astype(jnp.bfloat16), size)

    activated_slots, gate_up_slots = [], []
    for two, cot in zip(two_slots, cot_slots):
        gate_up = product(two, swiglu_matrix)
        gate_part, up_part = gate_up[:, :local_ff], gate_up[:, local_ff:]
        sigmoid_gate = jax.nn.sigmoid(gate_part)
        activated_slots.append((gate_part * sigmoid_gate * up_part).astype(jnp.bfloat16))
        activated_grad = contract_cols(cot, down_full)
        gate_grad = (
            activated_grad * up_part * sigmoid_gate * (1.0 + gate_part * (1.0 - sigmoid_gate))
        )
        up_grad = activated_grad * gate_part * sigmoid_gate
        gate_up_slots.append(
            jnp.concatenate([gate_grad, up_grad], axis=1).astype(jnp.bfloat16)
        )
    two_grad = ring_scatter(
        narrow_far([contract_cols(slot, swiglu_matrix) for slot in gate_up_slots]), size
    )
    hidden_norm_grad, mlp_gain_grad = norm_two_back(two_grad)
    hidden_grad = cotangent.astype(jnp.float32) + hidden_norm_grad
    attended_slots = ring_gather(hidden_grad.astype(jnp.bfloat16), size)

    cot_all = jnp.concatenate(cot_slots, axis=0)
    activated_all = jnp.concatenate(activated_slots, axis=0)
    down_part = contract_rows(activated_all, cot_all).astype(jnp.bfloat16)
    swiglu_part = contract_rows(
        jnp.concatenate(two_slots, axis=0), jnp.concatenate(gate_up_slots, axis=0)
    ).astype(jnp.bfloat16)
    swiglu_grad = lax.psum_scatter(swiglu_part, "dp", scatter_dimension=0, tiled=True)
    down_grad = lax.psum_scatter(down_part, "dp", scatter_dimension=1, tiled=True)

    projected_parts = narrow_far([product(slot, down_full) for slot in activated_slots])
    projected_parts[-1], _ = barrier((projected_parts[-1], attended_slots[-1]))
    projected = ring_scatter(projected_parts, size)
    outputs = (hidden + projected).astype(jnp.bfloat16)

    context_grad = jnp.zeros(context.shape, jnp.bfloat16)
    for place, slot in zip(places, attended_slots):
        context_grad = lax.dynamic_update_slice_in_dim(
            context_grad, contract_cols(slot, out_full).astype(jnp.bfloat16), place * rows, 0
        )
    context_ring = jnp.concatenate([pick(context, place, rows) for place in places], axis=0)
    out_part = contract_rows(context_ring, jnp.concatenate(attended_slots, axis=0))
    out_grad = lax.psum_scatter(
        out_part.astype(jnp.bfloat16), "dp", scatter_dimension=1, tiled=True
    )
    query_grad, key_grad, value_grad = attention_backward(
        query, key, value, context_grad, context, logs
    )
    query_pre, key_pre, qknorm_part = rotate_back(
        (
            query_grad.reshape(group_rows, local_kv, QUERY_PER_KEY, HEAD_WIDTH),
            key_grad.reshape(group_rows, local_kv, HEAD_WIDTH),
        )
    )
    mixed_grad = jnp.concatenate(
        [
            query_pre,
            key_pre[:, :, None],
            value_grad.reshape(group_rows, local_kv, 1, HEAD_WIDTH),
        ],
        axis=2,
    )
    mixed_grad = mixed_grad.astype(jnp.bfloat16).reshape(group_rows, -1)
    mixed_slots = [pick(mixed_grad, place, rows) for place in places]
    normed_grad = ring_scatter(
        narrow_far([contract_cols(slot, in_matrix) for slot in mixed_slots]), size
    )
    in_part = contract_rows(
        jnp.concatenate(normed_slots, axis=0), jnp.concatenate(mixed_slots, axis=0)
    )
    in_grad = lax.psum_scatter(
        in_part.astype(jnp.bfloat16), "dp", scatter_dimension=0, tiled=True
    )
    input_norm_grad, attn_gain_grad = norm_one_back(normed_grad)
    input_grad = (hidden_grad + input_norm_grad).astype(jnp.bfloat16)
    norm_grad, qknorm_grad = lax.psum(
        (jnp.stack([attn_gain_grad, mlp_gain_grad]), qknorm_part), ("dp", "tensor")
    )
    in_grad = in_grad.astype(jnp.float32).reshape(input_projection_weight.shape)
    out_grad = out_grad.astype(jnp.float32)
    swiglu_grad = swiglu_grad.astype(jnp.float32).reshape(swiglu_weight.shape)
    down_grad = down_grad.astype(jnp.float32)
    in_new, in_second = adamw(
        input_projection_weight,
        in_grad,
        input_first_moment,
        input_second_moment,
        MODEL_WIDTH ** (-0.5),
    )
    out_new, out_second = adamw(
        out_weight, out_grad, out_mean, out_square, (HQ * HEAD_WIDTH / 8.0) ** (-0.5)
    )
    swiglu_new, swiglu_second = adamw(
        swiglu_weight, swiglu_grad, swiglu_mean, swiglu_square, MODEL_WIDTH ** (-0.5)
    )
    down_new, down_second = adamw(down_weight, down_grad, down_mean, down_square, FF ** (-0.5))
    norm_new, norm_second = adamw(norm_gains, norm_grad, norm_mean, norm_square, gain_rate)
    qknorm_new, qknorm_second = adamw(
        qknorm_gains, qknorm_grad, qknorm_mean, qknorm_square, gain_rate
    )
    return (
        outputs,
        input_grad,
        in_grad,
        in_new,
        in_second,
        out_grad,
        out_new,
        out_second,
        swiglu_grad,
        swiglu_new,
        swiglu_second,
        down_grad,
        down_new,
        down_second,
        norm_grad,
        norm_new,
        norm_second,
        qknorm_grad,
        qknorm_new,
        qknorm_second,
    )


def solution(mesh):
    return jax.shard_map(
        local,
        mesh=mesh,
        in_specs=(
            P(("dp", "tensor"), None),
            P("dp", "tensor", None),
            P("dp", "tensor", None),
            P("dp", "tensor", None),
            P("tensor", "dp"),
            P("tensor", "dp"),
            P("tensor", "dp"),
            P("dp", None, "tensor"),
            P("dp", None, "tensor"),
            P("dp", None, "tensor"),
            P("tensor", "dp"),
            P("tensor", "dp"),
            P("tensor", "dp"),
            P(),
            P(),
            P(),
            P(),
            P(),
            P(),
            P(("dp", "tensor"), None),
        ),
        out_specs=(
            P(("dp", "tensor"), None),
            P(("dp", "tensor"), None),
            P("dp", "tensor", None),
            P("dp", "tensor", None),
            P("dp", "tensor", None),
            P("tensor", "dp"),
            P("tensor", "dp"),
            P("tensor", "dp"),
            P("dp", None, "tensor"),
            P("dp", None, "tensor"),
            P("dp", None, "tensor"),
            P("tensor", "dp"),
            P("tensor", "dp"),
            P("tensor", "dp"),
            P(),
            P(),
            P(),
            P(),
            P(),
            P(),
        ),
        check_vma=False,
    )
```

time: 2220 us -> 987 us (0.44)
  waiting for transfers between devices: 1320 us -> 379 us
  local copies, waits for them, and re-layouts: 230 us -> 81.1 us
  matrix products: 408 us -> 269 us
  other arithmetic: 160 us -> 78.8 us
  Pallas kernels: 0 us -> 57.2 us
  starting transfers between devices: 1.47 us -> 35.7 us
  loops' own time: 32.4 us -> 0 us
  blocking collectives: 40 us -> 64.9 us
    reduce_scatter x7 -> x4, waiting for transfers between devices: 813 us -> 0.03 us  [the longest x1 0.02 us: local(): lax.psum_scatter(out_part.astype(jnp.bfloat16), 'dp', scatter_dimension=1...]
    all_gather x8 -> x4, waiting for transfers between devices: 427 us -> 0.03 us  [the longest x1 0.02 us: local(): out_full = lax.all_gather(out_low, 'dp', axis=1, tiled=True)]
    ppermute x0 -> x32, waiting for transfers between devices: none -> 378 us  [the longest x4 95.8 us: ring_scatter(): going_back = lax.ppermute(to_left.astype(jnp.bfloat16), 'tensor', back)]
    dot_general x32 -> x16, matrix products: 244 us -> 89 us  [product(): return jnp.dot(left, right, preferred_element_type=jnp.float32)]
    dynamic_update_slice x12 -> x0, local copies, waits for them, and re-layouts: 105 us -> none  [the longest x8 99.9 us: local(): lax.scan(attend_back, start_totals, jnp.arange(block_count, dtype=jnp.int...]
    unnamed x17 -> x8, waiting for transfers between devices: 82.3 us -> 0.13 us
    convert_element_type x10 -> x2, other arithmetic: 63.2 us -> 2.82 us  [the longest x1 1.74 us: local(): in_low = input_projection_weight.astype(jnp.bfloat16).reshape(dp_rows, -1)]
    pallas_call x0 -> x2, Pallas kernels: none -> 57.2 us  [the longest x1 37.1 us: attention_backward(): pl.pallas_call(kernel, grid=(heads, sequences, steps), in_specs=[query_sp...]
  transfers between devices with their start and end apart: 16 -> 40, of which waited for: 15 -> 21; matrix products, arithmetic and copies ran while one was open for 30% -> 34% of each run, Pallas kernels for 0% -> 6%
where the time goes in v1:
time: 987 us; the launch traced here: 982 us
  waiting for transfers between devices  379 us (38%)
  matrix products  269 us (27%)
  local copies, waits for them, and re-layouts  81.1 us (8%)
  other arithmetic  78.8 us (8%)
  blocking collectives  64.9 us (7%)
  Pallas kernels  57.2 us (6%)
  starting transfers between devices  35.7 us (4%)
  between operations  16.1 us (2%)
    dot_general x16, matrix products, contract_cols(): lax.dot_general(left, right, (((1,), (1,)), ((), ())), preferred_element_...  104 us
    ppermute x4, waiting for transfers between devices, ring_scatter(): going_back = lax.ppermute(to_left.astype(jnp.bfloat16), 'tensor', back)  95.8 us
    dot_general x16, matrix products, product(): return jnp.dot(left, right, preferred_element_type=jnp.float32)  89 us
    ppermute x4, waiting for transfers between devices, ring_gather(): lax.ppermute(from_left, 'tensor', ahead)  88.1 us
    ppermute x4, waiting for transfers between devices, ring_gather(): lax.ppermute(from_right, 'tensor', back)  86.7 us
    dot_general x4, matrix products, contract_rows(): lax.dot_general(left, right, (((0,), (0,)), ((), ())), preferred_element_...  76.1 us
    psum x1, blocking collectives, local(): lax.psum((jnp.stack([attn_gain_grad, mlp_gain_grad]), qknorm_part), ('dp'...  64.9 us
    ppermute x4, waiting for transfers between devices, ring_scatter(): going_back = lax.ppermute(far[half:], 'tensor', back)  48.8 us
  transfers between devices with their start and end apart: 40, of which 21 were waited for; matrix products, arithmetic and copies ran while one was open for 34% of the time, Pallas kernels for 6%

profile of v1, /device:TPU:0, one launch (start us, length us, event | category | flops | bytes accessed | tf_op | source)
XLA Modules:
  0.0 981.9 jit_solution(17660619371680705926)
XLA Ops:
  22.9 44.6 %collective-permute-done.1 = bf16[512,2048]{1,0:T(8,128)(2,1)S(1)} collective-permute-done((bf16[512,2048]{1,0:T(8,128)(2,1)}, bf16[512,2048]{1,0:T(8,128)(2,1)S(1)}, u32[]{:S(2)}, u32[]{:S(2)}) %collective-permute-start.1) | collective-permute-done | bytes 2097184 | tf_op jit(solution)/shard_map/ppermute | solution.py:111
  78.2 13.9 %collective-permute-done.2 = bf16[256,2048]{1,0:T(8,128)(2,1)S(1)} collective-permute-done((bf16[256,2048]{1,0:T(8,128)(2,1)S(1)}, bf16[256,2048]{1,0:T(8,128)(2,1)S(1)}, u32[]{:S(2)}, u32[]{:S(2)}) %collective-permute-start.2) | collective-permute-done | bytes 1048608 | tf_op jit(solution)/shard_map/ppermute | solution.py:115
  128.8 20.0 %attend.1 = (bf16[2048,512]{1,0:T(8,128)(2,1)S(1)}, f32[2,4,2,512]{3,2,1,0:T(2,128)S(1)}) custom-call(bf16[2048,512]{1,0:T(8,128)(2,1)} %copy.60.refs_0_, bf16[2048,256]{1,0:T(8,128)(2,1)S(1)} %copy.61.refs_1_, bf16[2048,256]{1,0:T(8,128)(2,1)S(1)} %copy.62.refs_2_), custom_call_target="tpu_custom_call" | custom-call | flops 8589934592 | bytes 8388608 | tf_op jit(solution)/shard_map/attend/pallas_call | solution.py:195
  160.0 16.9 %collective-permute-done.6 = bf16[256,2048]{1,0:T(8,128)(2,1)S(1)} collective-permute-done((bf16[256,2048]{1,0:T(8,128)(2,1)S(1)}, bf16[256,2048]{1,0:T(8,128)(2,1)S(1)}, u32[]{:S(2)}, u32[]{:S(2)}) %collective-permute-start.6) | collective-permute-done | bytes 1048608 | tf_op jit(solution)/shard_map/ppermute | solution.py:125
  183.2 38.7 %collective-permute-done.7 = bf16[512,2048]{1,0:T(8,128)(2,1)S(1)} collective-permute-done((bf16[512,2048]{1,0:T(8,128)(2,1)S(1)}, bf16[512,2048]{1,0:T(8,128)(2,1)S(1)}, u32[]{:S(2)}, u32[]{:S(2)}) %collective-permute-start.7) | collective-permute-done | bytes 2097184 | tf_op jit(solution)/shard_map/ppermute | solution.py:139
  233.2 44.5 %collective-permute-done.8 = bf16[512,2048]{1,0:T(8,128)(2,1)S(1)} collective-permute-done((bf16[512,2048]{1,0:T(8,128)(2,1)S(1)}, bf16[512,2048]{1,0:T(8,128)(2,1)S(1)}, u32[]{:S(2)}, u32[]{:S(2)}) %collective-permute-start.8) | collective-permute-done | bytes 2097184 | tf_op jit(solution)/shard_map/ppermute | solution.py:112
  280.4 42.2 %collective-permute-done.12 = bf16[512,2048]{1,0:T(8,128)(2,1)S(1)} collective-permute-done((bf16[512,2048]{1,0:T(8,128)(2,1)S(1)}, bf16[512,2048]{1,0:T(8,128)(2,1)S(1)}, u32[]{:S(2)}, u32[]{:S(2)}) %collective-permute-start.12) | collective-permute-done | bytes 2097184 | tf_op jit(solution)/shard_map/ppermute | solution.py:112
  326.9 18.2 %collective-permute-done.11 = bf16[256,2048]{1,0:T(8,128)(2,1)S(1)} collective-permute-done((bf16[256,2048]{1,0:T(8,128)(2,1)S(1)}, bf16[256,2048]{1,0:T(8,128)(2,1)S(1)}, u32[]{:S(2)}, u32[]{:S(2)}) %collective-permute-start.11) | collective-permute-done | bytes 1048608 | tf_op jit(solution)/shard_map/ppermute | solution.py:116
  346.2 11.5 %fusion.78 = f32[512,3072]{1,0:T(8,128)} fusion(bf16[2048,3072]{1,0:T(8,128)(2,1)} %all-gather.9.cloned.1.call-done, bf16[256,2048]{1,0:T(8,128)(2,1)S(1)} %collective-permute-done.11, bf16[256,2048]{1,0:T(8,128)(2,1)} %collective-permute-done.10), kind=kOutput, calls=%fused_computation.137 | convolution fusion | flops 6446645248 | bytes 20971520 | tf_op jit(solution)/shard_map/dot_general | solution.py:72
  363.6 12.1 %multiply_convert_fusion.5 = (bf16[512,1536]{1,0:T(8,128)(2,1)}, bf16[512,1536]{1,0:T(8,128)(2,1)}, bf16[512,1536]{1,0:T(8,128)(2,1)}) fusion(f32[512,3072]{1,0:T(8,128)} %fusion.78, bf16[1536,2048]{1,0:T(8,128)(2,1)} %all-gather.11.cloned.1.call-done, bf16[256,2048]{1,0:T(8,128)(2,1)} %collective-permute-done.15, bf16[256,2048]{1,0:T(8,128)(2,1)} %collective-permute-done.14), kind=kOutput, calls=%fused_computation.90 | convolution fusion | flops 3238002688 | bytes 19398656 | tf_op jit(solution)/shard_map/dot_general | solution.py:66
  386.5 11.3 %fusion.142 = f32[512,3072]{1,0:T(8,128)} fusion(bf16[512,2048]{1,0:T(8,128)(2,1)S(1)} %copy-done.26, bf16[2048,3072]{1,0:T(8,128)(2,1)} %all-gather.9.cloned.1.call-done), kind=kOutput, calls=%fused_computation.279 | convolution fusion | flops 6442450944 | bytes 20971520 | tf_op jit(solution)/shard_map/dot_general | solution.py:72
  397.8 11.4 %fusion.140 = f32[512,3072]{1,0:T(8,128)} fusion(bf16[512,2048]{1,0:T(8,128)(2,1)S(1)} %collective-permute-done.8, bf16[2048,3072]{1,0:T(8,128)(2,1)} %all-gather.9.cloned.1.call-done), kind=kOutput, calls=%fused_computation.277 | convolution fusion | flops 6442450944 | bytes 20971520 | tf_op jit(solution)/shard_map/dot_general | solution.py:72
  475.5 18.1 %collective-permute-done.19 = bf16[512,2048]{1,0:T(8,128)(2,1)} collective-permute-done((bf16[512,2048]{1,0:T(8,128)(2,1)S(1)}, bf16[512,2048]{1,0:T(8,128)(2,1)}, u32[]{:S(2)}, u32[]{:S(2)}) %collective-permute-start.19) | collective-permute-done | bytes 2097184 | tf_op jit(solution)/shard_map/ppermute | solution.py:139
  495.7 14.3 %multiply_reduce_fusion.1 = (f32[2048]{0:T(1024)}, f32[512]{0:T(512)S(1)}, f32[512,2048]{1,0:T(8,128)}) fusion(f32[512,2048]{1,0:T(8,128)S(1)} %copy-done.7, f32[512]{0:T(512)S(1)} %copy-done.83, f32[2048]{0:T(1024)S(1)} %bitcast.127, bf16[512,2048]{1,0:T(8,128)(2,1)} %collective-permute-done.19, bf16[512,2048]{1,0:T(8,128)(2,1)} %copy-done.109, ...), kind=kOutput, calls=%fused_computation.54 | convolution fusion | flops 6459225600 | bytes 28332032 | tf_op jit(solution)/shard_map/dot_general | solution.py:66
  516.9 43.4 %collective-permute-done.20 = bf16[512,2048]{1,0:T(8,128)(2,1)S(1)} collective-permute-done((bf16[512,2048]{1,0:T(8,128)(2,1)S(1)}, bf16[512,2048]{1,0:T(8,128)(2,1)S(1)}, u32[]{:S(2)}, u32[]{:S(2)}) %collective-permute-start.20) | collective-permute-done | bytes 2097184 | tf_op jit(solution)/shard_map/ppermute | solution.py:111
  602.3 16.5 %convolution_convert_fusion = bf16[1536,2048]{1,0:T(8,128)(2,1)} fusion(bf16[2048,2048]{1,0:T(8,128)(2,1)S(1)} %copy-done.65, bf16[512,1536]{1,0:T(8,128)(2,1)} %get-tuple-element.76, bf16[512,1536]{1,0:T(8,128)(2,1)} %get-tuple-element.77, bf16[512,1536]{1,0:T(8,128)(2,1)S(1)} %copy-done.110, bf16[512,1536]{1,0:T(8,128)(2,1)} %get-tuple-element.75), kind=kOutput, calls=%fused_computation.22 | convolution fusion | flops 12913213440 | bytes 20971520 | tf_op jit(solution)/shard_map/dot_general | solution.py:60
  629.6 37.1 %attend_back.1 = (f32[2048,512]{1,0:T(8,128)}, f32[2048,256]{1,0:T(8,128)S(1)}, f32[2048,256]{1,0:T(8,128)}) custom-call(bf16[2048,512]{1,0:T(8,128)(2,1)} %copy.60.refs_0_, bf16[2048,256]{1,0:T(8,128)(2,1)S(1)} %copy-done.2, bf16[2048,256]{1,0:T(8,128)(2,1)S(1)} %copy-done.4, bf16[2048,512]{1,0:T(8,128)(2,1)} %copy-done.44, bf16[2048,512]{1,0:T(8,128)(2,1)} %copy-done, ...), custom_call_target="tpu_custom_call" | custom-call | flops 21474836480 | bytes 16777216 | tf_op jit(solution)/shard_map/attend_back/pallas_call | solution.py:296
  701.9 39.3 %fusion.16 = bf16[2048,3072]{1,0:T(8,128)(2,1)} fusion(bf16[2048,2048]{1,0:T(8,128)(2,1)} %constant_dynamic-update-slice_fusion.14, bf16[512,1536]{1,0:T(8,128)(2,1)} %get-tuple-element.71, bf16[512,1536]{1,0:T(8,128)(2,1)} %get-tuple-element.70, bf16[512,1536]{1,0:T(8,128)(2,1)} %copy-done.115, bf16[512,1536]{1,0:T(8,128)(2,1)} %copy-done.114, ...), kind=kOutput, calls=%fused_computation.16 | convolution fusion | flops 25876758528 | bytes 33554432 | tf_op jit(solution)/shard_map/dot_general | solution.py:60
  771.6 16.6 %collective-permute-done.30 = bf16[256,2048]{1,0:T(8,128)(2,1)S(1)} collective-permute-done((bf16[256,2048]{1,0:T(8,128)(2,1)S(1)}, bf16[256,2048]{1,0:T(8,128)(2,1)S(1)}, u32[]{:S(2)}, u32[]{:S(2)}) %collective-permute-start.30) | collective-permute-done | bytes 1048608 | tf_op jit(solution)/shard_map/ppermute | solution.py:125
  795.4 15.3 %collective-permute-done.26 = bf16[256,2048]{1,0:T(8,128)(2,1)S(1)} collective-permute-done((bf16[256,2048]{1,0:T(8,128)(2,1)S(1)}, bf16[256,2048]{1,0:T(8,128)(2,1)S(1)}, u32[]{:S(2)}, u32[]{:S(2)}) %collective-permute-start.26) | collective-permute-done | bytes 1048608 | tf_op jit(solution)/shard_map/ppermute | solution.py:125
  816.6 39.0 %collective-permute-done.31 = bf16[512,2048]{1,0:T(8,128)(2,1)S(1)} collective-permute-done((bf16[512,2048]{1,0:T(8,128)(2,1)S(1)}, bf16[512,2048]{1,0:T(8,128)(2,1)S(1)}, u32[]{:S(2)}, u32[]{:S(2)}) %collective-permute-start.31) | collective-permute-done | bytes 2097184 | tf_op jit(solution)/shard_map/ppermute | solution.py:139
  862.2 64.9 %all-reduce.6 = (f32[2,2048]{1,0:T(2,128)S(1)}, f32[2,128]{1,0:T(2,128)S(1)}) all-reduce(f32[2,2048]{1,0:T(2,128)S(1)} %pad_maximum_fusion.11, f32[2,128]{1,0:T(2,128)S(1)} %pad_add_fusion.2), channel_id=1, replica_groups=mesh['dp'=8,'tensor'=4] {'dp','tensor'}, use_global_device_ids=true, to_apply=%region_14.15 | all-reduce | flops 4352 | bytes 34816 | tf_op jit(solution)/shard_map/psum | solution.py:481
  928.5 13.2 %fusion.33 = (bf16[512,2048]{1,0:T(8,128)(2,1)}, bf16[512,2048]{1,0:T(8,128)(2,1)}) fusion(bf16[512,2048]{1,0:T(8,128)(2,1)S(1)} %copy-done.10, f32[512]{0:T(512)S(1)} %multiply_multiply_fusion.9, f32[2048]{0:T(1024)S(1)} %bitcast.132, f32[512]{0:T(512)S(1)} %copy-done.86, bf16[512,2048]{1,0:T(8,128)(2,1)} %copy-done.42, f32[512,2048]{1,0:T(8,128)} %get-tuple-element.119, ...), kind=kLoop, calls=%fused_computation.41 | loop fusion | flops 26214400 | bytes 33579008 | tf_op jit(solution)/shard_map/convert_element_type | solution.py:480
  962.6 12.3 %multiply_subtract_fusion = (f32[256,2,1536]{2,1,0:T(2,128)}, f32[256,2,1536]{2,1,0:T(2,128)}) fusion(f32[256,2,1536]{2,1,0:T(2,128)S(1)} %copy-done.21, f32[256,2,1536]{2,1,0:T(2,128)} %param.28, f32[256,2,1536]{2,1,0:T(2,128)} %reshape.296, f32[256,2,1536]{2,1,0:T(2,128)} %param.29), kind=kLoop, calls=%fused_computation.83 | loop fusion | flops 10223616 | bytes 18874368 | tf_op jit(solution)/shard_map/sub | solution.py:80
  (467 shorter events, 350.3 us)
Async XLA Ops:
  7.2 91.4 %all-gather.5.cloned.1.call-start = ((), (), s32[]{:S(2)}) async-start(), calls=%async_computation.4 | async-start | bytes 4718592 | tf_op jit(solution)/shard_map/all_gather | solution.py:365
  9.9 140.5 %all-gather.7.cloned.1.call-start = ((), (), s32[]{:S(2)}) async-start(), calls=%async_computation.5 | async-start | bytes 2359296 | tf_op jit(solution)/shard_map/all_gather | solution.py:366
  11.7 334.5 %all-gather.9.cloned.1.call-start = ((), (), s32[]{:S(2)}) async-start(), calls=%async_computation.6 | async-start | bytes 14155776 | tf_op jit(solution)/shard_map/all_gather | solution.py:367
  14.3 349.3 %all-gather.11.cloned.1.call-start = ((), (), s32[]{:S(2)}) async-start(), calls=%async_computation.7 | async-start | bytes 7077888 | tf_op jit(solution)/shard_map/all_gather | solution.py:368
  18.7 48.8 %collective-permute-start.1 = (bf16[512,2048]{1,0:T(8,128)(2,1)}, bf16[512,2048]{1,0:T(8,128)(2,1)S(1)}, u32[]{:S(2)}, u32[]{:S(2)}) collective-permute-start(bf16[512,2048]{1,0:T(8,128)(2,1)} %get-tuple-element.63), channel_id=1, source_target_pairs={{0,1},{1,3},{3,2},{2,0},{4,5},{5,7},{7,6},{6,4},{8,9},{9,11},{11,1... | collective-permute-start | bytes 6291464 | tf_op jit(solution)/shard_map/ppermute | solution.py:111
  21.7 49.6 %collective-permute-start = (bf16[512,2048]{1,0:T(8,128)(2,1)}, bf16[512,2048]{1,0:T(8,128)(2,1)}, u32[]{:S(2)}, u32[]{:S(2)}) collective-permute-start(bf16[512,2048]{1,0:T(8,128)(2,1)} %get-tuple-element.63), channel_id=1, source_target_pairs={{1,0},{3,1},{2,3},{0,2},{5,4},{7,5},{6,7},{4,6},{9,8},{11,9},{10,1... | collective-permute-start | bytes 6291464 | tf_op jit(solution)/shard_map/ppermute | solution.py:112
  22.8 919.0 %reduce-scatter.7.cloned.1.call-start = ((), (), s32[]{:S(2)}) async-start(), calls=%async_computation.9 | async-start | bytes 2359296 | tf_op jit(solution)/shard_map/reduce_scatter | solution.py:448
  229.1 48.6 %collective-permute-start.8 = (bf16[512,2048]{1,0:T(8,128)(2,1)S(1)}, bf16[512,2048]{1,0:T(8,128)(2,1)S(1)}, u32[]{:S(2)}, u32[]{:S(2)}) collective-permute-start(bf16[512,2048]{1,0:T(8,128)(2,1)S(1)} %get-tuple-element.54), channel_id=1, source_target_pairs={{1,0},{3,1},{2,3},{0,2},{5,4},{7,5},{6,7},{4,6},{9,8},{11,9},{10,1... | collective-permute-start | bytes 6291464 | tf_op jit(solution)/shard_map/ppermute | solution.py:112
  230.1 49.1 %collective-permute-start.9 = (bf16[512,2048]{1,0:T(8,128)(2,1)S(1)}, bf16[512,2048]{1,0:T(8,128)(2,1)S(1)}, u32[]{:S(2)}, u32[]{:S(2)}) collective-permute-start(bf16[512,2048]{1,0:T(8,128)(2,1)S(1)} %get-tuple-element.54), channel_id=1, source_target_pairs={{0,1},{1,3},{3,2},{2,0},{4,5},{5,7},{7,6},{6,4},{8,9},{9,11},{11,1... | collective-permute-start | bytes 6291464 | tf_op jit(solution)/shard_map/ppermute | solution.py:111
  231.1 91.5 %collective-permute-start.12 = (bf16[512,2048]{1,0:T(8,128)(2,1)S(1)}, bf16[512,2048]{1,0:T(8,128)(2,1)S(1)}, u32[]{:S(2)}, u32[]{:S(2)}) collective-permute-start(bf16[512,2048]{1,0:T(8,128)(2,1)S(1)} %copy-done.13), channel_id=1, source_target_pairs={{1,0},{3,1},{2,3},{0,2},{5,4},{7,5},{6,7},{4,6},{9,8},{11,9},{10,1... | collective-permute-start | bytes 6291464 | tf_op jit(solution)/shard_map/ppermute | solution.py:112
  232.1 92.6 %collective-permute-start.13 = (bf16[512,2048]{1,0:T(8,128)(2,1)S(1)}, bf16[512,2048]{1,0:T(8,128)(2,1)S(1)}, u32[]{:S(2)}, u32[]{:S(2)}) collective-permute-start(bf16[512,2048]{1,0:T(8,128)(2,1)S(1)} %copy-done.13), channel_id=1, source_target_pairs={{0,1},{1,3},{3,2},{2,0},{4,5},{5,7},{7,6},{6,4},{8,9},{9,11},{11,1... | collective-permute-start | bytes 6291464 | tf_op jit(solution)/shard_map/ppermute | solution.py:111
  277.8 67.3 %collective-permute-start.11 = (bf16[256,2048]{1,0:T(8,128)(2,1)S(1)}, bf16[256,2048]{1,0:T(8,128)(2,1)S(1)}, u32[]{:S(2)}, u32[]{:S(2)}) collective-permute-start(bf16[256,2048]{1,0:T(8,128)(2,1)S(1)} %slice.234), channel_id=1, source_target_pairs={{1,0},{3,1},{2,3},{0,2},{5,4},{7,5},{6,7},{4,6},{9,8},{11,9},{10,1... | collective-permute-start | bytes 3145736 | tf_op jit(solution)/shard_map/ppermute | solution.py:116
  279.4 66.8 %collective-permute-start.10 = (bf16[256,2048]{1,0:T(8,128)(2,1)S(1)}, bf16[256,2048]{1,0:T(8,128)(2,1)}, u32[]{:S(2)}, u32[]{:S(2)}) collective-permute-start(bf16[256,2048]{1,0:T(8,128)(2,1)S(1)} %slice.233), channel_id=1, source_target_pairs={{0,1},{1,3},{3,2},{2,0},{4,5},{5,7},{7,6},{6,4},{8,9},{9,11},{11,1... | collective-permute-start | bytes 3145736 | tf_op jit(solution)/shard_map/ppermute | solution.py:115
  384.2 66.6 %collective-permute-start.18 = (bf16[256,2048]{1,0:T(8,128)(2,1)S(1)}, bf16[256,2048]{1,0:T(8,128)(2,1)S(1)}, u32[]{:S(2)}, u32[]{:S(2)}) collective-permute-start(bf16[256,2048]{1,0:T(8,128)(2,1)S(1)} %get-tuple-element.97), channel_id=1, source_target_pairs={{1,0},{3,1},{2,3},{0,2},{5,4},{7,5},{6,7},{4,6},{9,8},{11,9},{10,1... | collective-permute-start | bytes 3145736 | tf_op jit(solution)/shard_map/ppermute | solution.py:125
  384.6 67.1 %collective-permute-start.16 = (bf16[256,2048]{1,0:T(8,128)(2,1)S(1)}, bf16[256,2048]{1,0:T(8,128)(2,1)S(1)}, u32[]{:S(2)}, u32[]{:S(2)}) collective-permute-start(bf16[256,2048]{1,0:T(8,128)(2,1)S(1)} %get-tuple-element.96), channel_id=1, source_target_pairs={{0,1},{1,3},{3,2},{2,0},{4,5},{5,7},{7,6},{6,4},{8,9},{9,11},{11,1... | collective-permute-start | bytes 3145736 | tf_op jit(solution)/shard_map/ppermute | solution.py:124
  514.7 45.6 %collective-permute-start.20 = (bf16[512,2048]{1,0:T(8,128)(2,1)S(1)}, bf16[512,2048]{1,0:T(8,128)(2,1)S(1)}, u32[]{:S(2)}, u32[]{:S(2)}) collective-permute-start(bf16[512,2048]{1,0:T(8,128)(2,1)S(1)} %get-tuple-element.59), channel_id=1, source_target_pairs={{0,1},{1,3},{3,2},{2,0},{4,5},{5,7},{7,6},{6,4},{8,9},{9,11},{11,1... | collective-permute-start | bytes 6291464 | tf_op jit(solution)/shard_map/ppermute | solution.py:111
  516.2 45.9 %collective-permute-start.22 = (bf16[512,2048]{1,0:T(8,128)(2,1)S(1)}, bf16[512,2048]{1,0:T(8,128)(2,1)S(1)}, u32[]{:S(2)}, u32[]{:S(2)}) collective-permute-start(bf16[512,2048]{1,0:T(8,128)(2,1)S(1)} %get-tuple-element.59), channel_id=1, source_target_pairs={{1,0},{3,1},{2,3},{0,2},{5,4},{7,5},{6,7},{4,6},{9,8},{11,9},{10,1... | collective-permute-start | bytes 6291464 | tf_op jit(solution)/shard_map/ppermute | solution.py:112
  591.3 352.9 %reduce-scatter.11.cloned.1.call-start = ((), (), s32[]{:S(2)}) async-start(), calls=%async_computation.11 | async-start | bytes 7077888 | tf_op jit(solution)/shard_map/reduce_scatter | solution.py:434
  618.8 330.2 %reduce-scatter.5.cloned.1.call-start = ((), (), s32[]{:S(2)}) async-start(), calls=%async_computation.8 | async-start | bytes 4718592 | tf_op jit(solution)/shard_map/reduce_scatter | solution.py:476
  701.9 255.2 %reduce-scatter.9.cloned.1.call-start = ((), (), s32[]{:S(2)}) async-start(), calls=%async_computation.10 | async-start | bytes 14155776 | tf_op jit(solution)/shard_map/reduce_scatter | solution.py:433
  788.6 67.0 %collective-permute-start.31 = (bf16[512,2048]{1,0:T(8,128)(2,1)S(1)}, bf16[512,2048]{1,0:T(8,128)(2,1)S(1)}, u32[]{:S(2)}, u32[]{:S(2)}) collective-permute-start(bf16[512,2048]{1,0:T(8,128)(2,1)S(1)} %pad_maximum_fusion.9), channel_id=1, source_target_pairs={{1,0},{3,1},{2,3},{0,2},{5,4},{7,5},{6,7},{4,6},{9,8},{11,9},{10,1... | collective-permute-start | bytes 6291464 | tf_op jit(solution)/shard_map/ppermute | solution.py:139
  789.9 66.4 %collective-permute-start.29 = (bf16[512,2048]{1,0:T(8,128)(2,1)S(1)}, bf16[512,2048]{1,0:T(8,128)(2,1)S(1)}, u32[]{:S(2)}, u32[]{:S(2)}) collective-permute-start(bf16[512,2048]{1,0:T(8,128)(2,1)S(1)} %pad_maximum_fusion.8), channel_id=1, source_target_pairs={{0,1},{1,3},{3,2},{2,0},{4,5},{5,7},{7,6},{6,4},{8,9},{9,11},{11,1... | collective-permute-start | bytes 6291464 | tf_op jit(solution)/shard_map/ppermute | solution.py:138
  812.5 116.0 %collective-permute-start.27 = (bf16[512,2048]{1,0:T(8,128)(2,1)}, bf16[512,2048]{1,0:T(8,128)(2,1)}, u32[]{:S(2)}, u32[]{:S(2)}) collective-permute-start(bf16[512,2048]{1,0:T(8,128)(2,1)} %pad_maximum_fusion.7), channel_id=1, source_target_pairs={{1,0},{3,1},{2,3},{0,2},{5,4},{7,5},{6,7},{4,6},{9,8},{11,9},{10,1... | collective-permute-start | bytes 6291464 | tf_op jit(solution)/shard_map/ppermute | solution.py:139
  815.1 113.3 %collective-permute-start.25 = (bf16[512,2048]{1,0:T(8,128)(2,1)}, bf16[512,2048]{1,0:T(8,128)(2,1)}, u32[]{:S(2)}, u32[]{:S(2)}) collective-permute-start(bf16[512,2048]{1,0:T(8,128)(2,1)} %pad_maximum_fusion.6), channel_id=1, source_target_pairs={{0,1},{1,3},{3,2},{2,0},{4,5},{5,7},{7,6},{6,4},{8,9},{9,11},{11,1... | collective-permute-start | bytes 6291464 | tf_op jit(solution)/shard_map/ppermute | solution.py:138
  (139 other events, 3203.8 us)
Sparse Core Ops, SparseCore 0:
  10.2 49.8 all-gather.4
  62.3 29.5 all-gather.6
  94.1 115.7 all-gather.8
  211.9 63.3 all-gather.10
  591.4 36.9 reduce-scatter.6
  630.6 68.4 reduce-scatter.10
  702.0 51.1 reduce-scatter.4
  755.5 127.3 reduce-scatter.8

commit v2 on v1

v2 whole, which is shorter than its diff:
```python
import jax
import jax.numpy as jnp
from jax import lax
from jax.experimental import pallas as pl
from jax.experimental.pallas import tpu as pltpu
from jax.sharding import PartitionSpec as P

MODEL_WIDTH = 2048
HQ = 16
HEAD_WIDTH = 128
FF = 6144
QUERY_PER_KEY = 2
SEQUENCE_TOKENS = 2048


norm_eps = 1e-06
rope_base = 1000000.0
beta_one = 0.5
beta_two = 0.55
step_count = 5.0
adam_eps = 1e-08
decay_rate = 0.1
gain_rate = 0.3
masked_score = -1e30
log2_e = 1.4426950408889634


def rms_gain(values, gain_row):
    return (
        values * lax.rsqrt(jnp.mean(values * values, axis=-1, keepdims=True) + norm_eps) * gain_row
    )


def rotary_tables(length, width):
    frequency = rope_base ** (
        -2.0 * jnp.arange(width // 2, dtype=jnp.int32).astype(jnp.float32) / width
    )
    angles = jnp.arange(length, dtype=jnp.int32).astype(jnp.float32)[:, None] * frequency[None, :]
    cos, sin = jnp.cos(angles), jnp.sin(angles)
    return jnp.concatenate([cos, cos], axis=1), jnp.concatenate([-sin, sin], axis=1)


def contract_rows(left, right):
    return lax.dot_general(
        left, right, (((0,), (0,)), ((), ())), preferred_element_type=jnp.float32
    )


def contract_cols(left, right):
    return lax.dot_general(
        left, right, (((1,), (1,)), ((), ())), preferred_element_type=jnp.float32
    )


def product(left, right):
    return jnp.dot(left, right, preferred_element_type=jnp.float32)


def adamw(weight, gradient, mean_old, square_old, rate):
    mean_new = beta_one * mean_old + (1.0 - beta_one) * gradient
    square_new = beta_two * square_old + (1.0 - beta_two) * gradient * gradient
    mean_hat = mean_new / (1.0 - beta_one**step_count)
    square_hat = square_new / (1.0 - beta_two**step_count)
    weight_new = weight - rate * (
        mean_hat / (jnp.sqrt(square_hat) + adam_eps) + decay_rate * weight
    )
    return (weight_new, square_new)


def ring_place(index, size):
    return jnp.where(index < size // 2, index, size // 2 + size - 1 - index)


def ring_pairs(size):
    half = size // 2
    order = list(range(half)) + list(range(size - 1, half - 1, -1))
    ahead = [(order[r], order[(r + 1) % size]) for r in range(size)]
    return ahead, [(b, a) for a, b in ahead]


def ring_offsets(size):
    offsets = [0]
    for step in range(1, size // 2):
        offsets += [step, -step]
    return offsets + [size // 2]


class Order:
    def __init__(self):
        self.last = ()

    def turn(self, *values):
        tied = lax.optimization_barrier(values + self.last)[: len(values)]
        return tied[0] if len(values) == 1 else tied

    def mark(self, *values):
        self.last = values
        return values[0] if len(values) == 1 else values


def ring_gather(rows, size, work, order, hold=()):
    ahead, back = ring_pairs(size)
    half = rows.shape[0] // 2
    groups = [[rows]]
    from_left = from_right = rows
    work(0, groups[0])
    for step in range(1, size // 2):
        from_left, from_right = (
            lax.ppermute(from_left, "tensor", ahead),
            lax.ppermute(from_right, "tensor", back),
        )
        held = tuple(hold) if step == size // 2 - 1 else ()
        from_left, from_right = lax.optimization_barrier(
            (from_left, from_right) + held + order.last
        )[:2]
        groups.append([from_right, from_left])
        work(step, groups[-1])
    low = lax.ppermute(from_left[:half], "tensor", ahead)
    high = lax.ppermute(from_right[half:], "tensor", back)
    groups.append(list(lax.optimization_barrier((low, high) + order.last)[:2]))
    work(size // 2, groups[-1])
    return groups


def relay_kernel(pair_ref, ahead_ref, back_ref, right_ref, left_ref):
    rows = right_ref.shape[0]
    taken = ahead_ref.shape[0]
    for first, out_ref, got_ref, low in (
        (0, right_ref, ahead_ref, 0),
        (rows, left_ref, back_ref, rows - taken),
    ):
        out_ref[low : low + taken, :] = (
            pair_ref[first + low : first + low + taken, :].astype(jnp.float32)
            + got_ref[...].astype(jnp.float32)
        ).astype(jnp.bfloat16)
        if taken < rows:
            rest = rows - taken - low
            out_ref[rest : rest + rows - taken, :] = pair_ref[
                first + rest : first + rest + rows - taken, :
            ].astype(jnp.bfloat16)


def relay(pair, going_ahead, going_back):
    rows, width = pair.shape[0] // 2, pair.shape[1]
    tile = tile_of(width, 512)
    spec = lambda count: pl.BlockSpec((count, tile), lambda i: (0, i))
    return pl.pallas_call(
        relay_kernel,
        grid=(width // tile,),
        in_specs=[spec(2 * rows), spec(going_ahead.shape[0]), spec(going_back.shape[0])],
        out_specs=[spec(rows)] * 2,
        out_shape=[jax.ShapeDtypeStruct((rows, width), jnp.bfloat16)] * 2,
        compiler_params=kernel_params(),
        cost_estimate=SMALL_COST,
        name="relay",
    )(pair, going_ahead, going_back)


def ring_scatter(size, part, order, hold=(), first=(), between=None, got=None):
    ahead, back = ring_pairs(size)
    low, high = part(size // 2)
    if hold:
        low, high = lax.optimization_barrier((low, high) + tuple(hold))[:2]
    going_ahead = lax.ppermute(low, "tensor", ahead)
    going_back = lax.ppermute(high, "tensor", back)
    for step in range(size // 2 - 1, 0, -1):
        pair = part(step)
        going_ahead, going_back = order.turn(going_ahead, going_back, *first)[:2]
        to_right, to_left = order.mark(*relay(pair, going_ahead, going_back))
        if got is not None:
            got[:] = [to_right, to_left]
        going_ahead = lax.ppermute(to_right, "tensor", ahead)
        going_back = lax.ppermute(to_left, "tensor", back)
    if between is not None:
        between()
    own = part(0)
    if size == 2:
        return own, (jnp.concatenate([going_ahead, going_back], axis=0),)
    return own, (going_ahead, going_back)


def total(own, received):
    return own + sum(block.astype(jnp.float32) for block in received)


def sum_everywhere(values, axes):
    for axis in axes:
        size = lax.axis_size(axis)
        if size & (size - 1):
            values = lax.psum(values, axis)
            continue
        reach = 1
        while reach < size:
            pairs = [(i, i ^ reach) for i in range(size)]
            values = values + lax.ppermute(values, axis, pairs)
            reach *= 2
    return values


def tile_of(width, most):
    return next(t for t in (most, 512, 256, 128) if t <= most and width % t == 0)


def kernel_params(mebibytes=32):
    return pltpu.CompilerParams(vmem_limit_bytes=mebibytes * 1024 * 1024)


SMALL_COST = pl.CostEstimate(flops=1_000_000, bytes_accessed=1_000_000, transcendentals=0)


class Piece:
    def __init__(self, array, count=None, index=0, entry=None):
        self.array, self.count = array, count or array.shape[0]
        self.index, self.entry = index, entry

    def row(self, table):
        return self.index if self.entry is None else table[self.entry]

    def spec(self, width=None):
        if width is None:
            return pl.BlockSpec(
                (self.count, self.array.shape[1]),
                lambda i, table: (self.row(table), 0),
                pipeline_mode=pl.Buffered(1),
            )
        return pl.BlockSpec((self.count, width), lambda i, table: (self.row(table), i))


def pieces_of(blocks):
    return [Piece(block) for block in blocks]


def stacked(refs):
    values = [ref[...] for ref in refs]
    return values[0] if len(values) == 1 else jnp.concatenate(values, axis=0)


def row_call(kernel, name, table, grid, operands, specs, outs, out_specs, aliases=None):
    return pl.pallas_call(
        kernel,
        grid_spec=pltpu.PrefetchScalarGridSpec(
            num_scalar_prefetch=1, grid=grid, in_specs=specs, out_specs=out_specs
        ),
        out_shape=outs,
        input_output_aliases=aliases or {},
        compiler_params=kernel_params(),
        cost_estimate=SMALL_COST,
        name=name,
    )(table, *operands)


def product_kernel(count, crossed, *refs):
    rows = stacked(refs[1 : 1 + count])
    matrix = refs[1 + count][...]
    result = contract_cols(rows, matrix) if crossed else product(rows, matrix)
    outs = refs[-2:] if refs[-1].shape[0] < rows.shape[0] else refs[-1:]
    size = rows.shape[0] // len(outs)
    for i, out_ref in enumerate(outs):
        out_ref[...] = result[i * size : (i + 1) * size].astype(out_ref.dtype)


def block_product(table, pieces, matrix, crossed, kind=jnp.bfloat16, halves=False, into=None):
    width = matrix.shape[0] if crossed else matrix.shape[1]
    tile = tile_of(width, 512)
    count = sum(piece.count for piece in pieces)
    if crossed:
        matrix_spec = pl.BlockSpec((tile, matrix.shape[1]), lambda i, table: (i, 0))
    else:
        matrix_spec = pl.BlockSpec((matrix.shape[0], tile), lambda i, table: (0, i))
    operands = [piece.array for piece in pieces] + [matrix]
    specs = [piece.spec() for piece in pieces] + [matrix_spec]
    aliases = {}
    index, all_rows = 0, count
    if into is not None:
        all_rows, index, so_far = into
        if so_far is not None:
            operands.append(so_far)
            specs.append(pl.BlockSpec(memory_space=pltpu.HBM))
            aliases = {len(operands): 0}
    if halves:
        count = all_rows = count // 2
    out_spec = pl.BlockSpec((count, tile), lambda i, table: (index, i))
    out = jax.ShapeDtypeStruct((all_rows, width), kind)
    result = row_call(
        lambda *refs: product_kernel(len(pieces), crossed, *refs),
        "block_product",
        table,
        (width // tile,),
        operands,
        specs,
        [out] * (2 if halves else 1),
        [out_spec] * (2 if halves else 1),
        aliases,
    )
    return result if halves else result[0]


def gate_kernel(count, *refs):
    rows = stacked(refs[1 : 1 + count])
    gate_ref, up_ref, activated_ref, gate_out, up_out = refs[1 + count :]
    gate = product(rows, gate_ref[...])
    up = product(rows, up_ref[...])
    activated_ref[...] = (gate * jax.nn.sigmoid(gate) * up).astype(jnp.bfloat16)
    gate_out[...] = gate.astype(gate_out.dtype)
    up_out[...] = up.astype(up_out.dtype)


def gate_up_product(table, pieces, matrix):
    depth, width = matrix.shape[0], matrix.shape[1] // 2
    count = sum(piece.count for piece in pieces)
    tile = tile_of(width, 256)
    steps = width // tile
    return row_call(
        lambda *refs: gate_kernel(len(pieces), *refs),
        "gate_up",
        table,
        (steps,),
        [piece.array for piece in pieces] + [matrix, matrix],
        [piece.spec() for piece in pieces]
        + [
            pl.BlockSpec((depth, tile), lambda i, table: (0, i)),
            pl.BlockSpec((depth, tile), lambda i, table: (0, steps + i)),
        ],
        [jax.ShapeDtypeStruct((count, width), jnp.bfloat16)] * 3,
        [pl.BlockSpec((count, tile), lambda i, table: (0, i))] * 3,
    )


def gate_grad_kernel(count, *refs):
    rows = stacked(refs[1 : 1 + count])
    down_ref, gate_ref, up_ref, out_ref = refs[1 + count :]
    step = pl.program_id(0)
    tile = gate_ref.shape[1]
    width = out_ref.shape[1] // 2
    grad = contract_cols(rows, down_ref[...])
    gate = gate_ref[...].astype(jnp.float32)
    up = up_ref[...].astype(jnp.float32)
    sigmoid_gate = jax.nn.sigmoid(gate)
    scaled = grad * sigmoid_gate
    start = pl.multiple_of(step * tile, tile)
    out_ref[:, pl.ds(start, tile)] = (
        scaled * up * (1.0 + gate * (1.0 - sigmoid_gate))
    ).astype(jnp.bfloat16)
    out_ref[:, pl.ds(pl.multiple_of(width + step * tile, tile), tile)] = (scaled * gate).astype(
        jnp.bfloat16
    )


def gate_up_gradient(table, pieces, down, gate, up):
    count, width = gate.shape
    tile = tile_of(width, 256)
    part = pl.BlockSpec((count, tile), lambda i, table: (0, i))
    return row_call(
        lambda *refs: gate_grad_kernel(len(pieces), *refs),
        "gate_up_grad",
        table,
        (width // tile,),
        [piece.array for piece in pieces] + [down, gate, up],
        [piece.spec() for piece in pieces]
        + [pl.BlockSpec((tile, down.shape[1]), lambda i, table: (i, 0)), part, part],
        [jax.ShapeDtypeStruct((count, 2 * width), jnp.bfloat16)],
        [pl.BlockSpec((count, 2 * width), lambda i, table: (0, 0))],
    )[0]


def rows_kernel(count, *refs):
    out_ref = refs[-1]
    out_ref[...] = sum(
        contract_rows(refs[1 + i][...], refs[1 + count + i][...]) for i in range(count)
    ).astype(out_ref.dtype)


def weight_gradient(table, lefts, rights):
    width, columns = lefts[0].array.shape[1], rights[0].array.shape[1]
    tile = tile_of(width, 256)
    return row_call(
        lambda *refs: rows_kernel(len(lefts), *refs),
        "weight_grad",
        table,
        (width // tile,),
        [piece.array for piece in lefts + rights],
        [piece.spec(tile) for piece in lefts] + [piece.spec() for piece in rights],
        [jax.ShapeDtypeStruct((width, columns), jnp.bfloat16)],
        [pl.BlockSpec((tile, columns), lambda i, table: (i, 0))],
    )[0]


def split_groups(groups, rows):
    own, *pairs, far = groups
    pieces = [Piece(own)]
    for pair in pairs:
        pieces += [Piece(pair, rows, 0), Piece(pair, rows, 1)]
    return pieces + [Piece(far, rows // 2, 0), Piece(far, rows // 2, 1)]


def project_kernel(count, *refs):
    rows = stacked(refs[1 : 1 + count])
    matrix_ref, gain_ref, cos_ref, sin_ref = refs[1 + count : 5 + count]
    query_ref, key_ref, value_ref, query_raw, key_raw = refs[-5:]
    width = HEAD_WIDTH
    mixed = product(rows, matrix_ref[...])
    cos, sin = cos_ref[...], sin_ref[...]
    for part in range(QUERY_PER_KEY + 1):
        values = mixed[:, part * width : (part + 1) * width]
        is_key = part == QUERY_PER_KEY
        gain = gain_ref[1:2, :] if is_key else gain_ref[0:1, :]
        scale = lax.rsqrt(jnp.mean(values * values, axis=1, keepdims=True) + norm_eps)
        scaled = values * scale * gain
        turned = scaled * cos + pltpu.roll(scaled, width // 2, 1) * sin
        if is_key:
            key_ref[...] = turned.astype(jnp.bfloat16)
            key_raw[...] = values
        else:
            query_ref[:, part * width : (part + 1) * width] = turned.astype(jnp.bfloat16)
            query_raw[:, part * width : (part + 1) * width] = values
    value_ref[...] = mixed[:, (QUERY_PER_KEY + 1) * width :].astype(jnp.bfloat16)


def project(blocks, matrix, gains, cos, sin, place, total_rows, before):
    count, depth = sum(block.shape[0] for block in blocks), matrix.shape[0]
    block = (QUERY_PER_KEY + 2) * HEAD_WIDTH
    heads = matrix.shape[1] // block
    wide = QUERY_PER_KEY * HEAD_WIDTH
    per_table = cos.shape[0] // count
    table_spec = pl.BlockSpec(
        (count, HEAD_WIDTH), lambda h, at: (lax.rem(at[0], per_table), 0)
    )
    widths = (wide, HEAD_WIDTH, HEAD_WIDTH, wide, HEAD_WIDTH)
    kinds = (jnp.bfloat16,) * 3 + (jnp.float32,) * 2
    kept = () if before is None else tuple(before)
    return pl.pallas_call(
        lambda *refs: project_kernel(len(blocks), *refs),
        grid_spec=pltpu.PrefetchScalarGridSpec(
            num_scalar_prefetch=1,
            grid=(heads,),
            in_specs=[
                pl.BlockSpec((rows.shape[0], depth), lambda h, at: (0, 0)) for rows in blocks
            ]
            + [
                pl.BlockSpec((depth, block), lambda h, at: (0, h)),
                pl.BlockSpec((2, HEAD_WIDTH), lambda h, at: (0, 0)),
                table_spec,
                table_spec,
            ]
            + [pl.BlockSpec(memory_space=pltpu.HBM)] * len(kept),
            out_specs=[pl.BlockSpec((count, w), lambda h, at: (at[0], h)) for w in widths],
        ),
        out_shape=[
            jax.ShapeDtypeStruct((total_rows, heads * w), kind) for w, kind in zip(widths, kinds)
        ],
        input_output_aliases={5 + len(blocks) + i: i for i in range(len(kept))},
        compiler_params=kernel_params(56),
        cost_estimate=SMALL_COST,
        name="project",
    )(place.reshape(1), *blocks, matrix, gains, cos, sin, *kept)


def attend_kernel(scale, query_ref, key_ref, value_ref, out_ref, log_ref):
    block = query_ref.shape[0]
    width = key_ref.shape[1]
    group = query_ref.shape[1] // width
    step = pl.program_id(2)
    below = lax.broadcasted_iota(jnp.int32, (block, block), 0) <= lax.broadcasted_iota(
        jnp.int32, (block, block), 1
    )
    queries = [query_ref[:, g * width : (g + 1) * width] for g in range(group)]

    def visit(start, carry, masked):
        keys = key_ref[pl.ds(start, block), :]
        values = value_ref[pl.ds(start, block), :]
        new = []
        for g in range(group):
            total, acc = carry[g]
            weights = jnp.exp2(contract_cols(keys, queries[g]) * (scale * log2_e))
            if masked:
                weights = jnp.where(below, weights, 0.0)
            total = total + jnp.sum(weights, axis=0, keepdims=True)
            acc = acc + contract_rows(values, weights.astype(jnp.bfloat16))
            new.append((total, acc))
        return tuple(new)

    start_carry = tuple(
        (jnp.zeros((1, block), jnp.float32), jnp.zeros((width, block), jnp.float32))
        for _ in range(group)
    )
    carry = lax.fori_loop(
        0, step, lambda j, c: visit(pl.multiple_of(j * block, block), c, False), start_carry
    )
    carry = visit(pl.multiple_of(step * block, block), carry, True)
    for g in range(group):
        total, acc = carry[g]
        out_ref[:, g * width : (g + 1) * width] = jnp.transpose(acc / total).astype(jnp.bfloat16)
        log_ref[0, 0, g : g + 1, :] = jnp.log2(total)


def attention_forward(query, key, value, block):
    rows = query.shape[0]
    heads = key.shape[1] // HEAD_WIDTH
    steps = SEQUENCE_TOKENS // block
    wide = QUERY_PER_KEY * HEAD_WIDTH
    sequences = rows // SEQUENCE_TOKENS
    query_spec = pl.BlockSpec((block, wide), lambda h, s, i: (s * steps + i, h))
    key_spec = pl.BlockSpec((SEQUENCE_TOKENS, HEAD_WIDTH), lambda h, s, i: (s, h))
    return pl.pallas_call(
        lambda *refs: attend_kernel(HEAD_WIDTH ** (-0.5), *refs),
        grid=(heads, sequences, steps),
        in_specs=[query_spec, key_spec, key_spec],
        out_specs=[
            query_spec,
            pl.BlockSpec(
                (1, 1, QUERY_PER_KEY, block), lambda h, s, i: (h, s * steps + i, 0, 0)
            ),
        ],
        out_shape=[
            jax.ShapeDtypeStruct(query.shape, jnp.bfloat16),
            jax.ShapeDtypeStruct((heads, rows // block, QUERY_PER_KEY, block), jnp.float32),
        ],
        compiler_params=kernel_params(56),
        cost_estimate=SMALL_COST,
        name="attend",
    )(query, key, value)


def norm_back(values, grad, gain, cos, sin):
    width = values.shape[1]
    turned = grad * cos + pltpu.roll(grad * sin, width // 2, 1)
    scale = lax.rsqrt(jnp.mean(values * values, axis=1, keepdims=True) + norm_eps)
    unit = values * scale
    inner = turned * gain
    back = scale * (inner - unit * jnp.mean(inner * unit, axis=1, keepdims=True))
    return back.astype(jnp.bfloat16), jnp.sum(turned * unit, axis=0, keepdims=True)


def attend_back_kernel(
    scale,
    table_ref,
    query_ref,
    key_ref,
    value_ref,
    grad_ref,
    context_ref,
    log_ref,
    query_raw,
    key_raw,
    gain_ref,
    cos_ref,
    sin_ref,
    *refs,
):
    mixed_out, gain_out, key_sum, value_sum = refs[-4:]
    block = query_ref.shape[0]
    width = key_ref.shape[1]
    group = query_ref.shape[1] // width
    sequence, step = pl.program_id(0), pl.program_id(1)
    below = lax.broadcasted_iota(jnp.int32, (block, block), 0) <= lax.broadcasted_iota(
        jnp.int32, (block, block), 1
    )

    @pl.when(step == 0)
    def _():
        key_sum[...] = jnp.zeros_like(key_sum)
        value_sum[...] = jnp.zeros_like(value_sum)

    @pl.when((step == 0) & (sequence == 0))
    def _():
        gain_out[...] = jnp.zeros_like(gain_out)

    queries, grads, logs, dots = [], [], [], []
    for g in range(group):
        cols = slice(g * width, (g + 1) * width)
        queries.append(query_ref[:, cols])
        grads.append(grad_ref[:, cols])
        logs.append(log_ref[0, 0, g : g + 1, :])
        both = grads[g].astype(jnp.float32) * context_ref[:, cols].astype(jnp.float32)
        dots.append(jnp.sum(jnp.transpose(both), axis=0, keepdims=True))

    def visit(start, carry, masked):
        rows = pl.ds(start, block)
        keys = key_ref[rows, :]
        values = value_ref[rows, :]
        new = []
        key_part = value_part = None
        for g in range(group):
            weights = jnp.exp2(contract_cols(keys, queries[g]) * (scale * log2_e) - logs[g])
            if masked:
                weights = jnp.where(below, weights, 0.0)
            slope = contract_cols(values, grads[g])
            score = (weights * (slope - dots[g])).astype(jnp.bfloat16)
            value_g = product(weights.astype(jnp.bfloat16), grads[g])
            key_g = product(score, queries[g])
            key_part = key_g if key_part is None else key_part + key_g
            value_part = value_g if value_part is None else value_part + value_g
            new.append(carry[g] + contract_rows(keys, score))
        key_sum[rows, :] += key_part
        value_sum[rows, :] += value_part
        return tuple(new)

    carry = tuple(jnp.zeros((width, block), jnp.float32) for _ in range(group))
    carry = lax.fori_loop(
        0, step, lambda j, c: visit(pl.multiple_of(j * block, block), c, False), carry
    )
    carry = visit(pl.multiple_of(step * block, block), carry, True)
    rows = pl.ds(pl.multiple_of(step * block, block), block)
    cos, sin = cos_ref[rows, :], sin_ref[rows, :]
    for g in range(group):
        cols = slice(g * width, (g + 1) * width)
        back, gain = norm_back(
            query_raw[:, cols], jnp.transpose(carry[g]) * scale, gain_ref[0:1, :], cos, sin
        )
        mixed_out[rows, cols] = back
        gain_out[0:1, :] += gain

    @pl.when(step == pl.num_programs(1) - 1)
    def _():
        def finish(j, _):
            rows = pl.ds(pl.multiple_of(j * block, block), block)
            back, gain = norm_back(
                key_raw[rows, :],
                key_sum[rows, :] * scale,
                gain_ref[1:2, :],
                cos_ref[rows, :],
                sin_ref[rows, :],
            )
            mixed_out[rows, group * width : (group + 1) * width] = back
            mixed_out[rows, (group + 1) * width :] = value_sum[rows, :].astype(jnp.bfloat16)
            gain_out[1:2, :] += gain
            return 0

        lax.fori_loop(0, pl.num_programs(1), finish, 0)


def attention_backward(
    slots, query, key, value, grad, context, logs, query_raw, key_raw, gains, cos, sin, head, before
):
    rows = query.shape[0]
    block = logs.shape[-1]
    steps = SEQUENCE_TOKENS // block
    wide = QUERY_PER_KEY * HEAD_WIDTH
    heads = key.shape[1] // HEAD_WIDTH
    sequences = rows // SEQUENCE_TOKENS
    mixed = (QUERY_PER_KEY + 2) * HEAD_WIDTH
    query_spec = pl.BlockSpec((block, wide), lambda s, i, slots: (s * steps + i, head))
    key_spec = pl.BlockSpec((SEQUENCE_TOKENS, HEAD_WIDTH), lambda s, i, slots: (s, head))
    table_spec = pl.BlockSpec((SEQUENCE_TOKENS, HEAD_WIDTH), lambda s, i, slots: (0, 0))
    gain_spec = pl.BlockSpec((2, HEAD_WIDTH), lambda s, i, slots: (0, 0))
    kept = () if before is None else (before,)
    return pl.pallas_call(
        lambda *refs: attend_back_kernel(HEAD_WIDTH ** (-0.5), *refs),
        grid_spec=pltpu.PrefetchScalarGridSpec(
            num_scalar_prefetch=1,
            grid=(sequences, steps),
            in_specs=[
            query_spec,
            key_spec,
            key_spec,
            pl.BlockSpec((block, wide), lambda s, i, slots: (slots[s * steps + i], head)),
            query_spec,
            pl.BlockSpec(
                (1, 1, QUERY_PER_KEY, block), lambda s, i, slots: (head, s * steps + i, 0, 0)
            ),
            query_spec,
            key_spec,
            gain_spec,
            table_spec,
            table_spec,
        ]
        + [pl.BlockSpec(memory_space=pltpu.HBM)] * len(kept),
        out_specs=[
            pl.BlockSpec((SEQUENCE_TOKENS, mixed), lambda s, i, slots: (s, head)),
            gain_spec,
        ],
        scratch_shapes=[pltpu.VMEM((SEQUENCE_TOKENS, HEAD_WIDTH), jnp.float32)] * 2,
        ),
        out_shape=[
            jax.ShapeDtypeStruct((rows, heads * mixed), jnp.bfloat16),
            jax.ShapeDtypeStruct((2, HEAD_WIDTH), jnp.float32),
        ],
        input_output_aliases={12: 0} if kept else {},
        compiler_params=kernel_params(56),
        cost_estimate=SMALL_COST,
        name="attend_back",
    )(slots, query, key, value, grad, context, logs, query_raw, key_raw, gains, cos, sin, *kept)


def local(
    inputs,
    input_projection_weight,
    input_first_moment,
    input_second_moment,
    out_weight,
    out_mean,
    out_square,
    swiglu_weight,
    swiglu_mean,
    swiglu_square,
    down_weight,
    down_mean,
    down_square,
    norm_gains,
    norm_mean,
    norm_square,
    qknorm_gains,
    qknorm_mean,
    qknorm_square,
    cotangent,
):
    size = lax.axis_size("tensor")
    rows = inputs.shape[0]
    half = rows // 2
    group_rows = rows * size
    last = size // 2
    dp_rows = input_projection_weight.shape[0]
    local_kv = input_projection_weight.shape[1]
    local_ff = swiglu_weight.shape[2]
    me = ring_place(lax.axis_index("tensor"), size)
    places = [ring_place((me + d + size) % size, size) for d in ring_offsets(size)]
    group_places = [places[:1]]
    for step in range(1, last):
        group_places.append(places[2 * step - 1 : 2 * step + 1])
    group_places.append(places[-1:])
    table = jnp.stack(places + [2 * places[-1], 2 * places[-1] + 1]).astype(jnp.int32)
    away = (ring_place(jnp.arange(size, dtype=jnp.int32), size) - me + size) % size
    slots = jnp.where(
        away == 0,
        size - 2,
        jnp.where(
            away == last,
            size - 1,
            jnp.where(away < last, 2 * away - 2, 2 * (size - away) - 1),
        ),
    ).astype(jnp.int32)
    order = Order()
    turn, mark = order.turn, order.mark
    tie = lax.optimization_barrier

    def ordered(array, group):
        entries = [0] if group == 0 else [2 * group - 1, 2 * group]
        if group == last:
            entries = [size - 1]
        return [Piece(array, rows, entry=entry) for entry in entries]

    def ordered_finely(array):
        pieces = [Piece(array, rows, entry=entry) for entry in range(size - 1)]
        return pieces + [Piece(array, half, entry=size + i) for i in range(2)]

    def flat(groups):
        return pieces_of([block for group in groups for block in group])

    in_low = input_projection_weight.astype(jnp.bfloat16).reshape(dp_rows, -1)
    out_low = out_weight.astype(jnp.bfloat16)
    swiglu_low = swiglu_weight.astype(jnp.bfloat16).reshape(dp_rows, 2 * local_ff)
    down_low = down_weight.astype(jnp.bfloat16)
    in_matrix = lax.all_gather(in_low, "dp", axis=0, tiled=True)
    out_full = lax.all_gather(out_low, "dp", axis=1, tiled=True)
    swiglu_matrix = lax.all_gather(swiglu_low, "dp", axis=0, tiled=True)
    down_full = lax.all_gather(down_low, "dp", axis=1, tiled=True)

    inputs_f = inputs.astype(jnp.float32)
    normed_f, norm_one_back = jax.vjp(lambda rows: rms_gain(rows, norm_gains[0]), inputs_f)
    cos, sin = rotary_tables(SEQUENCE_TOKENS, HEAD_WIDTH)
    projected = []

    def project_group(group, blocks):
        calls = [blocks] if group in (0, last) else [[block] for block in blocks]
        for place, call in zip(group_places[group], calls):
            call[0] = turn(call[0])
            projected[:] = mark(
                *project(
                    call, in_matrix, qknorm_gains, cos, sin, place, group_rows, projected or None
                )
            )

    normed_groups = ring_gather(
        normed_f.astype(jnp.bfloat16), size, project_group, order, hold=(in_matrix,)
    )
    query, key, value, query_raw, key_raw = projected
    cotangent_sent = tie((cotangent, *normed_groups[-1]))[0]

    context, logs = mark(*attention_forward(query, key, value, rows))
    cot_groups = ring_gather(cotangent_sent, size, lambda group, blocks: None, Order())

    def out_group(group):
        kind = jnp.float32 if group == 0 else jnp.bfloat16
        array = turn(context)
        part = block_product(
            table, ordered(array, group), out_full, False, kind, halves=group == last
        )
        return mark(*part) if group == last else mark(part)

    own, received = ring_scatter(size, out_group, order, first=cot_groups[-1])
    received = tie((*received, swiglu_matrix))[: len(received)]
    hidden = inputs_f + total(own, received)
    normed_two_f, norm_two_back = jax.vjp(rms_gain, hidden, norm_gains[1])

    gate_groups = []
    grads = [None] * (last + 1)

    def gate_group(group, blocks):
        blocks[0] = turn(blocks[0])
        gate_groups.append(mark(*gate_up_product(table, pieces_of(blocks), swiglu_matrix)))
        if group == 0:
            two_own.append(two_group(0))

    def two_group(group):
        cots = [turn(cot_groups[group][0])] + cot_groups[group][1:]
        grads[group] = mark(
            gate_up_gradient(table, pieces_of(cots), down_full, *gate_groups[group][1:])
        )
        kind = jnp.float32 if group == 0 else jnp.bfloat16
        part = block_product(
            table, [Piece(grads[group])], swiglu_matrix, True, kind, halves=group == last
        )
        return mark(*part) if group == last else mark(part)

    two_own = []

    two_groups = ring_gather(
        normed_two_f.astype(jnp.bfloat16), size, gate_group, order, hold=(down_full,)
    )
    activated = [parts[0] for parts in gate_groups]
    early = []

    def down_gradient():
        lefts = split_groups([turn(activated[0])] + activated[1:], rows)
        early.append(mark(weight_gradient(table, lefts, flat(cot_groups))))

    own, received = ring_scatter(
        size,
        lambda group: two_own[0] if group == 0 else two_group(group),
        order,
        between=down_gradient,
    )
    (down_part,) = early
    down_part, *received = tie((down_part, *received))
    down_grad = lax.psum_scatter(down_part, "dp", scatter_dimension=1, tiled=True)
    received = turn(*received) if len(received) > 1 else (turn(*received),)
    two_grad = total(own, received)
    hidden_norm_grad, mlp_gain_grad = norm_two_back(two_grad)
    hidden_grad = cotangent.astype(jnp.float32) + hidden_norm_grad

    context_grad = [None]
    more = []

    def context_group(group, blocks):
        blocks[0] = turn(blocks[0])
        index = size - 2 if group == 0 else size - 1 if group == last else group - 1
        context_grad[0] = mark(
            block_product(
                table, pieces_of(blocks), out_full, True, into=(group_rows, index, context_grad[0])
            )
        )
        if group == 0:
            twos = flat(two_groups)
            twos[0].array = turn(twos[0].array)
            more.append(mark(weight_gradient(table, twos, split_groups(grads, rows))))

    attended_groups = ring_gather(hidden_grad.astype(jnp.bfloat16), size, context_group, order)
    swiglu_part = tie((more[0], *attended_groups[last - 1]))[0]
    swiglu_grad = lax.psum_scatter(swiglu_part, "dp", scatter_dimension=0, tiled=True)
    head_grads, out_parts = [], []

    def head_backward(head):
        head_grads.append(
            mark(
                *attention_backward(
                    slots, turn(query), key, value, context_grad[0], context, logs, query_raw,
                    key_raw, qknorm_gains, cos, sin, head,
                    head_grads[-1][0] if head_grads else None,
                )
            )
        )

    def down_group(group):
        if group == 0:
            for head in range(1, local_kv):
                head_backward(head)
        kind = jnp.float32 if group == 0 else jnp.bfloat16
        part = block_product(
            table, [Piece(turn(activated[group]))], down_full, False, kind, halves=group == last
        )
        part = mark(*part) if group == last else mark(part)
        return part

    def out_gradient():
        out_parts.append(
            mark(weight_gradient(table, ordered_finely(turn(context)), flat(attended_groups)))
        )
        head_backward(0)

    own, received = ring_scatter(
        size, down_group, order, hold=attended_groups[-1], between=out_gradient
    )
    out_part, down_grad = tie((out_parts[0], down_grad, *received, *head_grads[-1]))[:2]
    out_grad = lax.psum_scatter(out_part, "dp", scatter_dimension=1, tiled=True)
    outputs = (hidden + total(own, received)).astype(jnp.bfloat16)
    mixed_grad = head_grads[-1][0]
    qknorm_part = sum(pair[1] for pair in head_grads)
    in_parts, gains = [], []

    def normed_group(group):
        kind = jnp.float32 if group == 0 else jnp.bfloat16
        array = turn(mixed_grad)
        part = block_product(
            table, ordered(array, group), in_matrix, True, kind, halves=group == last
        )
        part = mark(*part) if group == last else mark(part)
        if group == last:
            normeds = flat(normed_groups)
            normeds[0].array = turn(normeds[0].array)
            in_parts.append(
                mark(weight_gradient(table, normeds, ordered_finely(mixed_grad)))
            )
        if group == 1 or last == 1:
            gains.append(
                mark(
                    jnp.sum(
                        turn(in_parts[0]).astype(jnp.float32) * in_matrix.astype(jnp.float32),
                        axis=1,
                    )
                )
            )
        return part

    got = []
    own, received = ring_scatter(size, normed_group, order, hold=(outputs,), got=got)
    in_part, swiglu_grad = tie((in_parts[0], swiglu_grad, *got))[:2]
    in_grad = lax.psum_scatter(in_part, "dp", scatter_dimension=0, tiled=True)
    in_grad = in_grad.astype(jnp.float32).reshape(input_projection_weight.shape)
    out_grad, swiglu_grad, down_grad = tie((out_grad, swiglu_grad, down_grad, *got))[:3]
    swiglu_grad = swiglu_grad.astype(jnp.float32).reshape(swiglu_weight.shape)
    out_grad, down_grad = out_grad.astype(jnp.float32), down_grad.astype(jnp.float32)
    out_new, out_second = adamw(
        out_weight, out_grad, out_mean, out_square, (HQ * HEAD_WIDTH / 8.0) ** (-0.5)
    )
    swiglu_new, swiglu_second = adamw(
        swiglu_weight, swiglu_grad, swiglu_mean, swiglu_square, MODEL_WIDTH ** (-0.5)
    )
    down_new, down_second = adamw(down_weight, down_grad, down_mean, down_square, FF ** (-0.5))
    (
        received,
        own,
        out_grad,
        out_new,
        out_second,
        swiglu_grad,
        swiglu_new,
        swiglu_second,
        down_grad,
        down_new,
        down_second,
    ) = tie(
        (
            received,
            own,
            out_grad,
            out_new,
            out_second,
            swiglu_grad,
            swiglu_new,
            swiglu_second,
            down_grad,
            down_new,
            down_second,
        )
    )
    normed_grad = total(own, received)
    gain_rows = jnp.stack([tie((gains[0], *received))[0] / norm_gains[0], mlp_gain_grad])
    gain_sums = sum_everywhere(
        jnp.concatenate([gain_rows, qknorm_part], axis=1), ("tensor", "dp")
    )
    norm_grad, qknorm_grad = gain_sums[:, :MODEL_WIDTH], gain_sums[:, MODEL_WIDTH:]
    norm_new, norm_second = adamw(norm_gains, norm_grad, norm_mean, norm_square, gain_rate)
    qknorm_new, qknorm_second = adamw(
        qknorm_gains, qknorm_grad, qknorm_mean, qknorm_square, gain_rate
    )
    (input_norm_grad,) = norm_one_back(normed_grad)
    input_grad = (hidden_grad + input_norm_grad).astype(jnp.bfloat16)
    in_new, in_second = adamw(
        input_projection_weight,
        in_grad,
        input_first_moment,
        input_second_moment,
        MODEL_WIDTH ** (-0.5),
    )
    return (
        outputs,
        input_grad,
        in_grad,
        in_new,
        in_second,
        out_grad,
        out_new,
        out_second,
        swiglu_grad,
        swiglu_new,
        swiglu_second,
        down_grad,
        down_new,
        down_second,
        norm_grad,
        norm_new,
        norm_second,
        qknorm_grad,
        qknorm_new,
        qknorm_second,
    )


def solution(mesh):
    return jax.shard_map(
        local,
        mesh=mesh,
        in_specs=(
            P(("dp", "tensor"), None),
            P("dp", "tensor", None),
            P("dp", "tensor", None),
            P("dp", "tensor", None),
            P("tensor", "dp"),
            P("tensor", "dp"),
            P("tensor", "dp"),
            P("dp", None, "tensor"),
            P("dp", None, "tensor"),
            P("dp", None, "tensor"),
            P("tensor", "dp"),
            P("tensor", "dp"),
            P("tensor", "dp"),
            P(),
            P(),
            P(),
            P(),
            P(),
            P(),
            P(("dp", "tensor"), None),
        ),
        out_specs=(
            P(("dp", "tensor"), None),
            P(("dp", "tensor"), None),
            P("dp", "tensor", None),
            P("dp", "tensor", None),
            P("dp", "tensor", None),
            P("tensor", "dp"),
            P("tensor", "dp"),
            P("tensor", "dp"),
            P("dp", None, "tensor"),
            P("dp", None, "tensor"),
            P("dp", None, "tensor"),
            P("tensor", "dp"),
            P("tensor", "dp"),
            P("tensor", "dp"),
            P(),
            P(),
            P(),
            P(),
            P(),
            P(),
        ),
        check_vma=False,
    )
```

time: 987 us -> 774 us (0.78)
  Pallas kernels: 57.2 us -> 333 us
  matrix products: 269 us -> 0 us
  waiting for transfers between devices: 379 us -> 210 us
  blocking collectives: 64.9 us -> 0 us
  local copies, waits for them, and re-layouts: 81.1 us -> 93.6 us
    pallas_call x2 -> x36, Pallas kernels: 57.2 us -> 333 us  [the longest x25 221 us: row_call(): pl.pallas_call(kernel, grid_spec=pltpu.PrefetchScalarGridSpec(num_scalar_...]
    dot_general x36 -> x0, matrix products: 269 us -> none  [the longest x16 104 us: contract_cols(): lax.dot_general(left, right, (((1,), (1,)), ((), ())), preferred_element_...]
    ppermute x4, waiting for transfers between devices: 88.1 us -> 1.85 us  [ring_gather(): lax.ppermute(from_left, 'tensor', ahead)]
    ppermute x4, waiting for transfers between devices: 86.7 us -> 16.9 us  [ring_gather(): lax.ppermute(from_right, 'tensor', back)]
    psum x1 -> x0, blocking collectives: 64.9 us -> none  [local(): lax.psum((jnp.stack([attn_gain_grad, mlp_gain_grad]), qknorm_part), ('dp'...]
    ppermute x16 -> x21, waiting for transfers between devices: 151 us -> 105 us  [the longest x4 63.7 us: ring_scatter(): going_ahead = lax.ppermute(to_right, 'tensor', ahead)]
    all_gather x1, waiting for transfers between devices: 0.01 us -> 33 us  [local(): in_matrix = lax.all_gather(in_low, 'dp', axis=0, tiled=True)]
    unnamed x261 -> x238, local copies, waits for them, and re-layouts: 45.4 us -> 73 us
  transfers between devices with their start and end apart: 40 -> 45, of which waited for: 21 -> 25; matrix products, arithmetic and copies ran while one was open for 34% -> 11% of each run, Pallas kernels for 6% -> 40%
where the time goes in v2:
time: 774 us; the launch traced here: 765 us
  Pallas kernels  333 us (43%)
  waiting for transfers between devices  210 us (27%)
  local copies, waits for them, and re-layouts  93.6 us (12%)
  other arithmetic  75.1 us (10%)
  starting transfers between devices  37.7 us (5%)
  between operations  15.6 us (2%)
    pallas_call x25, Pallas kernels, row_call(): pl.pallas_call(kernel, grid_spec=pltpu.PrefetchScalarGridSpec(num_scalar_...  221 us
    unnamed x238, local copies, waits for them, and re-layouts  73 us
    ppermute x4, waiting for transfers between devices, ring_scatter(): going_ahead = lax.ppermute(to_right, 'tensor', ahead)  63.7 us
    pallas_call x2, Pallas kernels, attention_backward(): pl.pallas_call(lambda *refs: attend_back_kernel(HEAD_WIDTH ** (-0.5), *re...  50.1 us
    all_gather x1, waiting for transfers between devices, local(): in_matrix = lax.all_gather(in_low, 'dp', axis=0, tiled=True)  33 us
    pallas_call x4, Pallas kernels, project(): pl.pallas_call(lambda *refs: project_kernel(len(blocks), *refs), grid_spe...  31.9 us
    ppermute x4, waiting for transfers between devices, ring_scatter(): going_ahead = lax.ppermute(low, 'tensor', ahead)  28.1 us
    ppermute x4, waiting for transfers between devices, ring_gather(): high = lax.ppermute(from_right[half:], 'tensor', back)  26.9 us
  transfers between devices with their start and end apart: 45, of which 25 were waited for; matrix products, arithmetic and copies ran while one was open for 11% of the time, Pallas kernels for 40%

profile of v2, /device:TPU:0, one launch (start us, length us, event | category | flops | bytes accessed | tf_op | source)
XLA Modules:
  0.0 765.1 jit_solution(12411266731715274793)
XLA Ops:
  27.1 33.0 %all-gather.5.cloned.1.call-done.refs_2_.refs_3_ = bf16[2048,1024]{1,0:T(8,128)(2,1)} async-done(((bf16[256,1024]{1,0:T(8,128)(2,1)}), bf16[2048,1024]{1,0:T(8,128)(2,1)}) %all-gather.5.cloned.1.call-update) | async-done | bytes 4194320 | tf_op jit(solution)/shard_map/all_gather | solution.py:753
  110.3 20.7 %attend.1 = (bf16[2048,512]{1,0:T(8,128)(2,1)}, f32[2,4,2,512]{3,2,1,0:T(2,128)}) custom-call(bf16[2048,512]{1,0:T(8,128)(2,1)} %get-tuple-element.253.refs_0_.refs_1_, bf16[2048,256]{1,0:T(8,128)(2,1)} %get-tuple-element.179.refs_1_.refs_2_, bf16[2048,256]{1,0:T(8,128)(2,1)} %get-tuple-element.180.refs_2_.refs_3_), custom_call_target="tpu_custom_call" | custom-call | flops 1000000 | bytes 1000000 | tf_op jit(solution)/shard_map/attend/pallas_call | solution.py:504
  136.9 9.6 %collective-permute-done.7.refs_1_.refs_7_ = bf16[512,2048]{1,0:T(8,128)(2,1)} collective-permute-done((bf16[512,2048]{1,0:T(8,128)(2,1)S(1)}, bf16[512,2048]{1,0:T(8,128)(2,1)}, u32[]{:S(2)}, u32[]{:S(2)}) %collective-permute-start.7) | collective-permute-done | bytes 2097184 | tf_op jit(solution)/shard_map/ppermute | solution.py:110
  158.3 18.2 %collective-permute-done.9.refs_2_.refs_10_ = bf16[256,2048]{1,0:T(8,128)(2,1)S(1)} collective-permute-done((bf16[256,2048]{1,0:T(8,128)(2,1)S(1)}, bf16[256,2048]{1,0:T(8,128)(2,1)S(1)}, u32[]{:S(2)}, u32[]{:S(2)}) %collective-permute-start.9) | collective-permute-done | bytes 1048608 | tf_op jit(solution)/shard_map/ppermute | solution.py:119
  177.9 18.2 %collective-permute-done.4.ahead_ref = bf16[256,2048]{1,0:T(8,128)(2,1)S(1)} collective-permute-done((bf16[256,2048]{1,0:T(8,128)(2,1)S(1)}, bf16[256,2048]{1,0:T(8,128)(2,1)S(1)}, u32[]{:S(2)}, u32[]{:S(2)}) %collective-permute-start.4) | collective-permute-done | bytes 1048608 | tf_op jit(solution)/shard_map/ppermute | solution.py:164
  204.2 37.7 %collective-permute-done.10 = bf16[512,2048]{1,0:T(8,128)(2,1)S(1)} collective-permute-done((bf16[512,2048]{1,0:T(8,128)(2,1)S(1)}, bf16[512,2048]{1,0:T(8,128)(2,1)S(1)}, u32[]{:S(2)}, u32[]{:S(2)}) %collective-permute-start.10) | collective-permute-done | bytes 2097184 | tf_op jit(solution)/shard_map/ppermute | solution.py:172
  252.6 10.2 %gate_up.3 = (bf16[512,1536]{1,0:T(8,128)(2,1)S(1)}, bf16[512,1536]{1,0:T(8,128)(2,1)S(1)}, bf16[512,1536]{1,0:T(8,128)(2,1)S(1)}) custom-call(s32[6]{0:T(128)S(1)} %stack.34.refs_0_, bf16[512,2048]{1,0:T(8,128)(2,1)S(1)} %multiply_convert_fusion.refs_1_, bf16[2048,3072]{1,0:T(8,128)(2,1)S(1)} %copy-done, bf16[2048,3072]{1,0:T(8,128)(2,1)S(1)} %copy-done), custom_call_target="tpu_custom_call" | custom-call | flops 1000000 | bytes 1000000 | tf_op jit(solution)/shard_map/gate_up/pallas_call | solution.py:239
  266.3 9.5 %all-gather.11.cloned.1.call-done.refs_2_.refs_3_ = bf16[1536,2048]{1,0:T(8,128)(2,1)} async-done(((bf16[1536,256]{1,0:T(8,128)(2,1)}), bf16[1536,2048]{1,0:T(8,128)(2,1)}) %all-gather.11.cloned.1.call-update) | async-done | bytes 6291472 | tf_op jit(solution)/shard_map/all_gather | solution.py:756
  308.4 18.3 %gate_up.4 = (bf16[1024,1536]{1,0:T(8,128)(2,1)S(1)}, bf16[1024,1536]{1,0:T(8,128)(2,1)S(1)}, bf16[1024,1536]{1,0:T(8,128)(2,1)S(1)}) custom-call(s32[6]{0:T(128)S(1)} %stack.34.refs_0_, bf16[512,2048]{1,0:T(8,128)(2,1)} %collective-permute-done.13.refs_1_.refs_2_, bf16[512,2048]{1,0:T(8,128)(2,1)} %collective-permute-done.12.refs_2_.refs_3_, ...), custom_call_target="tpu_custom_call" | custom-call | flops 1000000 | bytes 1000000 | tf_op jit(solution)/shard_map/gate_up/pallas_call | solution.py:239
  336.7 10.2 %gate_up.5 = (bf16[512,1536]{1,0:T(8,128)(2,1)S(1)}, bf16[512,1536]{1,0:T(8,128)(2,1)S(1)}, bf16[512,1536]{1,0:T(8,128)(2,1)S(1)}) custom-call(s32[6]{0:T(128)S(1)} %stack.34.refs_0_, bf16[256,2048]{1,0:T(8,128)(2,1)S(1)} %copy-done.53, bf16[256,2048]{1,0:T(8,128)(2,1)S(1)} %copy-done.56, bf16[2048,3072]{1,0:T(8,128)(2,1)S(1)} %bitcast.15, ...), custom_call_target="tpu_custom_call" | custom-call | flops 1000000 | bytes 1000000 | tf_op jit(solution)/shard_map/gate_up/pallas_call | solution.py:239
  358.4 8.7 %block_product.19 = (bf16[256,2048]{1,0:T(8,128)(2,1)}, bf16[256,2048]{1,0:T(8,128)(2,1)}) custom-call(s32[6]{0:T(128)S(1)} %stack.34.refs_0_, bf16[512,3072]{1,0:T(8,128)(2,1)S(1)} %gate_up_grad.4.refs_1_.refs_9_.refs_10_, bf16[2048,3072]{1,0:T(8,128)(2,1)S(1)} %bitcast.15), custom_call_target="tpu_custom_call" | custom-call | flops 1000000 | bytes 1000000 | tf_op jit(solution)/shard_map/block_product/pallas_call | solution.py:239
  371.2 12.7 %gate_up_grad.5.refs_1_.refs_7_.refs_8_ = bf16[1024,3072]{1,0:T(8,128)(2,1)S(1)} custom-call(s32[6]{0:T(128)S(1)} %stack.34.refs_0_, bf16[512,2048]{1,0:T(8,128)(2,1)} %collective-permute-done.7.refs_1_.refs_7_, bf16[512,2048]{1,0:T(8,128)(2,1)} %collective-permute-done.6.refs_2_.refs_8_, bf16[1536,2048]{1,0:T(8,128)(2,1)} %all-gather.11.cloned.1.call-done.refs_2_.refs_3_, ...), custom_call_target="tpu_custom_call" | custom-call | flops 1000000 | bytes 1000000 | tf_op jit(solution)/shard_map/gate_up_grad/pallas_call | solution.py:239
  383.8 18.2 %block_product.20.pair_ref = bf16[1024,2048]{1,0:T(8,128)(2,1)S(1)} custom-call(s32[6]{0:T(128)S(1)} %stack.34.refs_0_, bf16[1024,3072]{1,0:T(8,128)(2,1)S(1)} %gate_up_grad.5.refs_1_.refs_7_.refs_8_, bf16[2048,3072]{1,0:T(8,128)(2,1)} %all-gather.9.cloned.1.call-done.refs_2_.refs_3_.refs_4_), custom_call_target="tpu_custom_call" | custom-call | flops 1000000 | bytes 1000000 | tf_op jit(solution)/shard_map/block_product/pallas_call | solution.py:239
  408.5 17.4 %weight_grad.4 = bf16[1536,2048]{1,0:T(8,128)(2,1)S(1)} custom-call(s32[6]{0:T(128)S(1)} %stack.34.refs_0_, bf16[512,1536]{1,0:T(8,128)(2,1)S(1)} %copy-done.46, bf16[1024,1536]{1,0:T(8,128)(2,1)S(1)} %get-tuple-element.240.refs_2_.refs_3_.refs_1_, bf16[1024,1536]{1,0:T(8,128)(2,1)S(1)} %get-tuple-element.240.refs_2_.refs_3_.refs_1_, ...), custom_call_target="tpu_custom_call" | custom-call | flops 1000000 | bytes 1000000 | tf_op jit(solution)/shard_map/weight_grad/pallas_call | solution.py:239
  428.6 24.4 %collective-permute-done.18 = bf16[512,2048]{1,0:T(8,128)(2,1)} collective-permute-done((bf16[512,2048]{1,0:T(8,128)(2,1)}, bf16[512,2048]{1,0:T(8,128)(2,1)}, u32[]{:S(2)}, u32[]{:S(2)}) %collective-permute-start.18) | collective-permute-done | bytes 2097184 | tf_op jit(solution)/shard_map/ppermute | solution.py:172
  475.7 31.1 %weight_grad.5 = bf16[2048,3072]{1,0:T(8,128)(2,1)} custom-call(s32[6]{0:T(128)S(1)} %stack.34.refs_0_, bf16[512,2048]{1,0:T(8,128)(2,1)S(1)} %copy-done.35, bf16[512,2048]{1,0:T(8,128)(2,1)} %collective-permute-done.13.refs_1_.refs_2_, bf16[512,2048]{1,0:T(8,128)(2,1)} %collective-permute-done.12.refs_2_.refs_3_, bf16[256,2048]{1,0:T(8,128)(2,1)S(1)} %copy-done.54, ...), custom_call_target="tpu_custom_call" | custom-call | flops 1000000 | bytes 1000000 | tf_op jit(solution)/shard_map/weight_grad/pallas_call | solution.py:239
  526.6 12.9 %collective-permute-done.22.refs_1_.refs_9_ = bf16[256,2048]{1,0:T(8,128)(2,1)S(1)} collective-permute-done((bf16[256,2048]{1,0:T(8,128)(2,1)S(1)}, bf16[256,2048]{1,0:T(8,128)(2,1)S(1)}, u32[]{:S(2)}, u32[]{:S(2)}) %collective-permute-start.22) | collective-permute-done | bytes 1048608 | tf_op jit(solution)/shard_map/ppermute | solution.py:118
  549.5 8.5 %block_product.25.pair_ref = bf16[1024,2048]{1,0:T(8,128)(2,1)S(1)} custom-call(s32[6]{0:T(128)S(1)} %stack.34.refs_0_, bf16[1024,1536]{1,0:T(8,128)(2,1)S(1)} %copy-done.32, bf16[1536,2048]{1,0:T(8,128)(2,1)S(1)} %bitcast.19), custom_call_target="tpu_custom_call" | custom-call | flops 1000000 | bytes 1000000 | tf_op jit(solution)/shard_map/block_product/pallas_call | solution.py:239
  558.0 10.0 %collective-permute-done.24.ahead_ref = bf16[256,2048]{1,0:T(8,128)(2,1)S(1)} collective-permute-done((bf16[256,2048]{1,0:T(8,128)(2,1)S(1)}, bf16[256,2048]{1,0:T(8,128)(2,1)S(1)}, u32[]{:S(2)}, u32[]{:S(2)}) %collective-permute-start.24) | collective-permute-done | bytes 1048608 | tf_op jit(solution)/shard_map/ppermute | solution.py:164
  574.9 9.3 %weight_grad.6 = bf16[512,2048]{1,0:T(8,128)(2,1)} custom-call(s32[6]{0:T(128)S(1)} %stack.34.refs_0_, bf16[2048,512]{1,0:T(8,128)(2,1)S(1)} %copy-done.11, bf16[2048,512]{1,0:T(8,128)(2,1)S(1)} %copy-done.11, bf16[2048,512]{1,0:T(8,128)(2,1)S(1)} %copy-done.11, bf16[2048,512]{1,0:T(8,128)(2,1)S(1)} %copy-done.11, bf16[2048,512]{1,0:T(8,128)(2,1)S(1)} %copy-done.11, ...), custom_call_target="tpu_custom_call" | custom-call | flops 1000000 | bytes 1000000 | tf_op jit(solution)/shard_map/weight_grad/pallas_call | solution.py:239
  584.2 25.1 %attend_back.2 = (bf16[2048,1024]{1,0:T(8,128)(2,1)}, f32[2,128]{1,0:T(2,128)}) custom-call(s32[4]{0:T(128)} %compare_select_fusion.5.refs_0_, bf16[2048,512]{1,0:T(8,128)(2,1)} %get-tuple-element.253.refs_0_.refs_1_, bf16[2048,256]{1,0:T(8,128)(2,1)} %get-tuple-element.179.refs_1_.refs_2_, bf16[2048,256]{1,0:T(8,128)(2,1)} %get-tuple-element.180.refs_2_.refs_3_, ...), custom_call_target="tpu_custom_call" | custom-call | flops 1000000 | bytes 1000000 | tf_op jit(solution)/shard_map/attend_back/pallas_call | solution.py:647
  609.3 25.0 %attend_back.3 = (bf16[2048,1024]{1,0:T(8,128)(2,1)}, f32[2,128]{1,0:T(2,128)}) custom-call(s32[4]{0:T(128)} %compare_select_fusion.5.refs_0_, bf16[2048,512]{1,0:T(8,128)(2,1)} %get-tuple-element.253.refs_0_.refs_1_, bf16[2048,256]{1,0:T(8,128)(2,1)} %get-tuple-element.179.refs_1_.refs_2_, ...), custom_call_target="tpu_custom_call", output_to_operand_aliasing={{0}: (12, {})} | custom-call | flops 1000000 | bytes 1000000 | tf_op jit(solution)/shard_map/attend_back/pallas_call | solution.py:647
  655.4 12.5 %weight_grad.7 = bf16[2048,1024]{1,0:T(8,128)(2,1)S(1)} custom-call(s32[6]{0:T(128)S(1)} %stack.34.refs_0_, bf16[512,2048]{1,0:T(8,128)(2,1)S(1)} %copy-done.37, bf16[512,2048]{1,0:T(8,128)(2,1)} %collective-permute-done.1.refs_1_.refs_2_, bf16[512,2048]{1,0:T(8,128)(2,1)} %collective-permute-done.refs_1_.refs_3_, ...), custom_call_target="tpu_custom_call" | custom-call | flops 1000000 | bytes 1000000 | tf_op jit(solution)/shard_map/weight_grad/pallas_call | solution.py:239
  714.4 11.8 %fusion.7 = (f32[256,2,1536]{2,1,0:T(2,128)}, f32[256,2,1536]{2,1,0:T(2,128)}) fusion(f32[256,2,1536]{2,1,0:T(2,128)S(1)} %copy-done.83, f32[256,2,1536]{2,1,0:T(2,128)S(1)} %copy-done.88, f32[256,2,1536]{2,1,0:T(2,128)S(1)} %copy-done.82, f32[256,2,1536]{2,1,0:T(2,128)} %param.28), kind=kLoop, calls=%fused_computation.23 | loop fusion | flops 10223616 | bytes 18874368 | tf_op jit(solution)/shard_map/add | solution.py:61
  (403 shorter events, 336.6 us)
Async XLA Ops:
  7.2 52.9 %all-gather.5.cloned.1.call-start = ((), (), s32[]{:S(2)}) async-start(), calls=%async_computation.4 | async-start | bytes 4718592 | tf_op jit(solution)/shard_map/all_gather | solution.py:753
  9.9 121.1 %all-gather.7.cloned.1.call-start = ((), (), s32[]{:S(2)}) async-start(), calls=%async_computation.5 | async-start | bytes 2359296 | tf_op jit(solution)/shard_map/all_gather | solution.py:754
  11.7 231.6 %all-gather.9.cloned.1.call-start = ((), (), s32[]{:S(2)}) async-start(), calls=%async_computation.6 | async-start | bytes 14155776 | tf_op jit(solution)/shard_map/all_gather | solution.py:755
  14.3 261.5 %all-gather.11.cloned.1.call-start = ((), (), s32[]{:S(2)}) async-start(), calls=%async_computation.7 | async-start | bytes 7077888 | tf_op jit(solution)/shard_map/all_gather | solution.py:756
  17.2 50.6 %collective-permute-start.1 = (bf16[512,2048]{1,0:T(8,128)(2,1)S(1)}, bf16[512,2048]{1,0:T(8,128)(2,1)}, u32[]{:S(2)}, u32[]{:S(2)}) collective-permute-start(bf16[512,2048]{1,0:T(8,128)(2,1)S(1)} %fusion.5.refs_1_), channel_id=1, source_target_pairs={{1,0},{3,1},{2,3},{0,2},{5,4},{7,5},{6,7},{4,6},{9,8},{11,9},{10,1... | collective-permute-start | bytes 6291464 | tf_op jit(solution)/shard_map/ppermute | solution.py:110
  20.2 47.6 %collective-permute-start = (bf16[512,2048]{1,0:T(8,128)(2,1)S(1)}, bf16[512,2048]{1,0:T(8,128)(2,1)}, u32[]{:S(2)}, u32[]{:S(2)}) collective-permute-start(bf16[512,2048]{1,0:T(8,128)(2,1)S(1)} %fusion.5.refs_1_), channel_id=1, source_target_pairs={{0,1},{1,3},{3,2},{2,0},{4,5},{5,7},{7,6},{6,4},{8,9},{9,11},{11,1... | collective-permute-start | bytes 6291464 | tf_op jit(solution)/shard_map/ppermute | solution.py:109
  21.3 613.1 %reduce-scatter.5.cloned.1.call-start = ((), (), s32[]{:S(2)}) async-start(), calls=%async_computation.8 | async-start | bytes 7077888 | tf_op jit(solution)/shard_map/reduce_scatter | solution.py:835
  99.8 46.7 %collective-permute-start.7 = (bf16[512,2048]{1,0:T(8,128)(2,1)S(1)}, bf16[512,2048]{1,0:T(8,128)(2,1)}, u32[]{:S(2)}, u32[]{:S(2)}) collective-permute-start(bf16[512,2048]{1,0:T(8,128)(2,1)S(1)} %copy-done.38), channel_id=1, source_target_pairs={{1,0},{3,1},{2,3},{0,2},{5,4},{7,5},{6,7},{4,6},{9,8},{11,9},{10,1... | collective-permute-start | bytes 6291464 | tf_op jit(solution)/shard_map/ppermute | solution.py:110
  101.2 46.5 %collective-permute-start.6 = (bf16[512,2048]{1,0:T(8,128)(2,1)S(1)}, bf16[512,2048]{1,0:T(8,128)(2,1)}, u32[]{:S(2)}, u32[]{:S(2)}) collective-permute-start(bf16[512,2048]{1,0:T(8,128)(2,1)S(1)} %copy-done.38), channel_id=1, source_target_pairs={{0,1},{1,3},{3,2},{2,0},{4,5},{5,7},{7,6},{6,4},{8,9},{9,11},{11,1... | collective-permute-start | bytes 6291464 | tf_op jit(solution)/shard_map/ppermute | solution.py:109
  152.4 43.7 %collective-permute-start.4 = (bf16[256,2048]{1,0:T(8,128)(2,1)S(1)}, bf16[256,2048]{1,0:T(8,128)(2,1)S(1)}, u32[]{:S(2)}, u32[]{:S(2)}) collective-permute-start(bf16[256,2048]{1,0:T(8,128)(2,1)S(1)} %get-tuple-element.184), channel_id=1, source_target_pairs={{0,1},{1,3},{3,2},{2,0},{4,5},{5,7},{7,6},{6,4},{8,9},{9,11},{11,1... | collective-permute-start | bytes 3145736 | tf_op jit(solution)/shard_map/ppermute | solution.py:164
  153.0 43.1 %collective-permute-start.5 = (bf16[256,2048]{1,0:T(8,128)(2,1)S(1)}, bf16[256,2048]{1,0:T(8,128)(2,1)S(1)}, u32[]{:S(2)}, u32[]{:S(2)}) collective-permute-start(bf16[256,2048]{1,0:T(8,128)(2,1)S(1)} %get-tuple-element.185), channel_id=1, source_target_pairs={{1,0},{3,1},{2,3},{0,2},{5,4},{7,5},{6,7},{4,6},{9,8},{11,9},{10,1... | collective-permute-start | bytes 3145736 | tf_op jit(solution)/shard_map/ppermute | solution.py:165
  197.5 44.5 %collective-permute-start.10 = (bf16[512,2048]{1,0:T(8,128)(2,1)S(1)}, bf16[512,2048]{1,0:T(8,128)(2,1)S(1)}, u32[]{:S(2)}, u32[]{:S(2)}) collective-permute-start(bf16[512,2048]{1,0:T(8,128)(2,1)S(1)} %get-tuple-element.194), channel_id=1, source_target_pairs={{0,1},{1,3},{3,2},{2,0},{4,5},{5,7},{7,6},{6,4},{8,9},{9,11},{11,1... | collective-permute-start | bytes 6291464 | tf_op jit(solution)/shard_map/ppermute | solution.py:172
  198.9 44.3 %collective-permute-start.11 = (bf16[512,2048]{1,0:T(8,128)(2,1)S(1)}, bf16[512,2048]{1,0:T(8,128)(2,1)}, u32[]{:S(2)}, u32[]{:S(2)}) collective-permute-start(bf16[512,2048]{1,0:T(8,128)(2,1)S(1)} %get-tuple-element.195), channel_id=1, source_target_pairs={{1,0},{3,1},{2,3},{0,2},{5,4},{7,5},{6,7},{4,6},{9,8},{11,9},{10,1... | collective-permute-start | bytes 6291464 | tf_op jit(solution)/shard_map/ppermute | solution.py:173
  250.2 53.3 %collective-permute-start.13 = (bf16[512,2048]{1,0:T(8,128)(2,1)S(1)}, bf16[512,2048]{1,0:T(8,128)(2,1)}, u32[]{:S(2)}, u32[]{:S(2)}) collective-permute-start(bf16[512,2048]{1,0:T(8,128)(2,1)S(1)} %multiply_convert_fusion.refs_1_), channel_id=1, source_target_pairs={{1,0},{3,1},{2,3},{0,2},{5,4},{7,5},{6,7},{4,6},{9,8},{11,9},{10,1... | collective-permute-start | bytes 6291464 | tf_op jit(solution)/shard_map/ppermute | solution.py:110
  250.9 52.6 %collective-permute-start.12 = (bf16[512,2048]{1,0:T(8,128)(2,1)S(1)}, bf16[512,2048]{1,0:T(8,128)(2,1)}, u32[]{:S(2)}, u32[]{:S(2)}) collective-permute-start(bf16[512,2048]{1,0:T(8,128)(2,1)S(1)} %multiply_convert_fusion.refs_1_), channel_id=1, source_target_pairs={{0,1},{1,3},{3,2},{2,0},{4,5},{5,7},{7,6},{6,4},{8,9},{9,11},{11,1... | collective-permute-start | bytes 6291464 | tf_op jit(solution)/shard_map/ppermute | solution.py:109
  406.5 46.5 %collective-permute-start.18 = (bf16[512,2048]{1,0:T(8,128)(2,1)}, bf16[512,2048]{1,0:T(8,128)(2,1)}, u32[]{:S(2)}, u32[]{:S(2)}) collective-permute-start(bf16[512,2048]{1,0:T(8,128)(2,1)} %get-tuple-element.222), channel_id=1, source_target_pairs={{0,1},{1,3},{3,2},{2,0},{4,5},{5,7},{7,6},{6,4},{8,9},{9,11},{11,1... | collective-permute-start | bytes 6291464 | tf_op jit(solution)/shard_map/ppermute | solution.py:172
  407.9 46.3 %collective-permute-start.19 = (bf16[512,2048]{1,0:T(8,128)(2,1)}, bf16[512,2048]{1,0:T(8,128)(2,1)}, u32[]{:S(2)}, u32[]{:S(2)}) collective-permute-start(bf16[512,2048]{1,0:T(8,128)(2,1)} %get-tuple-element.223), channel_id=1, source_target_pairs={{1,0},{3,1},{2,3},{0,2},{5,4},{7,5},{6,7},{4,6},{9,8},{11,9},{10,1... | collective-permute-start | bytes 6291464 | tf_op jit(solution)/shard_map/ppermute | solution.py:173
  454.2 231.3 %reduce-scatter.9.cloned.1.call-start = ((), (), s32[]{:S(2)}) async-start(), calls=%async_computation.10 | async-start | bytes 14155776 | tf_op jit(solution)/shard_map/reduce_scatter | solution.py:859
  468.7 45.4 %collective-permute-start.21 = (bf16[512,2048]{1,0:T(8,128)(2,1)}, bf16[512,2048]{1,0:T(8,128)(2,1)}, u32[]{:S(2)}, u32[]{:S(2)}) collective-permute-start(bf16[512,2048]{1,0:T(8,128)(2,1)} %get-tuple-element.229.refs_1_.refs_6_), channel_id=1, source_target_pairs={{1,0},{3,1},{2,3},{0,2},{5,4},{7,5},{6,7},{4,6},{9,8},{11,9},{10,1... | collective-permute-start | bytes 6291464 | tf_op jit(solution)/shard_map/ppermute | solution.py:110
  469.2 45.5 %collective-permute-start.20 = (bf16[512,2048]{1,0:T(8,128)(2,1)}, bf16[512,2048]{1,0:T(8,128)(2,1)}, u32[]{:S(2)}, u32[]{:S(2)}) collective-permute-start(bf16[512,2048]{1,0:T(8,128)(2,1)} %get-tuple-element.229.refs_1_.refs_6_), channel_id=1, source_target_pairs={{0,1},{1,3},{3,2},{2,0},{4,5},{5,7},{7,6},{6,4},{8,9},{9,11},{11,1... | collective-permute-start | bytes 6291464 | tf_op jit(solution)/shard_map/ppermute | solution.py:109
  514.8 183.8 %reduce-scatter.7.cloned.1.call-start = ((), (), s32[]{:S(2)}) async-start(), calls=%async_computation.9 | async-start | bytes 2359296 | tf_op jit(solution)/shard_map/reduce_scatter | solution.py:894
  572.1 62.2 %collective-permute-start.26 = (bf16[512,2048]{1,0:T(8,128)(2,1)}, bf16[512,2048]{1,0:T(8,128)(2,1)}, u32[]{:S(2)}, u32[]{:S(2)}) collective-permute-start(bf16[512,2048]{1,0:T(8,128)(2,1)} %get-tuple-element.245), channel_id=1, source_target_pairs={{0,1},{1,3},{3,2},{2,0},{4,5},{5,7},{7,6},{6,4},{8,9},{9,11},{11,1... | collective-permute-start | bytes 6291464 | tf_op jit(solution)/shard_map/ppermute | solution.py:172
  572.8 61.6 %collective-permute-start.27 = (bf16[512,2048]{1,0:T(8,128)(2,1)}, bf16[512,2048]{1,0:T(8,128)(2,1)}, u32[]{:S(2)}, u32[]{:S(2)}) collective-permute-start(bf16[512,2048]{1,0:T(8,128)(2,1)} %get-tuple-element.246), channel_id=1, source_target_pairs={{1,0},{3,1},{2,3},{0,2},{5,4},{7,5},{6,7},{4,6},{9,8},{11,9},{10,1... | collective-permute-start | bytes 6291464 | tf_op jit(solution)/shard_map/ppermute | solution.py:173
  634.4 116.3 %reduce-scatter.11.cloned.1.call-start = ((), (), s32[]{:S(2)}) async-start(), calls=%async_computation.11 | async-start | bytes 4718592 | tf_op jit(solution)/shard_map/reduce_scatter | solution.py:927
  (139 other events, 1480.4 us)
Sparse Core Ops, SparseCore 0:
  10.2 49.8 all-gather.4
  62.3 29.9 all-gather.6
  94.5 115.7 all-gather.8
  212.3 63.3 all-gather.10
  454.3 67.0 reduce-scatter.4
  523.6 127.5 reduce-scatter.8
  653.5 34.0 reduce-scatter.6
  690.0 48.7 reduce-scatter.10

commit v3 on v2

--- a/solution.py
+++ b/solution.py
@@ -98,102 +98,119 @@
         return values[0] if len(values) == 1 else values
 
 
-def ring_gather(rows, size, work, order, hold=()):
+def ring_near(blocks, size, work, order, hold=()):
     ahead, back = ring_pairs(size)
-    half = rows.shape[0] // 2
-    groups = [[rows]]
-    from_left = from_right = rows
-    work(0, groups[0])
+    tie = lax.optimization_barrier
+    groups = [list(blocks)]
+    left, right = list(blocks), list(blocks)
+    work(0, list(blocks))
     for step in range(1, size // 2):
-        from_left, from_right = (
-            lax.ppermute(from_left, "tensor", ahead),
-            lax.ppermute(from_right, "tensor", back),
-        )
+        left_low = lax.ppermute(left[0], "tensor", ahead)
+        right_high = lax.ppermute(right[1], "tensor", back)
+        left_high = lax.ppermute(left[1], "tensor", ahead)
+        right_low = lax.ppermute(right[0], "tensor", back)
         held = tuple(hold) if step == size // 2 - 1 else ()
-        from_left, from_right = lax.optimization_barrier(
-            (from_left, from_right) + held + order.last
-        )[:2]
-        groups.append([from_right, from_left])
-        work(step, groups[-1])
-    low = lax.ppermute(from_left[:half], "tensor", ahead)
-    high = lax.ppermute(from_right[half:], "tensor", back)
+        left_low, right_high = tie((left_low, right_high) + held + order.last)[:2]
+        left, right = [left_low, left_high], [right_low, right_high]
+        pair = tie((*right, *left) + order.last)[:4]
+        groups.append(list(pair))
+        work(step, list(pair))
+    return groups, (left[0], right[1])
+
+
+def ring_far(groups, carried, size, work, order):
+    ahead, back = ring_pairs(size)
+    low = lax.ppermute(carried[0], "tensor", ahead)
+    high = lax.ppermute(carried[1], "tensor", back)
     groups.append(list(lax.optimization_barrier((low, high) + order.last)[:2]))
-    work(size // 2, groups[-1])
+    work(size // 2, list(groups[-1]))
     return groups
 
 
-def relay_kernel(pair_ref, ahead_ref, back_ref, right_ref, left_ref):
-    rows = right_ref.shape[0]
-    taken = ahead_ref.shape[0]
-    for first, out_ref, got_ref, low in (
-        (0, right_ref, ahead_ref, 0),
-        (rows, left_ref, back_ref, rows - taken),
-    ):
-        out_ref[low : low + taken, :] = (
-            pair_ref[first + low : first + low + taken, :].astype(jnp.float32)
-            + got_ref[...].astype(jnp.float32)
+def ring_gather(blocks, size, work, order, hold=()):
+    groups, carried = ring_near(blocks, size, work, order, hold)
+    return ring_far(groups, carried, size, work, order)
+
+
+def relay_kernel(count, *refs):
+    for i in range(count):
+        refs[2 * count + i][...] = (
+            refs[i][...].astype(jnp.float32) + refs[count + i][...].astype(jnp.float32)
         ).astype(jnp.bfloat16)
-        if taken < rows:
-            rest = rows - taken - low
-            out_ref[rest : rest + rows - taken, :] = pair_ref[
-                first + rest : first + rest + rows - taken, :
-            ].astype(jnp.bfloat16)
-
-
-def relay(pair, going_ahead, going_back):
-    rows, width = pair.shape[0] // 2, pair.shape[1]
-    tile = tile_of(width, 512)
-    spec = lambda count: pl.BlockSpec((count, tile), lambda i: (0, i))
+
+
+def relay(terms, got):
+    rows, width = terms[0].shape
+    spec = pl.BlockSpec((rows, tile_of(width, 512)), lambda i: (0, i))
+    count = len(terms)
     return pl.pallas_call(
-        relay_kernel,
-        grid=(width // tile,),
-        in_specs=[spec(2 * rows), spec(going_ahead.shape[0]), spec(going_back.shape[0])],
-        out_specs=[spec(rows)] * 2,
-        out_shape=[jax.ShapeDtypeStruct((rows, width), jnp.bfloat16)] * 2,
+        lambda *refs: relay_kernel(count, *refs),
+        grid=(width // tile_of(width, 512),),
+        in_specs=[spec] * (2 * count),
+        out_specs=[spec] * count,
+        out_shape=[jax.ShapeDtypeStruct((rows, width), jnp.bfloat16)] * count,
         compiler_params=kernel_params(),
         cost_estimate=SMALL_COST,
         name="relay",
-    )(pair, going_ahead, going_back)
-
-
-def ring_scatter(size, part, order, hold=(), first=(), between=None, got=None):
+    )(*terms, *got)
+
+
+def ring_scatter(
+    size, part, order, hold=(), first=(), between=None, after=None, got=None, came=None,
+    eager=True,
+):
     ahead, back = ring_pairs(size)
+    send = lambda value, pairs: lax.ppermute(value, "tensor", pairs)
     low, high = part(size // 2)
     if hold:
         low, high = lax.optimization_barrier((low, high) + tuple(hold))[:2]
-    going_ahead = lax.ppermute(low, "tensor", ahead)
-    going_back = lax.ppermute(high, "tensor", back)
+    from_left, from_right = [send(low, ahead), None], [None, send(high, back)]
     for step in range(size // 2 - 1, 0, -1):
-        pair = part(step)
-        going_ahead, going_back = order.turn(going_ahead, going_back, *first)[:2]
-        to_right, to_left = order.mark(*relay(pair, going_ahead, going_back))
+        right_low, right_high, left_low, left_high = part(step)
+        full = from_left[1] is not None
+        if not full:
+            if eager:
+                early = send(right_high, ahead), send(left_low, back)
+            if between is not None:
+                between()
+        arrived = [from_left[0], from_right[1]] + ([from_left[1], from_right[0]] if full else [])
+        waited = (*first, *early) if eager and not full else tuple(first)
+        if came is not None and not full:
+            came[:] = arrived
+        tied = order.turn(*arrived, *waited)
+        arrived = tied[: len(arrived)]
+        if eager and not full:
+            early = tied[len(tied) - 2 :]
+        terms = [right_low, left_high] + ([right_high, left_low] if full else [])
+        passed = order.mark(*relay(terms, arrived))
         if got is not None:
-            got[:] = [to_right, to_left]
-        going_ahead = lax.ppermute(to_right, "tensor", ahead)
-        going_back = lax.ppermute(to_left, "tensor", back)
-    if between is not None:
-        between()
+            got[:] = passed
+        if full:
+            early = send(passed[2], ahead), send(passed[3], back)
+        elif not eager:
+            right_high, left_low = order.turn(right_high, left_low)
+            early = send(right_high, ahead), send(left_low, back)
+        from_left = [send(passed[0], ahead), early[0]]
+        from_right = [early[1], send(passed[1], back)]
+    if after is not None:
+        after()
     own = part(0)
     if size == 2:
-        return own, (jnp.concatenate([going_ahead, going_back], axis=0),)
-    return own, (going_ahead, going_back)
-
-
-def total(own, received):
-    return own + sum(block.astype(jnp.float32) for block in received)
-
-
-def sum_everywhere(values, axes):
-    for axis in axes:
-        size = lax.axis_size(axis)
-        if size & (size - 1):
-            values = lax.psum(values, axis)
-            continue
-        reach = 1
-        while reach < size:
-            pairs = [(i, i ^ reach) for i in range(size)]
-            values = values + lax.ppermute(values, axis, pairs)
-            reach *= 2
+        return own, [from_left[0]], [from_right[1]]
+    return own, [from_left[0], from_right[0]], [from_left[1], from_right[1]]
+
+
+def sum_over(values, axis, beside=()):
+    size = lax.axis_size(axis)
+    if size & (size - 1):
+        return lax.psum(values, axis)
+    reach, beside = 1, list(beside)
+    while reach < size:
+        pairs = [(i, i ^ reach) for i in range(size)]
+        values = values + lax.ppermute(values, axis, pairs)
+        if beside:
+            values = lax.optimization_barrier((values, beside.pop(0)))[0]
+        reach *= 2
     return values
 
 
@@ -201,7 +218,7 @@
     return next(t for t in (most, 512, 256, 128) if t <= most and width % t == 0)
 
 
-def kernel_params(mebibytes=32):
+def kernel_params(mebibytes=56):
     return pltpu.CompilerParams(vmem_limit_bytes=mebibytes * 1024 * 1024)
 
 
@@ -235,7 +252,9 @@
     return values[0] if len(values) == 1 else jnp.concatenate(values, axis=0)
 
 
-def row_call(kernel, name, table, grid, operands, specs, outs, out_specs, aliases=None):
+def row_call(
+    kernel, name, table, grid, operands, specs, outs, out_specs, aliases=None, mebibytes=56
+):
     return pl.pallas_call(
         kernel,
         grid_spec=pltpu.PrefetchScalarGridSpec(
@@ -243,7 +262,7 @@
         ),
         out_shape=outs,
         input_output_aliases=aliases or {},
-        compiler_params=kernel_params(),
+        compiler_params=kernel_params(mebibytes),
         cost_estimate=SMALL_COST,
         name=name,
     )(table, *operands)
@@ -253,13 +272,13 @@
     rows = stacked(refs[1 : 1 + count])
     matrix = refs[1 + count][...]
     result = contract_cols(rows, matrix) if crossed else product(rows, matrix)
-    outs = refs[-2:] if refs[-1].shape[0] < rows.shape[0] else refs[-1:]
-    size = rows.shape[0] // len(outs)
+    size = refs[-1].shape[0]
+    outs = refs[-(rows.shape[0] // size) :]
     for i, out_ref in enumerate(outs):
         out_ref[...] = result[i * size : (i + 1) * size].astype(out_ref.dtype)
 
 
-def block_product(table, pieces, matrix, crossed, kind=jnp.bfloat16, halves=False, into=None):
+def block_product(table, pieces, matrix, crossed, parts=1, into=None):
     width = matrix.shape[0] if crossed else matrix.shape[1]
     tile = tile_of(width, 512)
     count = sum(piece.count for piece in pieces)
@@ -277,10 +296,10 @@
             operands.append(so_far)
             specs.append(pl.BlockSpec(memory_space=pltpu.HBM))
             aliases = {len(operands): 0}
-    if halves:
-        count = all_rows = count // 2
+    if parts > 1:
+        count = all_rows = count // parts
     out_spec = pl.BlockSpec((count, tile), lambda i, table: (index, i))
-    out = jax.ShapeDtypeStruct((all_rows, width), kind)
+    out = jax.ShapeDtypeStruct((all_rows, width), jnp.bfloat16)
     result = row_call(
         lambda *refs: product_kernel(len(pieces), crossed, *refs),
         "block_product",
@@ -288,11 +307,12 @@
         (width // tile,),
         operands,
         specs,
-        [out] * (2 if halves else 1),
-        [out_spec] * (2 if halves else 1),
+        [out] * parts,
+        [out_spec] * parts,
         aliases,
-    )
-    return result if halves else result[0]
+        56 if matrix.size > 4 * 1024 * 1024 else 32,
+    )
+    return result if parts > 1 else result[0]
 
 
 def gate_kernel(count, *refs):
@@ -363,34 +383,145 @@
     )[0]
 
 
-def rows_kernel(count, *refs):
-    out_ref = refs[-1]
-    out_ref[...] = sum(
-        contract_rows(refs[1 + i][...], refs[1 + count + i][...]) for i in range(count)
-    ).astype(out_ref.dtype)
-
-
-def weight_gradient(table, lefts, rights):
+def rows_kernel(count, weighed, *refs):
+    out_ref = refs[2 * count + 1 + weighed]
+    result = sum(contract_rows(refs[1 + i][...], refs[1 + count + i][...]) for i in range(count))
+    out_ref[...] = result.astype(out_ref.dtype)
+    if weighed:
+        by_column = jnp.transpose(result * refs[2 * count + 1][...].astype(jnp.float32))
+        refs[-1][...] = jnp.sum(by_column, axis=0, keepdims=True)
+
+
+def weight_gradient(table, lefts, rights, weights=None):
     width, columns = lefts[0].array.shape[1], rights[0].array.shape[1]
     tile = tile_of(width, 256)
-    return row_call(
-        lambda *refs: rows_kernel(len(lefts), *refs),
+    weighed = weights is not None
+    block_spec = pl.BlockSpec((tile, columns), lambda i, table: (i, 0))
+    result = row_call(
+        lambda *refs: rows_kernel(len(lefts), weighed, *refs),
         "weight_grad",
         table,
         (width // tile,),
-        [piece.array for piece in lefts + rights],
-        [piece.spec(tile) for piece in lefts] + [piece.spec() for piece in rights],
-        [jax.ShapeDtypeStruct((width, columns), jnp.bfloat16)],
-        [pl.BlockSpec((tile, columns), lambda i, table: (i, 0))],
-    )[0]
-
-
-def split_groups(groups, rows):
-    own, *pairs, far = groups
-    pieces = [Piece(own)]
-    for pair in pairs:
-        pieces += [Piece(pair, rows, 0), Piece(pair, rows, 1)]
-    return pieces + [Piece(far, rows // 2, 0), Piece(far, rows // 2, 1)]
+        [piece.array for piece in lefts + rights] + ([weights] if weighed else []),
+        [piece.spec(tile) for piece in lefts]
+        + [piece.spec() for piece in rights]
+        + ([block_spec] if weighed else []),
+        [jax.ShapeDtypeStruct((width, columns), jnp.bfloat16)]
+        + ([jax.ShapeDtypeStruct((1, width), jnp.float32)] if weighed else []),
+        [block_spec] + ([pl.BlockSpec((1, tile), lambda i, table: (0, i))] if weighed else []),
+    )
+    return result if weighed else result[0]
+
+
+def split_groups(groups, half):
+    return [
+        Piece(array, half, i) for array in groups for i in range(array.shape[0] // half)
+    ]
+
+
+def arrived_sum(split, low_refs, high_refs):
+    low = sum(ref[...].astype(jnp.float32) for ref in low_refs)
+    high = sum(ref[...].astype(jnp.float32) for ref in high_refs)
+    return jnp.where(pl.program_id(0) < split, low, high)
+
+
+def half_specs(tile, split, width):
+    return (
+        pl.BlockSpec((tile, width), lambda i: (jnp.minimum(i, split - 1), 0)),
+        pl.BlockSpec((tile, width), lambda i: (jnp.maximum(i - split, 0), 0)),
+    )
+
+
+def put_half(split, low_ref, high_ref, value):
+    @pl.when(pl.program_id(0) < split)
+    def _():
+        low_ref[...] = value
+
+    @pl.when(pl.program_id(0) >= split)
+    def _():
+        high_ref[...] = value
+
+
+def row_kernel_call(kernel, name, whole, lows, highs, gain, outs):
+    rows, width = whole[0].shape
+    tile = min(rows // 2, 128)
+    split = rows // 2 // tile
+    spec = pl.BlockSpec((tile, width), lambda i: (i, 0))
+    low_spec, high_spec = half_specs(tile, split, width)
+    row_spec = pl.BlockSpec((1, width), lambda i: (0, 0))
+    shapes, specs = [], []
+    for out in outs:
+        if out == "halves":
+            shapes += [jax.ShapeDtypeStruct((rows // 2, width), jnp.bfloat16)] * 2
+            specs += [low_spec, high_spec]
+        elif out == "row":
+            shapes.append(jax.ShapeDtypeStruct((1, width), jnp.float32))
+            specs.append(row_spec)
+        else:
+            shapes.append(jax.ShapeDtypeStruct((rows, width), out))
+            specs.append(spec)
+    return pl.pallas_call(
+        lambda *refs: kernel(split, len(lows), *refs),
+        grid=(2 * split,),
+        in_specs=[spec] * len(whole)
+        + [low_spec] * len(lows)
+        + [high_spec] * len(highs)
+        + [row_spec],
+        out_specs=specs,
+        out_shape=shapes,
+        compiler_params=kernel_params(),
+        cost_estimate=SMALL_COST,
+        name=name,
+    )(*whole, *lows, *highs, gain)
+
+
+def add_norm_kernel(split, count, base_ref, own_ref, *refs):
+    gain_ref, sum_ref, low_ref, high_ref = refs[2 * count :]
+    values = base_ref[...].astype(jnp.float32) + own_ref[...].astype(jnp.float32)
+    values = values + arrived_sum(split, refs[:count], refs[count : 2 * count])
+    sum_ref[...] = values
+    put_half(split, low_ref, high_ref, rms_gain(values, gain_ref[...]).astype(jnp.bfloat16))
+
+
+def add_and_norm(base, own, lows, highs, gain):
+    outs = (jnp.float32, "halves")
+    return row_kernel_call(add_norm_kernel, "add_norm", [base, own], lows, highs, gain, outs)
+
+
+def add_kernel(split, count, base_ref, own_ref, *refs):
+    values = base_ref[...].astype(jnp.float32) + own_ref[...].astype(jnp.float32)
+    values = values + arrived_sum(split, refs[:count], refs[count : 2 * count])
+    refs[-1][...] = values.astype(jnp.bfloat16)
+
+
+def norm_gradient_kernel(split, count, base_ref, value_ref, own_ref, *refs):
+    gain_ref, outs = refs[2 * count], refs[2 * count + 1 :]
+    grad = own_ref[...].astype(jnp.float32)
+    grad = grad + arrived_sum(split, refs[:count], refs[count : 2 * count])
+    values = value_ref[...].astype(jnp.float32)
+    scale = lax.rsqrt(jnp.mean(values * values, axis=1, keepdims=True) + norm_eps)
+    unit = values * scale
+    inner = grad * gain_ref[...]
+    result = base_ref[...].astype(jnp.float32) + scale * (
+        inner - unit * jnp.mean(inner * unit, axis=1, keepdims=True)
+    )
+    if len(outs) == 1:
+        outs[0][...] = result.astype(jnp.bfloat16)
+        return
+    low_ref, high_ref, gain_out = outs
+    put_half(split, low_ref, high_ref, result.astype(jnp.bfloat16))
+
+    @pl.when(pl.program_id(0) == 0)
+    def _():
+        gain_out[...] = jnp.zeros_like(gain_out)
+
+    gain_out[...] += jnp.sum(grad * unit, axis=0, keepdims=True)
+
+
+def norm_gradient(base, values, own, lows, highs, gain, outs):
+    return row_kernel_call(
+        norm_gradient_kernel, "norm_gradient", [base, values, own], lows, highs, gain, outs
+    )
 
 
 def project_kernel(count, *refs):
@@ -718,7 +849,8 @@
     for step in range(1, last):
         group_places.append(places[2 * step - 1 : 2 * step + 1])
     group_places.append(places[-1:])
-    table = jnp.stack(places + [2 * places[-1], 2 * places[-1] + 1]).astype(jnp.int32)
+    halves = [2 * place + i for place in places for i in range(2)]
+    table = jnp.stack(places + halves).astype(jnp.int32)
     away = (ring_place(jnp.arange(size, dtype=jnp.int32), size) - me + size) % size
     slots = jnp.where(
         away == 0,
@@ -740,11 +872,16 @@
         return [Piece(array, rows, entry=entry) for entry in entries]
 
     def ordered_finely(array):
-        pieces = [Piece(array, rows, entry=entry) for entry in range(size - 1)]
-        return pieces + [Piece(array, half, entry=size + i) for i in range(2)]
+        return [Piece(array, half, entry=size + i) for i in range(2 * size)]
 
     def flat(groups):
         return pieces_of([block for group in groups for block in group])
+
+    def parts_of(group):
+        return 1 if group == 0 else 2 if group == last else 4
+
+    def marked(part):
+        return mark(*part) if isinstance(part, (list, tuple)) else mark(part)
 
     in_low = input_projection_weight.astype(jnp.bfloat16).reshape(dp_rows, -1)
     out_low = out_weight.astype(jnp.bfloat16)
@@ -755,13 +892,12 @@
     swiglu_matrix = lax.all_gather(swiglu_low, "dp", axis=0, tiled=True)
     down_full = lax.all_gather(down_low, "dp", axis=1, tiled=True)
 
-    inputs_f = inputs.astype(jnp.float32)
-    normed_f, norm_one_back = jax.vjp(lambda rows: rms_gain(rows, norm_gains[0]), inputs_f)
+    normed_f = rms_gain(inputs.astype(jnp.float32), norm_gains[0])
     cos, sin = rotary_tables(SEQUENCE_TOKENS, HEAD_WIDTH)
     projected = []
 
     def project_group(group, blocks):
-        calls = [blocks] if group in (0, last) else [[block] for block in blocks]
+        calls = [blocks] if group in (0, last) else [blocks[:2], blocks[2:]]
         for place, call in zip(group_places[group], calls):
             call[0] = turn(call[0])
             projected[:] = mark(
@@ -770,27 +906,30 @@
                 )
             )
 
+    normed = normed_f.astype(jnp.bfloat16)
     normed_groups = ring_gather(
-        normed_f.astype(jnp.bfloat16), size, project_group, order, hold=(in_matrix,)
+        (normed[:half], normed[half:]), size, project_group, order, hold=(in_matrix,)
     )
     query, key, value, query_raw, key_raw = projected
     cotangent_sent = tie((cotangent, *normed_groups[-1]))[0]
 
     context, logs = mark(*attention_forward(query, key, value, rows))
-    cot_groups = ring_gather(cotangent_sent, size, lambda group, blocks: None, Order())
+    cot_groups, cot_carried = ring_near(
+        (cotangent_sent[:half], cotangent_sent[half:]), size, lambda group, blocks: None, Order()
+    )
 
     def out_group(group):
-        kind = jnp.float32 if group == 0 else jnp.bfloat16
-        array = turn(context)
-        part = block_product(
-            table, ordered(array, group), out_full, False, kind, halves=group == last
+        return marked(
+            block_product(
+                table, ordered(turn(context), group), out_full, False, parts_of(group)
+            )
         )
-        return mark(*part) if group == last else mark(part)
-
-    own, received = ring_scatter(size, out_group, order, first=cot_groups[-1])
-    received = tie((*received, swiglu_matrix))[: len(received)]
-    hidden = inputs_f + total(own, received)
-    normed_two_f, norm_two_back = jax.vjp(rms_gain, hidden, norm_gains[1])
+
+    own, lows, highs = ring_scatter(
+        size, out_group, order, first=[half for group in cot_groups[1:] for half in group]
+    )
+    lows, highs = tie((lows, highs, swiglu_matrix))[:2]
+    hidden, *two_halves = mark(*add_and_norm(inputs, own, lows, highs, norm_gains[1:2]))
 
     gate_groups = []
     grads = [None] * (last + 1)
@@ -798,48 +937,61 @@
     def gate_group(group, blocks):
         blocks[0] = turn(blocks[0])
         gate_groups.append(mark(*gate_up_product(table, pieces_of(blocks), swiglu_matrix)))
-        if group == 0:
-            two_own.append(two_group(0))
-
-    def two_group(group):
+
+    two_groups, two_carried = ring_near(two_halves, size, gate_group, order)
+    two_groups = ring_far(two_groups, two_carried, size, gate_group, order)
+    cot_carried = tie((*cot_carried, *gate_groups[last - 1]))[:2]
+    cot_groups = ring_far(cot_groups, cot_carried, size, lambda group, blocks: None, order)
+    activated = [parts[0] for parts in gate_groups]
+    two_parts = [None] * (last + 1)
+
+    def two_grads(group):
         cots = [turn(cot_groups[group][0])] + cot_groups[group][1:]
         grads[group] = mark(
             gate_up_gradient(table, pieces_of(cots), down_full, *gate_groups[group][1:])
         )
-        kind = jnp.float32 if group == 0 else jnp.bfloat16
-        part = block_product(
-            table, [Piece(grads[group])], swiglu_matrix, True, kind, halves=group == last
+
+    def two_product(group):
+        two_parts[group] = marked(
+            block_product(
+                table, [Piece(turn(grads[group]))], swiglu_matrix, True, parts_of(group)
+            )
         )
-        return mark(*part) if group == last else mark(part)
-
-    two_own = []
-
-    two_groups = ring_gather(
-        normed_two_f.astype(jnp.bfloat16), size, gate_group, order, hold=(down_full,)
-    )
-    activated = [parts[0] for parts in gate_groups]
-    early = []
-
-    def down_gradient():
-        lefts = split_groups([turn(activated[0])] + activated[1:], rows)
-        early.append(mark(weight_gradient(table, lefts, flat(cot_groups))))
-
-    own, received = ring_scatter(
-        size,
-        lambda group: two_own[0] if group == 0 else two_group(group),
-        order,
-        between=down_gradient,
-    )
-    (down_part,) = early
-    down_part, *received = tie((down_part, *received))
+
+    for group in range(1, last):
+        two_grads(group)
+    lefts = split_groups([turn(activated[0])] + activated[1:], half)
+    down_part = mark(weight_gradient(table, lefts, flat(cot_groups)))
     down_grad = lax.psum_scatter(down_part, "dp", scatter_dimension=1, tiled=True)
-    received = turn(*received) if len(received) > 1 else (turn(*received),)
-    two_grad = total(own, received)
-    hidden_norm_grad, mlp_gain_grad = norm_two_back(two_grad)
-    hidden_grad = cotangent.astype(jnp.float32) + hidden_norm_grad
-
-    context_grad = [None]
+    for group in range(1, last):
+        two_product(group)
+    two_grads(last)
+    two_product(last)
     more = []
+
+    def own_part():
+        two_grads(0)
+        two_product(0)
+
+    def swiglu_gradient():
+        twos = flat(two_groups)
+        twos[0].array = turn(twos[0].array)
+        more.append(mark(weight_gradient(table, twos, split_groups(grads, half))))
+
+    if last == 1:
+        own_part()
+    own, lows, highs = ring_scatter(
+        size, lambda group: two_parts[group], order, between=own_part, after=swiglu_gradient
+    )
+    swiglu_part, lows, highs = tie((more[0], lows, highs))
+    swiglu_grad = lax.psum_scatter(swiglu_part, "dp", scatter_dimension=0, tiled=True)
+    *attended_halves, mlp_gain_grad = mark(
+        *norm_gradient(
+            cotangent, hidden, own, lows, highs, norm_gains[1:2], ("halves", "row")
+        )
+    )
+
+    context_grad, down_parts, new_down, head_grads = [None], [None] * (last + 1), [], []
 
     def context_group(group, blocks):
         blocks[0] = turn(blocks[0])
@@ -850,14 +1002,24 @@
             )
         )
         if group == 0:
-            twos = flat(two_groups)
-            twos[0].array = turn(twos[0].array)
-            more.append(mark(weight_gradient(table, twos, split_groups(grads, rows))))
-
-    attended_groups = ring_gather(hidden_grad.astype(jnp.bfloat16), size, context_group, order)
-    swiglu_part = tie((more[0], *attended_groups[last - 1]))[0]
-    swiglu_grad = lax.psum_scatter(swiglu_part, "dp", scatter_dimension=0, tiled=True)
-    head_grads, out_parts = [], []
+            for other in range(last, -1, -1):
+                down_parts[other] = marked(
+                    block_product(
+                        table, [Piece(turn(activated[other]))], down_full, False, parts_of(other)
+                    )
+                )
+            new_down[:] = mark(
+                turn(down_grad).astype(jnp.float32),
+                *adamw(
+                    down_weight,
+                    turn(down_grad).astype(jnp.float32),
+                    down_mean,
+                    down_square,
+                    FF ** (-0.5),
+                ),
+            )
+
+    attended_groups = ring_gather(attended_halves, size, context_group, order)
 
     def head_backward(head):
         head_grads.append(
@@ -870,117 +1032,111 @@
             )
         )
 
-    def down_group(group):
-        if group == 0:
-            for head in range(1, local_kv):
-                head_backward(head)
-        kind = jnp.float32 if group == 0 else jnp.bfloat16
-        part = block_product(
-            table, [Piece(turn(activated[group]))], down_full, False, kind, halves=group == last
-        )
-        part = mark(*part) if group == last else mark(part)
-        return part
-
-    def out_gradient():
-        out_parts.append(
-            mark(weight_gradient(table, ordered_finely(turn(context)), flat(attended_groups)))
-        )
+    out_part = mark(
+        weight_gradient(table, ordered_finely(turn(context)), flat(attended_groups))
+    )
+    if last == 1:
         head_backward(0)
 
-    own, received = ring_scatter(
-        size, down_group, order, hold=attended_groups[-1], between=out_gradient
-    )
-    out_part, down_grad = tie((out_parts[0], down_grad, *received, *head_grads[-1]))[:2]
-    out_grad = lax.psum_scatter(out_part, "dp", scatter_dimension=1, tiled=True)
-    outputs = (hidden + total(own, received)).astype(jnp.bfloat16)
+    def other_heads():
+        for head in range(1, local_kv):
+            head_backward(head)
+
+    own, lows, highs = ring_scatter(
+        size,
+        lambda group: down_parts[group],
+        order,
+        hold=attended_groups[-1],
+        between=lambda: head_backward(0),
+        after=other_heads,
+    )
+    (outputs,) = row_kernel_call(
+        add_kernel, "add", [hidden, own], lows, highs, norm_gains[0:1], (jnp.bfloat16,)
+    )
+    sent = lows + highs
     mixed_grad = head_grads[-1][0]
     qknorm_part = sum(pair[1] for pair in head_grads)
-    in_parts, gains = [], []
+    in_parts = []
 
     def normed_group(group):
-        kind = jnp.float32 if group == 0 else jnp.bfloat16
-        array = turn(mixed_grad)
-        part = block_product(
-            table, ordered(array, group), in_matrix, True, kind, halves=group == last
+        return marked(
+            block_product(
+                table, ordered(turn(mixed_grad), group), in_matrix, True, parts_of(group)
+            )
         )
-        part = mark(*part) if group == last else mark(part)
-        if group == last:
-            normeds = flat(normed_groups)
-            normeds[0].array = turn(normeds[0].array)
-            in_parts.append(
-                mark(weight_gradient(table, normeds, ordered_finely(mixed_grad)))
-            )
-        if group == 1 or last == 1:
-            gains.append(
-                mark(
-                    jnp.sum(
-                        turn(in_parts[0]).astype(jnp.float32) * in_matrix.astype(jnp.float32),
-                        axis=1,
-                    )
-                )
-            )
-        return part
-
-    got = []
-    own, received = ring_scatter(size, normed_group, order, hold=(outputs,), got=got)
-    in_part, swiglu_grad = tie((in_parts[0], swiglu_grad, *got))[:2]
+
+    def in_gradient():
+        normeds = flat(normed_groups)
+        normeds[0].array = turn(normeds[0].array)
+        in_parts[:] = mark(
+            *weight_gradient(table, normeds, ordered_finely(mixed_grad), in_matrix)
+        )
+
+    got, came = [], []
+    own, lows, highs = ring_scatter(
+        size, normed_group, order, between=in_gradient, got=got, came=came, eager=False
+    )
+    if not in_parts:
+        in_gradient()
+    rows_of_gains = jnp.concatenate([in_parts[1] / norm_gains[0:1], mlp_gain_grad], axis=0)
+    gain_sums = tie((jnp.concatenate([rows_of_gains, qknorm_part], axis=1), *got))[0]
+    gain_sums = sum_over(gain_sums, "tensor")
+    out_part, down_grad = tie((out_part, down_grad, *sent, mixed_grad))[:2]
+    out_grad = lax.psum_scatter(out_part, "dp", scatter_dimension=1, tiled=True)
+    in_part, swiglu_grad = tie((in_parts[0], swiglu_grad, *came))[:2]
     in_grad = lax.psum_scatter(in_part, "dp", scatter_dimension=0, tiled=True)
     in_grad = in_grad.astype(jnp.float32).reshape(input_projection_weight.shape)
-    out_grad, swiglu_grad, down_grad = tie((out_grad, swiglu_grad, down_grad, *got))[:3]
+    out_grad, swiglu_grad, outputs = tie((out_grad, swiglu_grad, outputs, *got))[:3]
+    out_grad = out_grad.astype(jnp.float32)
     swiglu_grad = swiglu_grad.astype(jnp.float32).reshape(swiglu_weight.shape)
-    out_grad, down_grad = out_grad.astype(jnp.float32), down_grad.astype(jnp.float32)
     out_new, out_second = adamw(
         out_weight, out_grad, out_mean, out_square, (HQ * HEAD_WIDTH / 8.0) ** (-0.5)
     )
     swiglu_new, swiglu_second = adamw(
         swiglu_weight, swiglu_grad, swiglu_mean, swiglu_square, MODEL_WIDTH ** (-0.5)
     )
-    down_new, down_second = adamw(down_weight, down_grad, down_mean, down_square, FF ** (-0.5))
+    down_grad, down_new, down_second = new_down
     (
-        received,
+        lows,
+        highs,
         own,
+        outputs,
         out_grad,
         out_new,
         out_second,
         swiglu_grad,
         swiglu_new,
         swiglu_second,
-        down_grad,
-        down_new,
-        down_second,
     ) = tie(
         (
-            received,
+            lows,
+            highs,
             own,
+            outputs,
             out_grad,
             out_new,
             out_second,
             swiglu_grad,
             swiglu_new,
             swiglu_second,
-            down_grad,
-            down_new,
-            down_second,
         )
     )
-    normed_grad = total(own, received)
-    gain_rows = jnp.stack([tie((gains[0], *received))[0] / norm_gains[0], mlp_gain_grad])
-    gain_sums = sum_everywhere(
-        jnp.concatenate([gain_rows, qknorm_part], axis=1), ("tensor", "dp")
-    )
-    norm_grad, qknorm_grad = gain_sums[:, :MODEL_WIDTH], gain_sums[:, MODEL_WIDTH:]
-    norm_new, norm_second = adamw(norm_gains, norm_grad, norm_mean, norm_square, gain_rate)
-    qknorm_new, qknorm_second = adamw(
-        qknorm_gains, qknorm_grad, qknorm_mean, qknorm_square, gain_rate
-    )
-    (input_norm_grad,) = norm_one_back(normed_grad)
-    input_grad = (hidden_grad + input_norm_grad).astype(jnp.bfloat16)
+    hidden_grad = jnp.concatenate(attended_halves, axis=0)
+    (input_grad,) = norm_gradient(
+        hidden_grad, inputs, own, lows, highs, norm_gains[0:1], (jnp.bfloat16,)
+    )
     in_new, in_second = adamw(
         input_projection_weight,
         in_grad,
         input_first_moment,
         input_second_moment,
         MODEL_WIDTH ** (-0.5),
+    )
+    gain_sums = sum_over(tie((gain_sums, *lows, *highs))[0], "dp", (input_grad, in_new))
+    norm_grad, qknorm_grad = gain_sums[:, :MODEL_WIDTH], gain_sums[:, MODEL_WIDTH:]
+    norm_new, norm_second = adamw(norm_gains, norm_grad, norm_mean, norm_square, gain_rate)
+    qknorm_new, qknorm_second = adamw(
+        qknorm_gains, qknorm_grad, qknorm_mean, qknorm_square, gain_rate
     )
     return (
         outputs,

time: 774 us -> 745 us (0.963)
  Pallas kernels: 333 us -> 411 us
  waiting for transfers between devices: 210 us -> 159 us
  local copies, waits for them, and re-layouts: 93.6 us -> 51.2 us
  other arithmetic: 75.1 us -> 42.5 us
  starting transfers between devices: 37.7 us -> 57 us
    pallas_call x4 -> x8, Pallas kernels: 9.93 us -> 49.4 us  [the longest x4 31.9 us: row_kernel_call(): pl.pallas_call(lambda *refs: kernel(split, len(lows), *refs), grid=(2 * s...]
    ppermute x37 -> x53, waiting for transfers between devices: 167 us -> 128 us  [the longest x24 61.5 us: ring_scatter(): send = lambda value, pairs: lax.ppermute(value, 'tensor', pairs)]
    pallas_call x25, Pallas kernels: 221 us -> 259 us  [row_call(): pl.pallas_call(kernel, grid_spec=pltpu.PrefetchScalarGridSpec(num_scalar_...]
    unnamed x238 -> x176, local copies, waits for them, and re-layouts: 73 us -> 42.7 us
    ppermute x37 -> x53, starting transfers between devices: 36.9 us -> 56.7 us  [the longest x24 25.3 us: ring_scatter(): send = lambda value, pairs: lax.ppermute(value, 'tensor', pairs)]
    convert_element_type x7 -> x2, other arithmetic: 20.5 us -> 1.38 us  [the longest x1 0.83 us: local(): out_grad = out_grad.astype(jnp.float32)]
    slice x9 -> x3, local copies, waits for them, and re-layouts: 13 us -> 0.98 us  [the longest x1 0.61 us: local(): norm_gains[1:2]]
    reduce_sum x3 -> x0, other arithmetic: 11.8 us -> none  [the longest x2 10.6 us: rms_gain(): values * lax.rsqrt(jnp.mean(values * values, axis=-1, keepdims=True) + no...]
  transfers between devices with their start and end apart: 45 -> 61, of which waited for: 25 -> 19; matrix products, arithmetic and copies ran while one was open for 11% -> 6% of each run, Pallas kernels for 40% -> 53%
where the time goes in v3:
time: 745 us; the launch traced here: 736 us
  Pallas kernels  411 us (55%)
  waiting for transfers between devices  159 us (21%)
  starting transfers between devices  57 us (8%)
  local copies, waits for them, and re-layouts  51.2 us (7%)
  other arithmetic  42.5 us (6%)
  between operations  15.5 us (2%)
    pallas_call x25, Pallas kernels, row_call(): pl.pallas_call(kernel, grid_spec=pltpu.PrefetchScalarGridSpec(num_scalar_...  259 us
    ppermute x24, waiting for transfers between devices, ring_scatter(): send = lambda value, pairs: lax.ppermute(value, 'tensor', pairs)  61.5 us
    pallas_call x2, Pallas kernels, attention_backward(): pl.pallas_call(lambda *refs: attend_back_kernel(HEAD_WIDTH ** (-0.5), *re...  50.2 us
    unnamed x176, local copies, waits for them, and re-layouts  42.7 us
    pallas_call x4, Pallas kernels, row_kernel_call(): pl.pallas_call(lambda *refs: kernel(split, len(lows), *refs), grid=(2 * s...  31.9 us
    pallas_call x4, Pallas kernels, project(): pl.pallas_call(lambda *refs: project_kernel(len(blocks), *refs), grid_spe...  31.6 us
    all_gather x1, waiting for transfers between devices, local(): in_matrix = lax.all_gather(in_low, 'dp', axis=0, tiled=True)  30.3 us
    ppermute x24, starting transfers between devices, ring_scatter(): send = lambda value, pairs: lax.ppermute(value, 'tensor', pairs)  25.3 us
  transfers between devices with their start and end apart: 61, of which 19 were waited for; matrix products, arithmetic and copies ran while one was open for 6% of the time, Pallas kernels for 53%

profile of v3, /device:TPU:0, one launch (start us, length us, event | category | flops | bytes accessed | tf_op | source)
XLA Modules:
  0.0 735.7 jit_solution(14373238888762285917)
XLA Ops:
  29.7 30.3 %all-gather.5.cloned.1.call-done.refs_3_.refs_2_.refs_17_ = bf16[2048,1024]{1,0:T(8,128)(2,1)} async-done(((bf16[256,1024]{1,0:T(8,128)(2,1)}), bf16[2048,1024]{1,0:T(8,128)(2,1)}) %all-gather.5.cloned.1.call-update) | async-done | bytes 4194320 | tf_op jit(solution)/shard_map/all_gather | solution.py:890
  107.3 20.7 %attend.1 = (bf16[2048,512]{1,0:T(8,128)(2,1)}, f32[2,4,2,512]{3,2,1,0:T(2,128)}) custom-call(bf16[2048,512]{1,0:T(8,128)(2,1)} %get-tuple-element.354.refs_0_.refs_1_, bf16[2048,256]{1,0:T(8,128)(2,1)} %get-tuple-element.237.refs_1_.refs_2_, bf16[2048,256]{1,0:T(8,128)(2,1)} %get-tuple-element.238.refs_2_.refs_3_), custom_call_target="tpu_custom_call" | custom-call | flops 1000000 | bytes 1000000 | tf_op jit(solution)/shard_map/attend/pallas_call | solution.py:635
  144.3 21.6 %collective-permute-done.6.refs_2_ = bf16[256,2048]{1,0:T(8,128)(2,1)S(1)} collective-permute-done((bf16[256,2048]{1,0:T(8,128)(2,1)S(1)}, bf16[256,2048]{1,0:T(8,128)(2,1)S(1)}, u32[]{:S(2)}, u32[]{:S(2)}) %collective-permute-start.6) | collective-permute-done | bytes 1048608 | tf_op jit(solution)/shard_map/ppermute | solution.py:163
  167.0 19.3 %collective-permute-done.12.refs_4_ = bf16[256,2048]{1,0:T(8,128)(2,1)S(1)} collective-permute-done((bf16[256,2048]{1,0:T(8,128)(2,1)S(1)}, bf16[256,2048]{1,0:T(8,128)(2,1)S(1)}, u32[]{:S(2)}, u32[]{:S(2)}) %collective-permute-start.12) | collective-permute-done | bytes 1048608 | tf_op jit(solution)/shard_map/ppermute | solution.py:163
  199.2 17.5 %collective-permute-done.14.refs_2_ = bf16[256,2048]{1,0:T(8,128)(2,1)S(1)} collective-permute-done((bf16[256,2048]{1,0:T(8,128)(2,1)}, bf16[256,2048]{1,0:T(8,128)(2,1)S(1)}, u32[]{:S(2)}, u32[]{:S(2)}) %collective-permute-start.14) | collective-permute-done | bytes 1048608 | tf_op jit(solution)/shard_map/ppermute | solution.py:163
  229.8 12.9 %gate_up.3 = (bf16[512,1536]{1,0:T(8,128)(2,1)}, bf16[512,1536]{1,0:T(8,128)(2,1)}, bf16[512,1536]{1,0:T(8,128)(2,1)}) custom-call(s32[12]{0:T(128)} %copy-done.32, bf16[256,2048]{1,0:T(8,128)(2,1)} %get-tuple-element.311.refs_1_, bf16[256,2048]{1,0:T(8,128)(2,1)} %get-tuple-element.268.refs_2_, ...), custom_call_target="tpu_custom_call" | custom-call | flops 1000000 | bytes 1000000 | tf_op jit(solution)/shard_map/gate_up/pallas_call | solution.py:258
  242.7 9.3 %collective-permute-done.17.refs_3_.refs_5_ = bf16[256,2048]{1,0:T(8,128)(2,1)S(1)} collective-permute-done((bf16[256,2048]{1,0:T(8,128)(2,1)}, bf16[256,2048]{1,0:T(8,128)(2,1)S(1)}, u32[]{:S(2)}, u32[]{:S(2)}) %collective-permute-start.17) | collective-permute-done | bytes 1048608 | tf_op jit(solution)/shard_map/ppermute | solution.py:108
  255.3 20.3 %collective-permute-done.16.refs_1_.refs_3_ = bf16[256,2048]{1,0:T(8,128)(2,1)S(1)} collective-permute-done((bf16[256,2048]{1,0:T(8,128)(2,1)}, bf16[256,2048]{1,0:T(8,128)(2,1)S(1)}, u32[]{:S(2)}, u32[]{:S(2)}) %collective-permute-start.16) | collective-permute-done | bytes 1048608 | tf_op jit(solution)/shard_map/ppermute | solution.py:111
  277.6 18.9 %gate_up.4 = (bf16[1024,1536]{1,0:T(8,128)(2,1)}, bf16[1024,1536]{1,0:T(8,128)(2,1)}, bf16[1024,1536]{1,0:T(8,128)(2,1)}) custom-call(s32[12]{0:T(128)} %copy-done.32, bf16[256,2048]{1,0:T(8,128)(2,1)} %copy-done.45, bf16[256,2048]{1,0:T(8,128)(2,1)} %copy-done.44, bf16[256,2048]{1,0:T(8,128)(2,1)} %copy-done.43, bf16[256,2048]{1,0:T(8,128)(2,1)} %copy-done.46, ...), custom_call_target="tpu_custom_call" | custom-call | flops 1000000 | bytes 1000000 | tf_op jit(solution)/shard_map/gate_up/pallas_call | solution.py:258
  300.5 12.9 %gate_up.5 = (bf16[512,1536]{1,0:T(8,128)(2,1)}, bf16[512,1536]{1,0:T(8,128)(2,1)}, bf16[512,1536]{1,0:T(8,128)(2,1)}) custom-call(s32[12]{0:T(128)} %copy-done.32, bf16[256,2048]{1,0:T(8,128)(2,1)} %copy-done.48, bf16[256,2048]{1,0:T(8,128)(2,1)} %copy-done.47, bf16[2048,3072]{1,0:T(8,128)(2,1)} %all-gather.9.cloned.1.call-done.refs_3_.refs_4_.refs_5_.refs_6_.refs_2_, ...), custom_call_target="tpu_custom_call" | custom-call | flops 1000000 | bytes 1000000 | tf_op jit(solution)/shard_map/gate_up/pallas_call | solution.py:258
  313.4 15.6 %gate_up_grad.3.refs_1_.refs_11_.refs_12_.refs_13_.refs_14_ = bf16[1024,3072]{1,0:T(8,128)(2,1)} custom-call(s32[12]{0:T(128)} %copy-done.32, bf16[256,2048]{1,0:T(8,128)(2,1)} %collective-permute-done.8.refs_1_.refs_11_, bf16[256,2048]{1,0:T(8,128)(2,1)} %collective-permute-done.10.refs_2_.refs_12_, ...), custom_call_target="tpu_custom_call" | custom-call | flops 1000000 | bytes 1000000 | tf_op jit(solution)/shard_map/gate_up_grad/pallas_call | solution.py:258
  329.9 20.0 %weight_grad.4 = bf16[1536,2048]{1,0:T(8,128)(2,1)} custom-call(s32[12]{0:T(128)} %copy-done.32, bf16[512,1536]{1,0:T(8,128)(2,1)} %get-tuple-element.330.refs_1_.refs_2_, bf16[512,1536]{1,0:T(8,128)(2,1)} %get-tuple-element.330.refs_1_.refs_2_, bf16[1024,1536]{1,0:T(8,128)(2,1)} %get-tuple-element.325.refs_3_.refs_4_.refs_5_.refs_6_.refs_1_, ...), custom_call_target="tpu_custom_call" | custom-call | flops 1000000 | bytes 1000000 | tf_op jit(solution)/shard_map/weight_grad/pallas_call | solution.py:258
  350.0 19.3 %block_product.18 = (bf16[256,2048]{1,0:T(8,128)(2,1)}, bf16[256,2048]{1,0:T(8,128)(2,1)}, bf16[256,2048]{1,0:T(8,128)(2,1)}, bf16[256,2048]{1,0:T(8,128)(2,1)}) custom-call(s32[12]{0:T(128)} %copy-done.32, bf16[1024,3072]{1,0:T(8,128)(2,1)} %gate_up_grad.3.refs_1_.refs_11_.refs_12_.refs_13_.refs_14_, ...), custom_call_target="tpu_custom_call" | custom-call | flops 1000000 | bytes 1000000 | tf_op jit(solution)/shard_map/block_product/pallas_call | solution.py:258
  371.4 10.8 %gate_up_grad.4.refs_1_.refs_15_.refs_16_ = bf16[512,3072]{1,0:T(8,128)(2,1)} custom-call(s32[12]{0:T(128)} %copy-done.32, bf16[256,2048]{1,0:T(8,128)(2,1)} %copy-done.51, bf16[256,2048]{1,0:T(8,128)(2,1)} %collective-permute-done.23.refs_16_.refs_2_, bf16[1536,2048]{1,0:T(8,128)(2,1)} %all-gather.11.cloned.1.call-done.refs_5_.refs_3_.refs_2_, ...), custom_call_target="tpu_custom_call" | custom-call | flops 1000000 | bytes 1000000 | tf_op jit(solution)/shard_map/gate_up_grad/pallas_call | solution.py:258
  382.2 12.0 %block_product.19 = (bf16[256,2048]{1,0:T(8,128)(2,1)}, bf16[256,2048]{1,0:T(8,128)(2,1)}) custom-call(s32[12]{0:T(128)} %copy-done.32, bf16[512,3072]{1,0:T(8,128)(2,1)} %gate_up_grad.4.refs_1_.refs_15_.refs_16_, bf16[2048,3072]{1,0:T(8,128)(2,1)} %all-gather.9.cloned.1.call-done.refs_3_.refs_4_.refs_5_.refs_6_.refs_2_), custom_call_target="tpu_custom_call" | custom-call | flops 1000000 | bytes 1000000 | tf_op jit(solution)/shard_map/block_product/pallas_call | solution.py:258
  396.5 10.8 %gate_up_grad.5.refs_1_.refs_9_.refs_10_ = bf16[512,3072]{1,0:T(8,128)(2,1)} custom-call(s32[12]{0:T(128)} %copy-done.32, bf16[256,2048]{1,0:T(8,128)(2,1)} %copy-done.41, bf16[256,2048]{1,0:T(8,128)(2,1)} %copy-done.40, bf16[1536,2048]{1,0:T(8,128)(2,1)} %all-gather.11.cloned.1.call-done.refs_5_.refs_3_.refs_2_, ...), custom_call_target="tpu_custom_call" | custom-call | flops 1000000 | bytes 1000000 | tf_op jit(solution)/shard_map/gate_up_grad/pallas_call | solution.py:258
  407.3 12.1 %block_product.20.refs_2_ = bf16[512,2048]{1,0:T(8,128)(2,1)} custom-call(s32[12]{0:T(128)} %copy-done.32, bf16[512,3072]{1,0:T(8,128)(2,1)} %gate_up_grad.5.refs_1_.refs_9_.refs_10_, bf16[2048,3072]{1,0:T(8,128)(2,1)} %all-gather.9.cloned.1.call-done.refs_3_.refs_4_.refs_5_.refs_6_.refs_2_), custom_call_target="tpu_custom_call" | custom-call | flops 1000000 | bytes 1000000 | tf_op jit(solution)/shard_map/block_product/pallas_call | solution.py:258
  427.7 35.2 %weight_grad.5 = bf16[2048,3072]{1,0:T(8,128)(2,1)} custom-call(s32[12]{0:T(128)} %copy-done.32, bf16[256,2048]{1,0:T(8,128)(2,1)} %get-tuple-element.311.refs_1_, bf16[256,2048]{1,0:T(8,128)(2,1)} %get-tuple-element.268.refs_2_, bf16[256,2048]{1,0:T(8,128)(2,1)} %copy-done.45, bf16[256,2048]{1,0:T(8,128)(2,1)} %copy-done.44, bf16[256,2048]{1,0:T(8,128)(2,1)} %copy-done.43, ...), custom_call_target="tpu_custom_call" | custom-call | flops 1000000 | bytes 1000000 | tf_op jit(solution)/shard_map/weight_grad/pallas_call | solution.py:258
  523.8 17.0 %collective-permute-done.32.refs_1_.refs_15_ = bf16[256,2048]{1,0:T(8,128)(2,1)S(1)} collective-permute-done((bf16[256,2048]{1,0:T(8,128)(2,1)S(1)}, bf16[256,2048]{1,0:T(8,128)(2,1)S(1)}, u32[]{:S(2)}, u32[]{:S(2)}) %collective-permute-start.32) | collective-permute-done | bytes 1048608 | tf_op jit(solution)/shard_map/ppermute | solution.py:123
  547.8 10.6 %weight_grad.6 = bf16[512,2048]{1,0:T(8,128)(2,1)} custom-call(s32[12]{0:T(128)} %copy-done.32, bf16[2048,512]{1,0:T(8,128)(2,1)} %get-tuple-element.344.refs_1_.refs_2_.refs_3_.refs_4_.refs_5_.refs_6_.refs_7_.refs_8_, bf16[2048,512]{1,0:T(8,128)(2,1)} %get-tuple-element.344.refs_1_.refs_2_.refs_3_.refs_4_.refs_5_.refs_6_.refs_7_.refs_8_, ...), custom_call_target="tpu_custom_call" | custom-call | flops 1000000 | bytes 1000000 | tf_op jit(solution)/shard_map/weight_grad/pallas_call | solution.py:258
  558.4 25.1 %attend_back.2 = (bf16[2048,1024]{1,0:T(8,128)(2,1)}, f32[2,128]{1,0:T(2,128)}) custom-call(s32[4]{0:T(128)} %compare_select_fusion.5.refs_0_, bf16[2048,512]{1,0:T(8,128)(2,1)} %get-tuple-element.354.refs_0_.refs_1_, bf16[2048,256]{1,0:T(8,128)(2,1)} %get-tuple-element.237.refs_1_.refs_2_, bf16[2048,256]{1,0:T(8,128)(2,1)} %get-tuple-element.238.refs_2_.refs_3_, ...), custom_call_target="tpu_custom_call" | custom-call | flops 1000000 | bytes 1000000 | tf_op jit(solution)/shard_map/attend_back/pallas_call | solution.py:778
  591.1 25.1 %attend_back.3 = (bf16[2048,1024]{1,0:T(8,128)(2,1)}, f32[2,128]{1,0:T(2,128)}) custom-call(s32[4]{0:T(128)} %compare_select_fusion.5.refs_0_, bf16[2048,512]{1,0:T(8,128)(2,1)} %get-tuple-element.354.refs_0_.refs_1_, bf16[2048,256]{1,0:T(8,128)(2,1)} %get-tuple-element.237.refs_1_.refs_2_, ...), custom_call_target="tpu_custom_call", output_to_operand_aliasing={{0}: (12, {})} | custom-call | flops 1000000 | bytes 1000000 | tf_op jit(solution)/shard_map/attend_back/pallas_call | solution.py:778
  635.0 16.8 %weight_grad.7 = (bf16[2048,1024]{1,0:T(8,128)(2,1)}, f32[1,2048]{1,0:T(1,128)}) custom-call(s32[12]{0:T(128)} %copy-done.32, bf16[256,2048]{1,0:T(8,128)(2,1)} %copy-done.39, bf16[256,2048]{1,0:T(8,128)(2,1)} %copy-done.38, bf16[256,2048]{1,0:T(8,128)(2,1)} %collective-permute-done.4.refs_1_.refs_3_, bf16[256,2048]{1,0:T(8,128)(2,1)} %copy-done.49, ...), custom_call_target="tpu_custom_call" | custom-call | flops 1000000 | bytes 1000000 | tf_op jit(solution)/shard_map/weight_grad/pallas_call | solution.py:258
  685.8 12.5 %fusion.3 = (f32[256,2,1536]{2,1,0:T(2,128)}, f32[256,2,1536]{2,1,0:T(2,128)}) fusion(f32[256,2,1536]{2,1,0:T(2,128)} %reshape.87, f32[256,2,1536]{2,1,0:T(2,128)} %param.29, f32[256,2,1536]{2,1,0:T(2,128)} %param.27, f32[256,2,1536]{2,1,0:T(2,128)} %param.28), kind=kLoop, calls=%fused_computation.6 | loop fusion | flops 10223616 | bytes 18874368 | tf_op jit(solution)/shard_map/add | solution.py:61
  (357 shorter events, 293.7 us)
Async XLA Ops:
  7.2 52.8 %all-gather.5.cloned.1.call-start = ((), (), s32[]{:S(2)}) async-start(), calls=%async_computation.4 | async-start | bytes 4718592 | tf_op jit(solution)/shard_map/all_gather | solution.py:890
  9.9 118.1 %all-gather.7.cloned.1.call-start = ((), (), s32[]{:S(2)}) async-start(), calls=%async_computation.5 | async-start | bytes 2359296 | tf_op jit(solution)/shard_map/all_gather | solution.py:891
  11.7 205.7 %all-gather.9.cloned.1.call-start = ((), (), s32[]{:S(2)}) async-start(), calls=%async_computation.6 | async-start | bytes 14155776 | tf_op jit(solution)/shard_map/all_gather | solution.py:892
  14.3 299.1 %all-gather.11.cloned.1.call-start = ((), (), s32[]{:S(2)}) async-start(), calls=%async_computation.7 | async-start | bytes 7077888 | tf_op jit(solution)/shard_map/all_gather | solution.py:893
  16.9 492.5 %reduce-scatter.5.cloned.1.call-start = ((), (), s32[]{:S(2)}) async-start(), calls=%async_computation.8 | async-start | bytes 7077888 | tf_op jit(solution)/shard_map/reduce_scatter | solution.py:965
  18.9 48.8 %collective-permute-start.1 = (bf16[256,2048]{1,0:T(8,128)(2,1)S(1)}, bf16[256,2048]{1,0:T(8,128)(2,1)S(1)}, u32[]{:S(2)}, u32[]{:S(2)}) collective-permute-start(bf16[256,2048]{1,0:T(8,128)(2,1)S(1)} %get-tuple-element.415.refs_2_), channel_id=1, source_target_pairs={{1,0},{3,1},{2,3},{0,2},{5,4},{7,5},{6,7},{4,6},{9,8},{11,9},{10,1... | collective-permute-start | bytes 3145736 | tf_op jit(solution)/shard_map/ppermute | solution.py:109
  21.9 45.8 %collective-permute-start = (bf16[256,2048]{1,0:T(8,128)(2,1)S(1)}, bf16[256,2048]{1,0:T(8,128)(2,1)}, u32[]{:S(2)}, u32[]{:S(2)}) collective-permute-start(bf16[256,2048]{1,0:T(8,128)(2,1)S(1)} %get-tuple-element.365.refs_1_), channel_id=1, source_target_pairs={{0,1},{1,3},{3,2},{2,0},{4,5},{5,7},{7,6},{6,4},{8,9},{9,11},{11,1... | collective-permute-start | bytes 3145736 | tf_op jit(solution)/shard_map/ppermute | solution.py:108
  22.0 48.0 %collective-permute-start.5 = (bf16[256,2048]{1,0:T(8,128)(2,1)S(1)}, bf16[256,2048]{1,0:T(8,128)(2,1)}, u32[]{:S(2)}, u32[]{:S(2)}) collective-permute-start(bf16[256,2048]{1,0:T(8,128)(2,1)S(1)} %get-tuple-element.415.refs_2_), channel_id=1, source_target_pairs={{0,1},{1,3},{3,2},{2,0},{4,5},{5,7},{7,6},{6,4},{8,9},{9,11},{11,1... | collective-permute-start | bytes 3145736 | tf_op jit(solution)/shard_map/ppermute | solution.py:110
  23.9 46.0 %collective-permute-start.4 = (bf16[256,2048]{1,0:T(8,128)(2,1)S(1)}, bf16[256,2048]{1,0:T(8,128)(2,1)}, u32[]{:S(2)}, u32[]{:S(2)}) collective-permute-start(bf16[256,2048]{1,0:T(8,128)(2,1)S(1)} %get-tuple-element.365.refs_1_), channel_id=1, source_target_pairs={{1,0},{3,1},{2,3},{0,2},{5,4},{7,5},{6,7},{4,6},{9,8},{11,9},{10,1... | collective-permute-start | bytes 3145736 | tf_op jit(solution)/shard_map/ppermute | solution.py:111
  94.8 46.2 %collective-permute-start.11 = (bf16[256,2048]{1,0:T(8,128)(2,1)S(1)}, bf16[256,2048]{1,0:T(8,128)(2,1)S(1)}, u32[]{:S(2)}, u32[]{:S(2)}) collective-permute-start(bf16[256,2048]{1,0:T(8,128)(2,1)S(1)} %get-tuple-element.413.refs_10_.refs_2_), channel_id=1, source_target_pairs={{0,1},{1,3},{3,2},{2,0},{4,5},{5,7},{7,6},{6,4},{8,9},{9,11},{11,1... | collective-permute-start | bytes 3145736 | tf_op jit(solution)/shard_map/ppermute | solution.py:110
  96.2 45.5 %collective-permute-start.10 = (bf16[256,2048]{1,0:T(8,128)(2,1)S(1)}, bf16[256,2048]{1,0:T(8,128)(2,1)}, u32[]{:S(2)}, u32[]{:S(2)}) collective-permute-start(bf16[256,2048]{1,0:T(8,128)(2,1)S(1)} %get-tuple-element.413.refs_10_.refs_2_), channel_id=1, source_target_pairs={{1,0},{3,1},{2,3},{0,2},{5,4},{7,5},{6,7},{4,6},{9,8},{11,9},{10,1... | collective-permute-start | bytes 3145736 | tf_op jit(solution)/shard_map/ppermute | solution.py:109
  96.8 46.6 %collective-permute-start.9 = (bf16[256,2048]{1,0:T(8,128)(2,1)S(1)}, bf16[256,2048]{1,0:T(8,128)(2,1)}, u32[]{:S(2)}, u32[]{:S(2)}) collective-permute-start(bf16[256,2048]{1,0:T(8,128)(2,1)S(1)} %get-tuple-element.305.refs_9_.refs_1_), channel_id=1, source_target_pairs={{0,1},{1,3},{3,2},{2,0},{4,5},{5,7},{7,6},{6,4},{8,9},{9,11},{11,1... | collective-permute-start | bytes 3145736 | tf_op jit(solution)/shard_map/ppermute | solution.py:108
  98.3 46.0 %collective-permute-start.8 = (bf16[256,2048]{1,0:T(8,128)(2,1)S(1)}, bf16[256,2048]{1,0:T(8,128)(2,1)}, u32[]{:S(2)}, u32[]{:S(2)}) collective-permute-start(bf16[256,2048]{1,0:T(8,128)(2,1)S(1)} %get-tuple-element.305.refs_9_.refs_1_), channel_id=1, source_target_pairs={{1,0},{3,1},{2,3},{0,2},{5,4},{7,5},{6,7},{4,6},{9,8},{11,9},{10,1... | collective-permute-start | bytes 3145736 | tf_op jit(solution)/shard_map/ppermute | solution.py:111
  141.6 44.7 %collective-permute-start.12 = (bf16[256,2048]{1,0:T(8,128)(2,1)S(1)}, bf16[256,2048]{1,0:T(8,128)(2,1)S(1)}, u32[]{:S(2)}, u32[]{:S(2)}) collective-permute-start(bf16[256,2048]{1,0:T(8,128)(2,1)S(1)} %get-tuple-element.254), channel_id=1, source_target_pairs={{0,1},{1,3},{3,2},{2,0},{4,5},{5,7},{7,6},{6,4},{8,9},{9,11},{11,1... | collective-permute-start | bytes 3145736 | tf_op jit(solution)/shard_map/ppermute | solution.py:163
  227.7 47.8 %collective-permute-start.16 = (bf16[256,2048]{1,0:T(8,128)(2,1)}, bf16[256,2048]{1,0:T(8,128)(2,1)S(1)}, u32[]{:S(2)}, u32[]{:S(2)}) collective-permute-start(bf16[256,2048]{1,0:T(8,128)(2,1)} %get-tuple-element.311.refs_1_), channel_id=1, source_target_pairs={{1,0},{3,1},{2,3},{0,2},{5,4},{7,5},{6,7},{4,6},{9,8},{11,9},{10,1... | collective-permute-start | bytes 3145736 | tf_op jit(solution)/shard_map/ppermute | solution.py:111
  228.8 46.8 %collective-permute-start.19 = (bf16[256,2048]{1,0:T(8,128)(2,1)}, bf16[256,2048]{1,0:T(8,128)(2,1)S(1)}, u32[]{:S(2)}, u32[]{:S(2)}) collective-permute-start(bf16[256,2048]{1,0:T(8,128)(2,1)} %get-tuple-element.268.refs_2_), channel_id=1, source_target_pairs={{0,1},{1,3},{3,2},{2,0},{4,5},{5,7},{7,6},{6,4},{8,9},{9,11},{11,1... | collective-permute-start | bytes 3145736 | tf_op jit(solution)/shard_map/ppermute | solution.py:110
  253.1 45.4 %collective-permute-start.21 = (bf16[256,2048]{1,0:T(8,128)(2,1)S(1)}, bf16[256,2048]{1,0:T(8,128)(2,1)S(1)}, u32[]{:S(2)}, u32[]{:S(2)}) collective-permute-start(bf16[256,2048]{1,0:T(8,128)(2,1)S(1)} %collective-permute-done.18.refs_2_.refs_4_), channel_id=1, source_target_pairs={{1,0},{3,1},{2,3},{0,2},{5,4},{7,5},{6,7},{4,6},{9,8},{11,9},{10,1... | collective-permute-start | bytes 3145736 | tf_op jit(solution)/shard_map/ppermute | solution.py:124
  350.0 301.9 %reduce-scatter.9.cloned.1.call-start = ((), (), s32[]{:S(2)}) async-start(), calls=%async_computation.10 | async-start | bytes 14155776 | tf_op jit(solution)/shard_map/reduce_scatter | solution.py:987
  369.4 50.1 %collective-permute-start.26 = (bf16[256,2048]{1,0:T(8,128)(2,1)}, bf16[256,2048]{1,0:T(8,128)(2,1)S(1)}, u32[]{:S(2)}, u32[]{:S(2)}) collective-permute-start(bf16[256,2048]{1,0:T(8,128)(2,1)} %get-tuple-element.298), channel_id=1, source_target_pairs={{0,1},{1,3},{3,2},{2,0},{4,5},{5,7},{7,6},{6,4},{8,9},{9,11},{11,1... | collective-permute-start | bytes 3145736 | tf_op jit(solution)/shard_map/ppermute | solution.py:163
  370.1 49.4 %collective-permute-start.27 = (bf16[256,2048]{1,0:T(8,128)(2,1)}, bf16[256,2048]{1,0:T(8,128)(2,1)S(1)}, u32[]{:S(2)}, u32[]{:S(2)}) collective-permute-start(bf16[256,2048]{1,0:T(8,128)(2,1)} %get-tuple-element.299), channel_id=1, source_target_pairs={{1,0},{3,1},{2,3},{0,2},{5,4},{7,5},{6,7},{4,6},{9,8},{11,9},{10,1... | collective-permute-start | bytes 3145736 | tf_op jit(solution)/shard_map/ppermute | solution.py:163
  464.3 216.1 %reduce-scatter.7.cloned.1.call-start = ((), (), s32[]{:S(2)}) async-start(), calls=%async_computation.9 | async-start | bytes 2359296 | tf_op jit(solution)/shard_map/reduce_scatter | solution.py:1085
  516.7 66.8 %collective-permute-start.38 = (bf16[256,2048]{1,0:T(8,128)(2,1)}, bf16[256,2048]{1,0:T(8,128)(2,1)}, u32[]{:S(2)}, u32[]{:S(2)}) collective-permute-start(bf16[256,2048]{1,0:T(8,128)(2,1)} %get-tuple-element.328), channel_id=1, source_target_pairs={{0,1},{1,3},{3,2},{2,0},{4,5},{5,7},{7,6},{6,4},{8,9},{9,11},{11,1... | collective-permute-start | bytes 3145736 | tf_op jit(solution)/shard_map/ppermute | solution.py:163
  517.8 65.7 %collective-permute-start.39 = (bf16[256,2048]{1,0:T(8,128)(2,1)}, bf16[256,2048]{1,0:T(8,128)(2,1)}, u32[]{:S(2)}, u32[]{:S(2)}) collective-permute-start(bf16[256,2048]{1,0:T(8,128)(2,1)} %get-tuple-element.329), channel_id=1, source_target_pairs={{1,0},{3,1},{2,3},{0,2},{5,4},{7,5},{6,7},{4,6},{9,8},{11,9},{10,1... | collective-permute-start | bytes 3145736 | tf_op jit(solution)/shard_map/ppermute | solution.py:163
  616.3 98.7 %reduce-scatter.11.cloned.1.call-start = ((), (), s32[]{:S(2)}) async-start(), calls=%async_computation.11 | async-start | bytes 4718592 | tf_op jit(solution)/shard_map/reduce_scatter | solution.py:1087
  (124 other events, 1764.8 us)
Sparse Core Ops, SparseCore 0:
  10.2 49.7 all-gather.4
  62.2 29.5 all-gather.6
  94.1 115.7 all-gather.8
  211.3 63.3 all-gather.10
  350.1 67.9 reduce-scatter.4
  464.4 127.4 reduce-scatter.8
  616.4 34.6 reduce-scatter.6
  653.4 48.6 reduce-scatter.10

commit v4 on v3

--- a/solution.py
+++ b/solution.py
@@ -65,6 +65,41 @@
         mean_hat / (jnp.sqrt(square_hat) + adam_eps) + decay_rate * weight
     )
     return (weight_new, square_new)
+
+
+def adam_kernel(rate, weight_ref, mean_ref, square_ref, *refs):
+    *grad_refs, grad_out, new_out, second_out = refs
+    width = weight_ref.shape[2]
+    for part in range(weight_ref.shape[1]):
+        start = part * width
+        for grad_ref in grad_refs:
+            if start < grad_ref.shape[1]:
+                break
+            start -= grad_ref.shape[1]
+        grad = grad_ref[:, start : start + width].astype(jnp.float32)
+        new, second = adamw(
+            weight_ref[:, part, :], grad, mean_ref[:, part, :], square_ref[:, part, :], rate
+        )
+        grad_out[:, part, :] = grad
+        new_out[:, part, :] = new
+        second_out[:, part, :] = second
+
+
+def adamw_parts(weight, grads, mean_old, square_old, rate):
+    rows, parts, width = weight.shape
+    tile = min(rows, 64)
+    spec = pl.BlockSpec((tile, parts, width), lambda i: (i, 0, 0))
+    return pl.pallas_call(
+        lambda *refs: adam_kernel(rate, *refs),
+        grid=(rows // tile,),
+        in_specs=[spec] * 3
+        + [pl.BlockSpec((tile, grad.shape[1]), lambda i: (i, 0)) for grad in grads],
+        out_specs=[spec] * 3,
+        out_shape=[jax.ShapeDtypeStruct(weight.shape, jnp.float32)] * 3,
+        compiler_params=kernel_params(),
+        cost_estimate=SMALL_COST,
+        name="adamw",
+    )(weight, mean_old, square_old, *grads)
 
 
 def ring_place(index, size):
@@ -141,11 +176,12 @@
 
 def relay(terms, got):
     rows, width = terms[0].shape
-    spec = pl.BlockSpec((rows, tile_of(width, 512)), lambda i: (0, i))
+    tile = min(rows, 64)
+    spec = pl.BlockSpec((tile, width), lambda i: (i, 0))
     count = len(terms)
     return pl.pallas_call(
         lambda *refs: relay_kernel(count, *refs),
-        grid=(width // tile_of(width, 512),),
+        grid=(rows // tile,),
         in_specs=[spec] * (2 * count),
         out_specs=[spec] * count,
         out_shape=[jax.ShapeDtypeStruct((rows, width), jnp.bfloat16)] * count,
@@ -206,11 +242,14 @@
         return lax.psum(values, axis)
     reach, beside = 1, list(beside)
     while reach < size:
-        pairs = [(i, i ^ reach) for i in range(size)]
-        values = values + lax.ppermute(values, axis, pairs)
+        ways = 4 if size >= 4 * reach else 2
+        values = values + sum(
+            lax.ppermute(values, axis, [(i, i ^ (way * reach)) for i in range(size)])
+            for way in range(1, ways)
+        )
         if beside:
             values = lax.optimization_barrier((values, beside.pop(0)))[0]
-        reach *= 2
+        reach *= ways
     return values
 
 
@@ -226,9 +265,10 @@
 
 
 class Piece:
-    def __init__(self, array, count=None, index=0, entry=None):
+    def __init__(self, array, count=None, index=0, entry=None, side=0, sides=1):
         self.array, self.count = array, count or array.shape[0]
         self.index, self.entry = index, entry
+        self.side, self.columns = side, array.shape[1] // sides
 
     def row(self, table):
         return self.index if self.entry is None else table[self.entry]
@@ -236,8 +276,8 @@
     def spec(self, width=None):
         if width is None:
             return pl.BlockSpec(
-                (self.count, self.array.shape[1]),
-                lambda i, table: (self.row(table), 0),
+                (self.count, self.columns),
+                lambda i, table: (self.row(table), self.side),
                 pipeline_mode=pl.Buffered(1),
             )
         return pl.BlockSpec((self.count, width), lambda i, table: (self.row(table), i))
@@ -393,7 +433,7 @@
 
 
 def weight_gradient(table, lefts, rights, weights=None):
-    width, columns = lefts[0].array.shape[1], rights[0].array.shape[1]
+    width, columns = lefts[0].array.shape[1], rights[0].columns
     tile = tile_of(width, 256)
     weighed = weights is not None
     block_spec = pl.BlockSpec((tile, columns), lambda i, table: (i, 0))
@@ -413,9 +453,11 @@
     return result if weighed else result[0]
 
 
-def split_groups(groups, half):
+def split_groups(groups, half, side=0, sides=1):
     return [
-        Piece(array, half, i) for array in groups for i in range(array.shape[0] // half)
+        Piece(array, half, i, side=side, sides=sides)
+        for array in groups
+        for i in range(array.shape[0] // half)
     ]
 
 
@@ -508,7 +550,8 @@
     if len(outs) == 1:
         outs[0][...] = result.astype(jnp.bfloat16)
         return
-    low_ref, high_ref, gain_out = outs
+    low_ref, high_ref, whole_ref, gain_out = outs
+    whole_ref[...] = result.astype(jnp.bfloat16)
     put_half(split, low_ref, high_ref, result.astype(jnp.bfloat16))
 
     @pl.when(pl.program_id(0) == 0)
@@ -586,38 +629,57 @@
     )(place.reshape(1), *blocks, matrix, gains, cos, sin, *kept)
 
 
+def causal(keys, queries):
+    rows = lax.broadcasted_iota(jnp.int32, (keys, queries), 0)
+    return rows <= lax.broadcasted_iota(jnp.int32, (keys, queries), 1)
+
+
+def add_after(whole, part, low):
+    if low == 0:
+        return whole + part
+    return jnp.concatenate([whole[:, :low], whole[:, low:] + part], axis=1)
+
+
+def walk(visit, step, block, carry, pieces):
+    carry = lax.fori_loop(
+        0,
+        step,
+        lambda j, c: visit(pl.multiple_of(j * block, block), c, block, 0, False),
+        carry,
+    )
+    start = pl.multiple_of(step * block, block)
+    count = block // pieces
+    for low in range(0, block, count):
+        carry = visit(start + low, carry, count, low, True)
+    return carry
+
+
 def attend_kernel(scale, query_ref, key_ref, value_ref, out_ref, log_ref):
     block = query_ref.shape[0]
     width = key_ref.shape[1]
     group = query_ref.shape[1] // width
     step = pl.program_id(2)
-    below = lax.broadcasted_iota(jnp.int32, (block, block), 0) <= lax.broadcasted_iota(
-        jnp.int32, (block, block), 1
-    )
     queries = [query_ref[:, g * width : (g + 1) * width] for g in range(group)]
 
-    def visit(start, carry, masked):
-        keys = key_ref[pl.ds(start, block), :]
-        values = value_ref[pl.ds(start, block), :]
+    def visit(start, carry, count, low, masked):
+        keys = key_ref[pl.ds(start, count), :]
+        values = value_ref[pl.ds(start, count), :]
         new = []
         for g in range(group):
             total, acc = carry[g]
-            weights = jnp.exp2(contract_cols(keys, queries[g]) * (scale * log2_e))
+            weights = jnp.exp2(contract_cols(keys, queries[g][low:]) * (scale * log2_e))
             if masked:
-                weights = jnp.where(below, weights, 0.0)
-            total = total + jnp.sum(weights, axis=0, keepdims=True)
-            acc = acc + contract_rows(values, weights.astype(jnp.bfloat16))
+                weights = jnp.where(causal(count, block - low), weights, 0.0)
+            total = add_after(total, jnp.sum(weights, axis=0, keepdims=True), low)
+            acc = add_after(acc, contract_rows(values, weights.astype(jnp.bfloat16)), low)
             new.append((total, acc))
         return tuple(new)
 
-    start_carry = tuple(
+    carry = tuple(
         (jnp.zeros((1, block), jnp.float32), jnp.zeros((width, block), jnp.float32))
         for _ in range(group)
     )
-    carry = lax.fori_loop(
-        0, step, lambda j, c: visit(pl.multiple_of(j * block, block), c, False), start_carry
-    )
-    carry = visit(pl.multiple_of(step * block, block), carry, True)
+    carry = walk(visit, step, block, carry, 1)
     for g in range(group):
         total, acc = carry[g]
         out_ref[:, g * width : (g + 1) * width] = jnp.transpose(acc / total).astype(jnp.bfloat16)
@@ -683,10 +745,6 @@
     width = key_ref.shape[1]
     group = query_ref.shape[1] // width
     sequence, step = pl.program_id(0), pl.program_id(1)
-    below = lax.broadcasted_iota(jnp.int32, (block, block), 0) <= lax.broadcasted_iota(
-        jnp.int32, (block, block), 1
-    )
-
     @pl.when(step == 0)
     def _():
         key_sum[...] = jnp.zeros_like(key_sum)
@@ -705,32 +763,30 @@
         both = grads[g].astype(jnp.float32) * context_ref[:, cols].astype(jnp.float32)
         dots.append(jnp.sum(jnp.transpose(both), axis=0, keepdims=True))
 
-    def visit(start, carry, masked):
-        rows = pl.ds(start, block)
+    def visit(start, carry, count, low, masked):
+        rows = pl.ds(start, count)
         keys = key_ref[rows, :]
         values = value_ref[rows, :]
         new = []
         key_part = value_part = None
         for g in range(group):
-            weights = jnp.exp2(contract_cols(keys, queries[g]) * (scale * log2_e) - logs[g])
+            seen, sought = queries[g][low:], grads[g][low:]
+            weights = jnp.exp2(contract_cols(keys, seen) * (scale * log2_e) - logs[g][:, low:])
             if masked:
-                weights = jnp.where(below, weights, 0.0)
-            slope = contract_cols(values, grads[g])
-            score = (weights * (slope - dots[g])).astype(jnp.bfloat16)
-            value_g = product(weights.astype(jnp.bfloat16), grads[g])
-            key_g = product(score, queries[g])
+                weights = jnp.where(causal(count, block - low), weights, 0.0)
+            slope = contract_cols(values, sought)
+            score = (weights * (slope - dots[g][:, low:])).astype(jnp.bfloat16)
+            value_g = product(weights.astype(jnp.bfloat16), sought)
+            key_g = product(score, seen)
             key_part = key_g if key_part is None else key_part + key_g
             value_part = value_g if value_part is None else value_part + value_g
-            new.append(carry[g] + contract_rows(keys, score))
+            new.append(add_after(carry[g], contract_rows(keys, score), low))
         key_sum[rows, :] += key_part
         value_sum[rows, :] += value_part
         return tuple(new)
 
     carry = tuple(jnp.zeros((width, block), jnp.float32) for _ in range(group))
-    carry = lax.fori_loop(
-        0, step, lambda j, c: visit(pl.multiple_of(j * block, block), c, False), carry
-    )
-    carry = visit(pl.multiple_of(step * block, block), carry, True)
+    carry = walk(visit, step, block, carry, 2)
     rows = pl.ds(pl.multiple_of(step * block, block), block)
     cos, sin = cos_ref[rows, :], sin_ref[rows, :]
     for g in range(group):
@@ -976,7 +1032,8 @@
     def swiglu_gradient():
         twos = flat(two_groups)
         twos[0].array = turn(twos[0].array)
-        more.append(mark(weight_gradient(table, twos, split_groups(grads, half))))
+        side = len(more)
+        more.append(mark(weight_gradient(table, twos, split_groups(grads, half, side, 2))))
 
     if last == 1:
         own_part()
@@ -984,10 +1041,10 @@
         size, lambda group: two_parts[group], order, between=own_part, after=swiglu_gradient
     )
     swiglu_part, lows, highs = tie((more[0], lows, highs))
-    swiglu_grad = lax.psum_scatter(swiglu_part, "dp", scatter_dimension=0, tiled=True)
-    *attended_halves, mlp_gain_grad = mark(
+    gate_weight_grad = lax.psum_scatter(swiglu_part, "dp", scatter_dimension=0, tiled=True)
+    *attended_halves, hidden_grad, mlp_gain_grad = mark(
         *norm_gradient(
-            cotangent, hidden, own, lows, highs, norm_gains[1:2], ("halves", "row")
+            cotangent, hidden, own, lows, highs, norm_gains[1:2], ("halves", jnp.bfloat16, "row")
         )
     )
 
@@ -1018,8 +1075,12 @@
                     FF ** (-0.5),
                 ),
             )
+        if group == last - 1:
+            swiglu_gradient()
 
     attended_groups = ring_gather(attended_halves, size, context_group, order)
+    swiglu_part = tie((more[1], *attended_groups[last]))[0]
+    up_weight_grad = lax.psum_scatter(swiglu_part, "dp", scatter_dimension=0, tiled=True)
 
     def head_backward(head):
         head_grads.append(
@@ -1050,10 +1111,7 @@
         between=lambda: head_backward(0),
         after=other_heads,
     )
-    (outputs,) = row_kernel_call(
-        add_kernel, "add", [hidden, own], lows, highs, norm_gains[0:1], (jnp.bfloat16,)
-    )
-    sent = lows + highs
+    sent, outputs = (own, lows, highs), []
     mixed_grad = head_grads[-1][0]
     qknorm_part = sum(pair[1] for pair in head_grads)
     in_parts = []
@@ -1071,29 +1129,44 @@
         in_parts[:] = mark(
             *weight_gradient(table, normeds, ordered_finely(mixed_grad), in_matrix)
         )
-
-    got, came = [], []
-    own, lows, highs = ring_scatter(
-        size, normed_group, order, between=in_gradient, got=got, came=came, eager=False
-    )
+        own, lows, highs = sent
+        outputs[:] = mark(
+            *row_kernel_call(
+                add_kernel,
+                "add",
+                [hidden, turn(own)],
+                lows,
+                highs,
+                norm_gains[0:1],
+                (jnp.bfloat16,),
+            ),
+            in_parts[0],
+        )[:1]
+
+    got = []
+    own, lows, highs = ring_scatter(size, normed_group, order, between=in_gradient, got=got)
     if not in_parts:
         in_gradient()
     rows_of_gains = jnp.concatenate([in_parts[1] / norm_gains[0:1], mlp_gain_grad], axis=0)
-    gain_sums = tie((jnp.concatenate([rows_of_gains, qknorm_part], axis=1), *got))[0]
+    gain_sums = jnp.concatenate([rows_of_gains, qknorm_part], axis=1)
+    (outputs,) = outputs
+    gain_sums = tie((gain_sums, own, *got))[0]
     gain_sums = sum_over(gain_sums, "tensor")
-    out_part, down_grad = tie((out_part, down_grad, *sent, mixed_grad))[:2]
+    out_part, gate_weight_grad = tie((out_part, gate_weight_grad, sent, mixed_grad))[:2]
     out_grad = lax.psum_scatter(out_part, "dp", scatter_dimension=1, tiled=True)
-    in_part, swiglu_grad = tie((in_parts[0], swiglu_grad, *came))[:2]
+    in_part, up_weight_grad = tie((in_parts[0], up_weight_grad, *got))[:2]
     in_grad = lax.psum_scatter(in_part, "dp", scatter_dimension=0, tiled=True)
-    in_grad = in_grad.astype(jnp.float32).reshape(input_projection_weight.shape)
-    out_grad, swiglu_grad, outputs = tie((out_grad, swiglu_grad, outputs, *got))[:3]
+    out_grad, gate_weight_grad = tie((out_grad, gate_weight_grad, *got))[:2]
     out_grad = out_grad.astype(jnp.float32)
-    swiglu_grad = swiglu_grad.astype(jnp.float32).reshape(swiglu_weight.shape)
     out_new, out_second = adamw(
         out_weight, out_grad, out_mean, out_square, (HQ * HEAD_WIDTH / 8.0) ** (-0.5)
     )
-    swiglu_new, swiglu_second = adamw(
-        swiglu_weight, swiglu_grad, swiglu_mean, swiglu_square, MODEL_WIDTH ** (-0.5)
+    swiglu_grad, swiglu_new, swiglu_second = adamw_parts(
+        swiglu_weight,
+        (gate_weight_grad, up_weight_grad),
+        swiglu_mean,
+        swiglu_square,
+        MODEL_WIDTH ** (-0.5),
     )
     down_grad, down_new, down_second = new_down
     (
@@ -1121,13 +1194,12 @@
             swiglu_second,
         )
     )
-    hidden_grad = jnp.concatenate(attended_halves, axis=0)
     (input_grad,) = norm_gradient(
         hidden_grad, inputs, own, lows, highs, norm_gains[0:1], (jnp.bfloat16,)
     )
-    in_new, in_second = adamw(
+    in_grad, in_new, in_second = adamw_parts(
         input_projection_weight,
-        in_grad,
+        (in_grad,),
         input_first_moment,
         input_second_moment,
         MODEL_WIDTH ** (-0.5),

time: 745 us -> 735 us (0.987)
  Pallas kernels: 411 us -> 429 us
  other arithmetic: 42.5 us -> 25.3 us
  waiting for transfers between devices: 159 us -> 142 us
    ppermute x4, waiting for transfers between devices: 24.7 us -> 7.68 us  [ring_far(): low = lax.ppermute(carried[0], 'tensor', ahead)]
    pallas_call x4 -> x6, Pallas kernels: 17.5 us -> 32.5 us  [the longest x4 17.2 us: relay(): pl.pallas_call(lambda *refs: relay_kernel(count, *refs), grid=(rows // ti...]
    unnamed x176 -> x180, local copies, waits for them, and re-layouts: 42.7 us -> 54.1 us
    add x2 -> x1, other arithmetic: 13.8 us -> 2.46 us  [adamw(): square_new = beta_two * square_old + (1.0 - beta_two) * gradient * gradient]
    pallas_call x25 -> x26, Pallas kernels: 259 us -> 263 us  [row_call(): pl.pallas_call(kernel, grid_spec=pltpu.PrefetchScalarGridSpec(num_scalar_...]
  transfers between devices with their start and end apart: 61 -> 64, of which waited for: 19 -> 20; matrix products, arithmetic and copies ran while one was open for 6% -> 3% of each run, Pallas kernels for 53% -> 56%
where the time goes in v4:
time: 735 us; the launch traced here: 726 us
  Pallas kernels  429 us (58%)
  waiting for transfers between devices  142 us (19%)
  starting transfers between devices  59.1 us (8%)
  local copies, waits for them, and re-layouts  55.2 us (8%)
  other arithmetic  25.3 us (3%)
  between operations  15.3 us (2%)
    pallas_call x26, Pallas kernels, row_call(): pl.pallas_call(kernel, grid_spec=pltpu.PrefetchScalarGridSpec(num_scalar_...  263 us
    ppermute x24, waiting for transfers between devices, ring_scatter(): send = lambda value, pairs: lax.ppermute(value, 'tensor', pairs)  64.4 us
    unnamed x180, local copies, waits for them, and re-layouts  54.1 us
    pallas_call x2, Pallas kernels, attention_backward(): pl.pallas_call(lambda *refs: attend_back_kernel(HEAD_WIDTH ** (-0.5), *re...  49.3 us
    pallas_call x4, Pallas kernels, project(): pl.pallas_call(lambda *refs: project_kernel(len(blocks), *refs), grid_spe...  31.7 us
    pallas_call x4, Pallas kernels, row_kernel_call(): pl.pallas_call(lambda *refs: kernel(split, len(lows), *refs), grid=(2 * s...  31.6 us
    all_gather x1, waiting for transfers between devices, local(): in_matrix = lax.all_gather(in_low, 'dp', axis=0, tiled=True)  30.4 us
    ppermute x24, starting transfers between devices, ring_scatter(): send = lambda value, pairs: lax.ppermute(value, 'tensor', pairs)  25.2 us
  transfers between devices with their start and end apart: 64, of which 20 were waited for; matrix products, arithmetic and copies ran while one was open for 3% of the time, Pallas kernels for 56%

profile of v4, /device:TPU:0, one launch (start us, length us, event | category | flops | bytes accessed | tf_op | source)
XLA Modules:
  0.0 726.0 jit_solution(13994206707242419459)
XLA Ops:
  29.7 30.4 %all-gather.5.cloned.1.call-done.refs_3_.refs_2_.refs_17_ = bf16[2048,1024]{1,0:T(8,128)(2,1)} async-done(((bf16[256,1024]{1,0:T(8,128)(2,1)}), bf16[2048,1024]{1,0:T(8,128)(2,1)}) %all-gather.5.cloned.1.call-update) | async-done | bytes 4194320 | tf_op jit(solution)/shard_map/all_gather | solution.py:946
  107.4 20.5 %attend.1 = (bf16[2048,512]{1,0:T(8,128)(2,1)}, f32[2,4,2,512]{3,2,1,0:T(2,128)}) custom-call(bf16[2048,512]{1,0:T(8,128)(2,1)} %get-tuple-element.366.refs_0_.refs_1_, bf16[2048,256]{1,0:T(8,128)(2,1)} %get-tuple-element.247.refs_1_.refs_2_, bf16[2048,256]{1,0:T(8,128)(2,1)} %get-tuple-element.248.refs_2_.refs_3_), custom_call_target="tpu_custom_call" | custom-call | flops 1000000 | bytes 1000000 | tf_op jit(solution)/shard_map/attend/pallas_call | solution.py:697
  144.6 21.3 %collective-permute-done.6.refs_2_ = bf16[256,2048]{1,0:T(8,128)(2,1)S(1)} collective-permute-done((bf16[256,2048]{1,0:T(8,128)(2,1)S(1)}, bf16[256,2048]{1,0:T(8,128)(2,1)S(1)}, u32[]{:S(2)}, u32[]{:S(2)}) %collective-permute-start.6) | collective-permute-done | bytes 1048608 | tf_op jit(solution)/shard_map/ppermute | solution.py:199
  167.1 19.4 %collective-permute-done.12.refs_4_ = bf16[256,2048]{1,0:T(8,128)(2,1)S(1)} collective-permute-done((bf16[256,2048]{1,0:T(8,128)(2,1)S(1)}, bf16[256,2048]{1,0:T(8,128)(2,1)S(1)}, u32[]{:S(2)}, u32[]{:S(2)}) %collective-permute-start.12) | collective-permute-done | bytes 1048608 | tf_op jit(solution)/shard_map/ppermute | solution.py:199
  199.3 17.6 %collective-permute-done.14.refs_2_ = bf16[256,2048]{1,0:T(8,128)(2,1)S(1)} collective-permute-done((bf16[256,2048]{1,0:T(8,128)(2,1)}, bf16[256,2048]{1,0:T(8,128)(2,1)S(1)}, u32[]{:S(2)}, u32[]{:S(2)}) %collective-permute-start.14) | collective-permute-done | bytes 1048608 | tf_op jit(solution)/shard_map/ppermute | solution.py:199
  230.3 12.9 %gate_up.3 = (bf16[512,1536]{1,0:T(8,128)(2,1)}, bf16[512,1536]{1,0:T(8,128)(2,1)}, bf16[512,1536]{1,0:T(8,128)(2,1)}) custom-call(s32[12]{0:T(128)} %copy-done.32, bf16[256,2048]{1,0:T(8,128)(2,1)} %get-tuple-element.350.refs_1_, bf16[256,2048]{1,0:T(8,128)(2,1)} %get-tuple-element.278.refs_2_, ...), custom_call_target="tpu_custom_call" | custom-call | flops 1000000 | bytes 1000000 | tf_op jit(solution)/shard_map/gate_up/pallas_call | solution.py:298
  255.9 20.1 %collective-permute-done.16.refs_1_.refs_3_ = bf16[256,2048]{1,0:T(8,128)(2,1)S(1)} collective-permute-done((bf16[256,2048]{1,0:T(8,128)(2,1)}, bf16[256,2048]{1,0:T(8,128)(2,1)S(1)}, u32[]{:S(2)}, u32[]{:S(2)}) %collective-permute-start.16) | collective-permute-done | bytes 1048608 | tf_op jit(solution)/shard_map/ppermute | solution.py:146
  278.0 18.9 %gate_up.4 = (bf16[1024,1536]{1,0:T(8,128)(2,1)}, bf16[1024,1536]{1,0:T(8,128)(2,1)}, bf16[1024,1536]{1,0:T(8,128)(2,1)}) custom-call(s32[12]{0:T(128)} %copy-done.32, bf16[256,2048]{1,0:T(8,128)(2,1)} %copy-done.45, bf16[256,2048]{1,0:T(8,128)(2,1)} %copy-done.44, bf16[256,2048]{1,0:T(8,128)(2,1)} %copy-done.43, bf16[256,2048]{1,0:T(8,128)(2,1)} %copy-done.46, ...), custom_call_target="tpu_custom_call" | custom-call | flops 1000000 | bytes 1000000 | tf_op jit(solution)/shard_map/gate_up/pallas_call | solution.py:298
  300.8 12.8 %gate_up.5 = (bf16[512,1536]{1,0:T(8,128)(2,1)}, bf16[512,1536]{1,0:T(8,128)(2,1)}, bf16[512,1536]{1,0:T(8,128)(2,1)}) custom-call(s32[12]{0:T(128)} %copy-done.32, bf16[256,2048]{1,0:T(8,128)(2,1)} %copy-done.48, bf16[256,2048]{1,0:T(8,128)(2,1)} %copy-done.47, bf16[2048,3072]{1,0:T(8,128)(2,1)} %all-gather.9.cloned.1.call-done.refs_3_.refs_4_.refs_5_.refs_6_.refs_2_, ...), custom_call_target="tpu_custom_call" | custom-call | flops 1000000 | bytes 1000000 | tf_op jit(solution)/shard_map/gate_up/pallas_call | solution.py:298
  313.6 15.6 %gate_up_grad.3.refs_1_.refs_11_.refs_12_.refs_13_.refs_14_ = bf16[1024,3072]{1,0:T(8,128)(2,1)} custom-call(s32[12]{0:T(128)} %copy-done.32, bf16[256,2048]{1,0:T(8,128)(2,1)} %collective-permute-done.8.refs_1_.refs_11_, bf16[256,2048]{1,0:T(8,128)(2,1)} %collective-permute-done.10.refs_2_.refs_12_, ...), custom_call_target="tpu_custom_call" | custom-call | flops 1000000 | bytes 1000000 | tf_op jit(solution)/shard_map/gate_up_grad/pallas_call | solution.py:298
  330.2 20.1 %weight_grad.5 = bf16[1536,2048]{1,0:T(8,128)(2,1)} custom-call(s32[12]{0:T(128)} %copy-done.32, bf16[512,1536]{1,0:T(8,128)(2,1)} %get-tuple-element.341.refs_1_.refs_2_, bf16[512,1536]{1,0:T(8,128)(2,1)} %get-tuple-element.341.refs_1_.refs_2_, bf16[1024,1536]{1,0:T(8,128)(2,1)} %get-tuple-element.336.refs_3_.refs_4_.refs_5_.refs_6_.refs_1_, ...), custom_call_target="tpu_custom_call" | custom-call | flops 1000000 | bytes 1000000 | tf_op jit(solution)/shard_map/weight_grad/pallas_call | solution.py:298
  350.3 19.2 %block_product.18 = (bf16[256,2048]{1,0:T(8,128)(2,1)}, bf16[256,2048]{1,0:T(8,128)(2,1)}, bf16[256,2048]{1,0:T(8,128)(2,1)}, bf16[256,2048]{1,0:T(8,128)(2,1)}) custom-call(s32[12]{0:T(128)} %copy-done.32, bf16[1024,3072]{1,0:T(8,128)(2,1)} %gate_up_grad.3.refs_1_.refs_11_.refs_12_.refs_13_.refs_14_, ...), custom_call_target="tpu_custom_call" | custom-call | flops 1000000 | bytes 1000000 | tf_op jit(solution)/shard_map/block_product/pallas_call | solution.py:298
  371.5 10.9 %gate_up_grad.4.refs_1_.refs_15_.refs_16_ = bf16[512,3072]{1,0:T(8,128)(2,1)} custom-call(s32[12]{0:T(128)} %copy-done.32, bf16[256,2048]{1,0:T(8,128)(2,1)} %copy-done.56, bf16[256,2048]{1,0:T(8,128)(2,1)} %collective-permute-done.23.refs_16_.refs_2_, bf16[1536,2048]{1,0:T(8,128)(2,1)} %all-gather.11.cloned.1.call-done.refs_5_.refs_3_.refs_2_, ...), custom_call_target="tpu_custom_call" | custom-call | flops 1000000 | bytes 1000000 | tf_op jit(solution)/shard_map/gate_up_grad/pallas_call | solution.py:298
  382.4 11.9 %block_product.19 = (bf16[256,2048]{1,0:T(8,128)(2,1)}, bf16[256,2048]{1,0:T(8,128)(2,1)}) custom-call(s32[12]{0:T(128)} %copy-done.32, bf16[512,3072]{1,0:T(8,128)(2,1)} %gate_up_grad.4.refs_1_.refs_15_.refs_16_, bf16[2048,3072]{1,0:T(8,128)(2,1)} %all-gather.9.cloned.1.call-done.refs_3_.refs_4_.refs_5_.refs_6_.refs_2_), custom_call_target="tpu_custom_call" | custom-call | flops 1000000 | bytes 1000000 | tf_op jit(solution)/shard_map/block_product/pallas_call | solution.py:298
  396.5 10.9 %gate_up_grad.5.refs_1_.refs_9_.refs_10_ = bf16[512,3072]{1,0:T(8,128)(2,1)} custom-call(s32[12]{0:T(128)} %copy-done.32, bf16[256,2048]{1,0:T(8,128)(2,1)} %copy-done.52, bf16[256,2048]{1,0:T(8,128)(2,1)} %copy-done.51, bf16[1536,2048]{1,0:T(8,128)(2,1)} %all-gather.11.cloned.1.call-done.refs_5_.refs_3_.refs_2_, ...), custom_call_target="tpu_custom_call" | custom-call | flops 1000000 | bytes 1000000 | tf_op jit(solution)/shard_map/gate_up_grad/pallas_call | solution.py:298
  407.4 12.1 %block_product.20.refs_2_ = bf16[512,2048]{1,0:T(8,128)(2,1)} custom-call(s32[12]{0:T(128)} %copy-done.32, bf16[512,3072]{1,0:T(8,128)(2,1)} %gate_up_grad.5.refs_1_.refs_9_.refs_10_, bf16[2048,3072]{1,0:T(8,128)(2,1)} %all-gather.9.cloned.1.call-done.refs_3_.refs_4_.refs_5_.refs_6_.refs_2_), custom_call_target="tpu_custom_call" | custom-call | flops 1000000 | bytes 1000000 | tf_op jit(solution)/shard_map/block_product/pallas_call | solution.py:298
  427.7 19.8 %weight_grad.6 = bf16[2048,1536]{1,0:T(8,128)(2,1)} custom-call(s32[12]{0:T(128)} %copy-done.32, bf16[256,2048]{1,0:T(8,128)(2,1)} %get-tuple-element.350.refs_1_, bf16[256,2048]{1,0:T(8,128)(2,1)} %get-tuple-element.278.refs_2_, bf16[256,2048]{1,0:T(8,128)(2,1)} %copy-done.45, bf16[256,2048]{1,0:T(8,128)(2,1)} %copy-done.44, bf16[256,2048]{1,0:T(8,128)(2,1)} %copy-done.43, ...), custom_call_target="tpu_custom_call" | custom-call | flops 1000000 | bytes 1000000 | tf_op jit(solution)/shard_map/weight_grad/pallas_call | solution.py:298
  448.9 9.5 %norm_gradient.2 = (bf16[256,2048]{1,0:T(8,128)(2,1)}, bf16[256,2048]{1,0:T(8,128)(2,1)}, bf16[512,2048]{1,0:T(8,128)(2,1)}, f32[1,2048]{1,0:T(1,128)}) custom-call(bf16[512,2048]{1,0:T(8,128)(2,1)} %refs_0_.5, f32[512,2048]{1,0:T(8,128)} %get-tuple-element.279.refs_1_.refs_0_, bf16[512,2048]{1,0:T(8,128)(2,1)} %block_product.20.refs_2_, ...), custom_call_target="tpu_custom_call" | custom-call | flops 1000000 | bytes 1000000 | tf_op jit(solution)/shard_map/norm_gradient/pallas_call | solution.py:505
  512.8 19.9 %weight_grad.7 = bf16[2048,1536]{1,0:T(8,128)(2,1)} custom-call(s32[12]{0:T(128)} %copy-done.32, bf16[256,2048]{1,0:T(8,128)(2,1)} %get-tuple-element.350.refs_1_, bf16[256,2048]{1,0:T(8,128)(2,1)} %get-tuple-element.278.refs_2_, bf16[256,2048]{1,0:T(8,128)(2,1)} %copy-done.45, bf16[256,2048]{1,0:T(8,128)(2,1)} %copy-done.44, bf16[256,2048]{1,0:T(8,128)(2,1)} %copy-done.43, ...), custom_call_target="tpu_custom_call" | custom-call | flops 1000000 | bytes 1000000 | tf_op jit(solution)/shard_map/weight_grad/pallas_call | solution.py:298
  543.7 10.6 %weight_grad.8 = bf16[512,2048]{1,0:T(8,128)(2,1)} custom-call(s32[12]{0:T(128)} %copy-done.32, bf16[2048,512]{1,0:T(8,128)(2,1)} %get-tuple-element.356.refs_1_.refs_2_.refs_3_.refs_4_.refs_5_.refs_6_.refs_7_.refs_8_, bf16[2048,512]{1,0:T(8,128)(2,1)} %get-tuple-element.356.refs_1_.refs_2_.refs_3_.refs_4_.refs_5_.refs_6_.refs_7_.refs_8_, ...), custom_call_target="tpu_custom_call" | custom-call | flops 1000000 | bytes 1000000 | tf_op jit(solution)/shard_map/weight_grad/pallas_call | solution.py:298
  554.3 24.6 %attend_back.2 = (bf16[2048,1024]{1,0:T(8,128)(2,1)}, f32[2,128]{1,0:T(2,128)}) custom-call(s32[4]{0:T(128)} %compare_select_fusion.5.refs_0_, bf16[2048,512]{1,0:T(8,128)(2,1)} %get-tuple-element.366.refs_0_.refs_1_, bf16[2048,256]{1,0:T(8,128)(2,1)} %get-tuple-element.247.refs_1_.refs_2_, bf16[2048,256]{1,0:T(8,128)(2,1)} %get-tuple-element.248.refs_2_.refs_3_, ...), custom_call_target="tpu_custom_call" | custom-call | flops 1000000 | bytes 1000000 | tf_op jit(solution)/shard_map/attend_back/pallas_call | solution.py:834
  585.4 24.7 %attend_back.3 = (bf16[2048,1024]{1,0:T(8,128)(2,1)}, f32[2,128]{1,0:T(2,128)}) custom-call(s32[4]{0:T(128)} %compare_select_fusion.5.refs_0_, bf16[2048,512]{1,0:T(8,128)(2,1)} %get-tuple-element.366.refs_0_.refs_1_, bf16[2048,256]{1,0:T(8,128)(2,1)} %get-tuple-element.247.refs_1_.refs_2_, ...), custom_call_target="tpu_custom_call", output_to_operand_aliasing={{0}: (12, {})} | custom-call | flops 1000000 | bytes 1000000 | tf_op jit(solution)/shard_map/attend_back/pallas_call | solution.py:834
  632.4 16.8 %weight_grad.9 = (bf16[2048,1024]{1,0:T(8,128)(2,1)}, f32[1,2048]{1,0:T(1,128)}) custom-call(s32[12]{0:T(128)} %copy-done.32, bf16[256,2048]{1,0:T(8,128)(2,1)} %copy-done.50, bf16[256,2048]{1,0:T(8,128)(2,1)} %copy-done.49, bf16[256,2048]{1,0:T(8,128)(2,1)} %collective-permute-done.4.refs_1_.refs_3_, bf16[256,2048]{1,0:T(8,128)(2,1)} %copy-done.54, ...), custom_call_target="tpu_custom_call" | custom-call | flops 1000000 | bytes 1000000 | tf_op jit(solution)/shard_map/weight_grad/pallas_call | solution.py:298
  686.2 10.2 %adamw.2 = (f32[256,2,1536]{2,1,0:T(2,128)}, f32[256,2,1536]{2,1,0:T(2,128)}, f32[256,2,1536]{2,1,0:T(2,128)}) custom-call(f32[256,2,1536]{2,1,0:T(2,128)} %refs_0_.6, f32[256,2,1536]{2,1,0:T(2,128)} %refs_1_.3, f32[256,2,1536]{2,1,0:T(2,128)} %refs_2_.2, bf16[256,1536]{1,0:T(8,128)(2,1)} %reduce-scatter.8.cloned.1.call-done.refs_3_, ...), custom_call_target="tpu_custom_call" | custom-call | flops 1000000 | bytes 1000000 | tf_op jit(solution)/shard_map/adamw/pallas_call | solution.py:92
  (364 shorter events, 300.3 us)
Async XLA Ops:
  7.2 52.9 %all-gather.5.cloned.1.call-start = ((), (), s32[]{:S(2)}) async-start(), calls=%async_computation.5 | async-start | bytes 4718592 | tf_op jit(solution)/shard_map/all_gather | solution.py:946
  9.9 118.0 %all-gather.7.cloned.1.call-start = ((), (), s32[]{:S(2)}) async-start(), calls=%async_computation.6 | async-start | bytes 2359296 | tf_op jit(solution)/shard_map/all_gather | solution.py:947
  11.7 205.8 %all-gather.9.cloned.1.call-start = ((), (), s32[]{:S(2)}) async-start(), calls=%async_computation.7 | async-start | bytes 14155776 | tf_op jit(solution)/shard_map/all_gather | solution.py:948
  14.3 299.4 %all-gather.11.cloned.1.call-start = ((), (), s32[]{:S(2)}) async-start(), calls=%async_computation.8 | async-start | bytes 7077888 | tf_op jit(solution)/shard_map/all_gather | solution.py:949
  16.9 480.1 %reduce-scatter.6.cloned.1.call-start = ((), (), s32[]{:S(2)}) async-start(), calls=%async_computation.9 | async-start | bytes 7077888 | tf_op jit(solution)/shard_map/reduce_scatter | solution.py:1021
  18.9 48.8 %collective-permute-start.1 = (bf16[256,2048]{1,0:T(8,128)(2,1)S(1)}, bf16[256,2048]{1,0:T(8,128)(2,1)S(1)}, u32[]{:S(2)}, u32[]{:S(2)}) collective-permute-start(bf16[256,2048]{1,0:T(8,128)(2,1)S(1)} %get-tuple-element.431.refs_2_), channel_id=1, source_target_pairs={{1,0},{3,1},{2,3},{0,2},{5,4},{7,5},{6,7},{4,6},{9,8},{11,9},{10,1... | collective-permute-start | bytes 3145736 | tf_op jit(solution)/shard_map/ppermute | solution.py:144
  22.0 45.8 %collective-permute-start = (bf16[256,2048]{1,0:T(8,128)(2,1)S(1)}, bf16[256,2048]{1,0:T(8,128)(2,1)}, u32[]{:S(2)}, u32[]{:S(2)}) collective-permute-start(bf16[256,2048]{1,0:T(8,128)(2,1)S(1)} %get-tuple-element.377.refs_1_), channel_id=1, source_target_pairs={{0,1},{1,3},{3,2},{2,0},{4,5},{5,7},{7,6},{6,4},{8,9},{9,11},{11,1... | collective-permute-start | bytes 3145736 | tf_op jit(solution)/shard_map/ppermute | solution.py:143
  22.0 48.1 %collective-permute-start.5 = (bf16[256,2048]{1,0:T(8,128)(2,1)S(1)}, bf16[256,2048]{1,0:T(8,128)(2,1)}, u32[]{:S(2)}, u32[]{:S(2)}) collective-permute-start(bf16[256,2048]{1,0:T(8,128)(2,1)S(1)} %get-tuple-element.431.refs_2_), channel_id=1, source_target_pairs={{0,1},{1,3},{3,2},{2,0},{4,5},{5,7},{7,6},{6,4},{8,9},{9,11},{11,1... | collective-permute-start | bytes 3145736 | tf_op jit(solution)/shard_map/ppermute | solution.py:145
  24.0 46.1 %collective-permute-start.4 = (bf16[256,2048]{1,0:T(8,128)(2,1)S(1)}, bf16[256,2048]{1,0:T(8,128)(2,1)}, u32[]{:S(2)}, u32[]{:S(2)}) collective-permute-start(bf16[256,2048]{1,0:T(8,128)(2,1)S(1)} %get-tuple-element.377.refs_1_), channel_id=1, source_target_pairs={{1,0},{3,1},{2,3},{0,2},{5,4},{7,5},{6,7},{4,6},{9,8},{11,9},{10,1... | collective-permute-start | bytes 3145736 | tf_op jit(solution)/shard_map/ppermute | solution.py:146
  94.8 46.2 %collective-permute-start.11 = (bf16[256,2048]{1,0:T(8,128)(2,1)S(1)}, bf16[256,2048]{1,0:T(8,128)(2,1)S(1)}, u32[]{:S(2)}, u32[]{:S(2)}) collective-permute-start(bf16[256,2048]{1,0:T(8,128)(2,1)S(1)} %get-tuple-element.429.refs_10_.refs_2_), channel_id=1, source_target_pairs={{0,1},{1,3},{3,2},{2,0},{4,5},{5,7},{7,6},{6,4},{8,9},{9,11},{11,1... | collective-permute-start | bytes 3145736 | tf_op jit(solution)/shard_map/ppermute | solution.py:145
  96.4 45.2 %collective-permute-start.10 = (bf16[256,2048]{1,0:T(8,128)(2,1)S(1)}, bf16[256,2048]{1,0:T(8,128)(2,1)}, u32[]{:S(2)}, u32[]{:S(2)}) collective-permute-start(bf16[256,2048]{1,0:T(8,128)(2,1)S(1)} %get-tuple-element.429.refs_10_.refs_2_), channel_id=1, source_target_pairs={{1,0},{3,1},{2,3},{0,2},{5,4},{7,5},{6,7},{4,6},{9,8},{11,9},{10,1... | collective-permute-start | bytes 3145736 | tf_op jit(solution)/shard_map/ppermute | solution.py:144
  96.9 46.6 %collective-permute-start.9 = (bf16[256,2048]{1,0:T(8,128)(2,1)S(1)}, bf16[256,2048]{1,0:T(8,128)(2,1)}, u32[]{:S(2)}, u32[]{:S(2)}) collective-permute-start(bf16[256,2048]{1,0:T(8,128)(2,1)S(1)} %get-tuple-element.315.refs_9_.refs_1_), channel_id=1, source_target_pairs={{0,1},{1,3},{3,2},{2,0},{4,5},{5,7},{7,6},{6,4},{8,9},{9,11},{11,1... | collective-permute-start | bytes 3145736 | tf_op jit(solution)/shard_map/ppermute | solution.py:143
  98.5 46.1 %collective-permute-start.8 = (bf16[256,2048]{1,0:T(8,128)(2,1)S(1)}, bf16[256,2048]{1,0:T(8,128)(2,1)}, u32[]{:S(2)}, u32[]{:S(2)}) collective-permute-start(bf16[256,2048]{1,0:T(8,128)(2,1)S(1)} %get-tuple-element.315.refs_9_.refs_1_), channel_id=1, source_target_pairs={{1,0},{3,1},{2,3},{0,2},{5,4},{7,5},{6,7},{4,6},{9,8},{11,9},{10,1... | collective-permute-start | bytes 3145736 | tf_op jit(solution)/shard_map/ppermute | solution.py:146
  228.3 47.7 %collective-permute-start.16 = (bf16[256,2048]{1,0:T(8,128)(2,1)}, bf16[256,2048]{1,0:T(8,128)(2,1)S(1)}, u32[]{:S(2)}, u32[]{:S(2)}) collective-permute-start(bf16[256,2048]{1,0:T(8,128)(2,1)} %get-tuple-element.350.refs_1_), channel_id=1, source_target_pairs={{1,0},{3,1},{2,3},{0,2},{5,4},{7,5},{6,7},{4,6},{9,8},{11,9},{10,1... | collective-permute-start | bytes 3145736 | tf_op jit(solution)/shard_map/ppermute | solution.py:146
  229.7 46.3 %collective-permute-start.19 = (bf16[256,2048]{1,0:T(8,128)(2,1)}, bf16[256,2048]{1,0:T(8,128)(2,1)S(1)}, u32[]{:S(2)}, u32[]{:S(2)}) collective-permute-start(bf16[256,2048]{1,0:T(8,128)(2,1)} %get-tuple-element.278.refs_2_), channel_id=1, source_target_pairs={{0,1},{1,3},{3,2},{2,0},{4,5},{5,7},{7,6},{6,4},{8,9},{9,11},{11,1... | collective-permute-start | bytes 3145736 | tf_op jit(solution)/shard_map/ppermute | solution.py:145
  253.5 45.4 %collective-permute-start.21 = (bf16[256,2048]{1,0:T(8,128)(2,1)S(1)}, bf16[256,2048]{1,0:T(8,128)(2,1)S(1)}, u32[]{:S(2)}, u32[]{:S(2)}) collective-permute-start(bf16[256,2048]{1,0:T(8,128)(2,1)S(1)} %collective-permute-done.18.refs_2_.refs_4_), channel_id=1, source_target_pairs={{1,0},{3,1},{2,3},{0,2},{5,4},{7,5},{6,7},{4,6},{9,8},{11,9},{10,1... | collective-permute-start | bytes 3145736 | tf_op jit(solution)/shard_map/ppermute | solution.py:159
  350.3 259.8 %reduce-scatter.8.cloned.1.call-start = ((), (), s32[]{:S(2)}) async-start(), calls=%async_computation.10 | async-start | bytes 7077888 | tf_op jit(solution)/shard_map/reduce_scatter | solution.py:1044
  369.5 49.9 %collective-permute-start.26 = (bf16[256,2048]{1,0:T(8,128)(2,1)}, bf16[256,2048]{1,0:T(8,128)(2,1)S(1)}, u32[]{:S(2)}, u32[]{:S(2)}) collective-permute-start(bf16[256,2048]{1,0:T(8,128)(2,1)} %get-tuple-element.308), channel_id=1, source_target_pairs={{0,1},{1,3},{3,2},{2,0},{4,5},{5,7},{7,6},{6,4},{8,9},{9,11},{11,1... | collective-permute-start | bytes 3145736 | tf_op jit(solution)/shard_map/ppermute | solution.py:199
  370.7 48.8 %collective-permute-start.27 = (bf16[256,2048]{1,0:T(8,128)(2,1)}, bf16[256,2048]{1,0:T(8,128)(2,1)S(1)}, u32[]{:S(2)}, u32[]{:S(2)}) collective-permute-start(bf16[256,2048]{1,0:T(8,128)(2,1)} %get-tuple-element.309), channel_id=1, source_target_pairs={{1,0},{3,1},{2,3},{0,2},{5,4},{7,5},{6,7},{4,6},{9,8},{11,9},{10,1... | collective-permute-start | bytes 3145736 | tf_op jit(solution)/shard_map/ppermute | solution.py:199
  448.9 213.9 %reduce-scatter.12.cloned.1.call-start = ((), (), s32[]{:S(2)}) async-start(), calls=%async_computation.12 | async-start | bytes 7077888 | tf_op jit(solution)/shard_map/reduce_scatter | solution.py:1083
  460.5 45.0 %collective-permute-start.34 = (bf16[256,2048]{1,0:T(8,128)(2,1)}, bf16[256,2048]{1,0:T(8,128)(2,1)}, u32[]{:S(2)}, u32[]{:S(2)}) collective-permute-start(bf16[256,2048]{1,0:T(8,128)(2,1)} %get-tuple-element.332.refs_1_.refs_9_), channel_id=1, source_target_pairs={{1,0},{3,1},{2,3},{0,2},{5,4},{7,5},{6,7},{4,6},{9,8},{11,9},{10,1... | collective-permute-start | bytes 3145736 | tf_op jit(solution)/shard_map/ppermute | solution.py:146
  532.8 149.1 %reduce-scatter.10.cloned.1.call-start = ((), (), s32[]{:S(2)}) async-start(), calls=%async_computation.11 | async-start | bytes 2359296 | tf_op jit(solution)/shard_map/reduce_scatter | solution.py:1156
  532.9 46.0 %collective-permute-start.38 = (bf16[256,2048]{1,0:T(8,128)(2,1)}, bf16[256,2048]{1,0:T(8,128)(2,1)}, u32[]{:S(2)}, u32[]{:S(2)}) collective-permute-start(bf16[256,2048]{1,0:T(8,128)(2,1)} %copy-done.40), channel_id=1, source_target_pairs={{0,1},{1,3},{3,2},{2,0},{4,5},{5,7},{7,6},{6,4},{8,9},{9,11},{11,1... | collective-permute-start | bytes 3145736 | tf_op jit(solution)/shard_map/ppermute | solution.py:199
  610.2 102.5 %reduce-scatter.14.cloned.1.call-start = ((), (), s32[]{:S(2)}) async-start(), calls=%async_computation.13 | async-start | bytes 4718592 | tf_op jit(solution)/shard_map/reduce_scatter | solution.py:1158
  (129 other events, 1727.0 us)
Sparse Core Ops, SparseCore 0:
  10.2 49.8 all-gather.4
  62.3 29.5 all-gather.6
  94.1 115.7 all-gather.8
  211.3 63.3 all-gather.10
  350.4 68.5 reduce-scatter.5
  449.0 68.4 reduce-scatter.7
  533.0 68.6 reduce-scatter.11
  610.3 34.5 reduce-scatter.9
  663.0 49.5 reduce-scatter.13

commit v5 on v4

--- a/solution.py
+++ b/solution.py
@@ -386,41 +386,64 @@
     )
 
 
-def gate_grad_kernel(count, *refs):
-    rows = stacked(refs[1 : 1 + count])
-    down_ref, gate_ref, up_ref, out_ref = refs[1 + count :]
+def gate_grad_kernel(count, steps, *refs):
+    down_ref, gate_ref, up_ref, matrix_ref, out_ref = refs[1 + count : 6 + count]
+    part_refs = refs[6 + count :]
     step = pl.program_id(0)
     tile = gate_ref.shape[1]
     width = out_ref.shape[1] // 2
-    grad = contract_cols(rows, down_ref[...])
-    gate = gate_ref[...].astype(jnp.float32)
-    up = up_ref[...].astype(jnp.float32)
-    sigmoid_gate = jax.nn.sigmoid(gate)
-    scaled = grad * sigmoid_gate
-    start = pl.multiple_of(step * tile, tile)
-    out_ref[:, pl.ds(start, tile)] = (
-        scaled * up * (1.0 + gate * (1.0 - sigmoid_gate))
-    ).astype(jnp.bfloat16)
-    out_ref[:, pl.ds(pl.multiple_of(width + step * tile, tile), tile)] = (scaled * gate).astype(
-        jnp.bfloat16
-    )
-
-
-def gate_up_gradient(table, pieces, down, gate, up):
+
+    @pl.when(step < steps)
+    def _():
+        grad = contract_cols(stacked(refs[1 : 1 + count]), down_ref[...])
+        gate = gate_ref[...].astype(jnp.float32)
+        up = up_ref[...].astype(jnp.float32)
+        sigmoid_gate = jax.nn.sigmoid(gate)
+        scaled = grad * sigmoid_gate
+        start = pl.multiple_of(step * tile, tile)
+        out_ref[:, pl.ds(start, tile)] = (
+            scaled * up * (1.0 + gate * (1.0 - sigmoid_gate))
+        ).astype(jnp.bfloat16)
+        out_ref[:, pl.ds(pl.multiple_of(width + step * tile, tile), tile)] = (
+            scaled * gate
+        ).astype(jnp.bfloat16)
+
+    @pl.when(step >= steps)
+    def _():
+        result = contract_cols(out_ref[...], matrix_ref[...])
+        size = part_refs[0].shape[0]
+        for i, part_ref in enumerate(part_refs):
+            part_ref[...] = result[i * size : (i + 1) * size].astype(part_ref.dtype)
+
+
+def gate_up_gradient(table, pieces, down, gate, up, matrix, parts):
     count, width = gate.shape
     tile = tile_of(width, 256)
-    part = pl.BlockSpec((count, tile), lambda i, table: (0, i))
-    return row_call(
-        lambda *refs: gate_grad_kernel(len(pieces), *refs),
+    steps = width // tile
+    out_width = matrix.shape[0]
+    out_tile = tile_of(out_width, 512)
+    first = lambda i: jnp.minimum(i, steps - 1)
+    later = lambda i: jnp.maximum(i - steps, 0)
+    part = pl.BlockSpec((count, tile), lambda i, table: (0, first(i)))
+    grads, *products = row_call(
+        lambda *refs: gate_grad_kernel(len(pieces), steps, *refs),
         "gate_up_grad",
         table,
-        (width // tile,),
-        [piece.array for piece in pieces] + [down, gate, up],
+        (steps + out_width // out_tile,),
+        [piece.array for piece in pieces] + [down, gate, up, matrix],
         [piece.spec() for piece in pieces]
-        + [pl.BlockSpec((tile, down.shape[1]), lambda i, table: (i, 0)), part, part],
-        [jax.ShapeDtypeStruct((count, 2 * width), jnp.bfloat16)],
-        [pl.BlockSpec((count, 2 * width), lambda i, table: (0, 0))],
-    )[0]
+        + [
+            pl.BlockSpec((tile, down.shape[1]), lambda i, table: (first(i), 0)),
+            part,
+            part,
+            pl.BlockSpec((out_tile, 2 * width), lambda i, table: (later(i), 0)),
+        ],
+        [jax.ShapeDtypeStruct((count, 2 * width), jnp.bfloat16)]
+        + [jax.ShapeDtypeStruct((count // parts, out_width), jnp.bfloat16)] * parts,
+        [pl.BlockSpec((count, 2 * width), lambda i, table: (0, 0))]
+        + [pl.BlockSpec((count // parts, out_tile), lambda i, table: (0, later(i)))] * parts,
+    )
+    return grads, products if parts > 1 else products[0]
 
 
 def rows_kernel(count, weighed, *refs):
@@ -1001,33 +1024,28 @@
     activated = [parts[0] for parts in gate_groups]
     two_parts = [None] * (last + 1)
 
-    def two_grads(group):
+    def two_part(group):
         cots = [turn(cot_groups[group][0])] + cot_groups[group][1:]
-        grads[group] = mark(
-            gate_up_gradient(table, pieces_of(cots), down_full, *gate_groups[group][1:])
+        grads[group], part = gate_up_gradient(
+            table,
+            pieces_of(cots),
+            down_full,
+            *gate_groups[group][1:],
+            swiglu_matrix,
+            parts_of(group),
         )
-
-    def two_product(group):
-        two_parts[group] = marked(
-            block_product(
-                table, [Piece(turn(grads[group]))], swiglu_matrix, True, parts_of(group)
-            )
-        )
+        two_parts[group] = marked(part)
 
     for group in range(1, last):
-        two_grads(group)
+        two_part(group)
     lefts = split_groups([turn(activated[0])] + activated[1:], half)
     down_part = mark(weight_gradient(table, lefts, flat(cot_groups)))
     down_grad = lax.psum_scatter(down_part, "dp", scatter_dimension=1, tiled=True)
-    for group in range(1, last):
-        two_product(group)
-    two_grads(last)
-    two_product(last)
+    two_part(last)
     more = []
 
     def own_part():
-        two_grads(0)
-        two_product(0)
+        two_part(0)
 
     def swiglu_gradient():
         twos = flat(two_groups)

time: 735 us -> 731 us (level)
  Pallas kernels: 429 us -> 420 us
    pallas_call x26 -> x23, Pallas kernels: 263 us -> 255 us  [row_call(): pl.pallas_call(kernel, grid_spec=pltpu.PrefetchScalarGridSpec(num_scalar_...]
    unnamed x180 -> x184, local copies, waits for them, and re-layouts: 54.1 us -> 53.3 us
  transfers between devices with their start and end apart: 64 -> 64, of which waited for: 20 -> 22; matrix products, arithmetic and copies ran while one was open for 3% -> 3% of each run, Pallas kernels for 56% -> 50%
where the time goes in v5:
time: 731 us; the launch traced here: 722 us
  Pallas kernels  420 us (57%)
  waiting for transfers between devices  147 us (20%)
  starting transfers between devices  59.6 us (8%)
  local copies, waits for them, and re-layouts  54.4 us (7%)
  other arithmetic  25.3 us (3%)
  between operations  15.3 us (2%)
    pallas_call x23, Pallas kernels, row_call(): pl.pallas_call(kernel, grid_spec=pltpu.PrefetchScalarGridSpec(num_scalar_...  255 us
    ppermute x24, waiting for transfers between devices, ring_scatter(): send = lambda value, pairs: lax.ppermute(value, 'tensor', pairs)  65.3 us
    unnamed x184, local copies, waits for them, and re-layouts  53.3 us
    pallas_call x2, Pallas kernels, attention_backward(): pl.pallas_call(lambda *refs: attend_back_kernel(HEAD_WIDTH ** (-0.5), *re...  49.3 us
    pallas_call x4, Pallas kernels, row_kernel_call(): pl.pallas_call(lambda *refs: kernel(split, len(lows), *refs), grid=(2 * s...  31.7 us
    pallas_call x4, Pallas kernels, project(): pl.pallas_call(lambda *refs: project_kernel(len(blocks), *refs), grid_spe...  31.7 us
    all_gather x1, waiting for transfers between devices, local(): in_matrix = lax.all_gather(in_low, 'dp', axis=0, tiled=True)  30.4 us
    ppermute x24, starting transfers between devices, ring_scatter(): send = lambda value, pairs: lax.ppermute(value, 'tensor', pairs)  25.3 us
  transfers between devices with their start and end apart: 64, of which 22 were waited for; matrix products, arithmetic and copies ran while one was open for 3% of the time, Pallas kernels for 50%

profile of v5, /device:TPU:0, one launch (start us, length us, event | category | flops | bytes accessed | tf_op | source)
XLA Modules:
  0.0 721.6 jit_solution(17655221581277428574)
XLA Ops:
  29.7 30.4 %all-gather.5.cloned.1.call-done.refs_3_.refs_2_.refs_17_ = bf16[2048,1024]{1,0:T(8,128)(2,1)} async-done(((bf16[256,1024]{1,0:T(8,128)(2,1)}), bf16[2048,1024]{1,0:T(8,128)(2,1)}) %all-gather.5.cloned.1.call-update) | async-done | bytes 4194320 | tf_op jit(solution)/shard_map/all_gather | solution.py:969
  99.1 8.3 %project.7 = (bf16[2048,512]{1,0:T(8,128)(2,1)}, bf16[2048,256]{1,0:T(8,128)(2,1)}, bf16[2048,256]{1,0:T(8,128)(2,1)}, f32[2048,512]{1,0:T(8,128)}, f32[2048,256]{1,0:T(8,128)}) custom-call(s32[1]{0:T(128)} %bitcast.3.refs_0_, ...), custom_call_target="tpu_custom_call", output_to_operand_aliasing={{0}: (7, {}), {1}: (8, {}), {2}: (9, {}), {3}: (10, {}), {4... | custom-call | flops 1000000 | bytes 1000000 | tf_op jit(solution)/shard_map/project/pallas_call | solution.py:628
  107.3 20.5 %attend.1 = (bf16[2048,512]{1,0:T(8,128)(2,1)}, f32[2,4,2,512]{3,2,1,0:T(2,128)}) custom-call(bf16[2048,512]{1,0:T(8,128)(2,1)} %get-tuple-element.368.refs_0_.refs_1_, bf16[2048,256]{1,0:T(8,128)(2,1)} %get-tuple-element.248.refs_1_.refs_2_, bf16[2048,256]{1,0:T(8,128)(2,1)} %get-tuple-element.249.refs_2_.refs_3_), custom_call_target="tpu_custom_call" | custom-call | flops 1000000 | bytes 1000000 | tf_op jit(solution)/shard_map/attend/pallas_call | solution.py:720
  144.6 21.3 %collective-permute-done.6.refs_2_ = bf16[256,2048]{1,0:T(8,128)(2,1)S(1)} collective-permute-done((bf16[256,2048]{1,0:T(8,128)(2,1)S(1)}, bf16[256,2048]{1,0:T(8,128)(2,1)S(1)}, u32[]{:S(2)}, u32[]{:S(2)}) %collective-permute-start.6) | collective-permute-done | bytes 1048608 | tf_op jit(solution)/shard_map/ppermute | solution.py:199
  167.1 19.3 %collective-permute-done.12.refs_4_ = bf16[256,2048]{1,0:T(8,128)(2,1)S(1)} collective-permute-done((bf16[256,2048]{1,0:T(8,128)(2,1)S(1)}, bf16[256,2048]{1,0:T(8,128)(2,1)S(1)}, u32[]{:S(2)}, u32[]{:S(2)}) %collective-permute-start.12) | collective-permute-done | bytes 1048608 | tf_op jit(solution)/shard_map/ppermute | solution.py:199
  199.3 17.6 %collective-permute-done.14.refs_2_ = bf16[256,2048]{1,0:T(8,128)(2,1)S(1)} collective-permute-done((bf16[256,2048]{1,0:T(8,128)(2,1)}, bf16[256,2048]{1,0:T(8,128)(2,1)S(1)}, u32[]{:S(2)}, u32[]{:S(2)}) %collective-permute-start.14) | collective-permute-done | bytes 1048608 | tf_op jit(solution)/shard_map/ppermute | solution.py:199
  230.3 12.9 %gate_up.3 = (bf16[512,1536]{1,0:T(8,128)(2,1)}, bf16[512,1536]{1,0:T(8,128)(2,1)}, bf16[512,1536]{1,0:T(8,128)(2,1)}) custom-call(s32[12]{0:T(128)} %copy-done.32, bf16[256,2048]{1,0:T(8,128)(2,1)} %get-tuple-element.352.refs_1_, bf16[256,2048]{1,0:T(8,128)(2,1)} %get-tuple-element.279.refs_2_, ...), custom_call_target="tpu_custom_call" | custom-call | flops 1000000 | bytes 1000000 | tf_op jit(solution)/shard_map/gate_up/pallas_call | solution.py:298
  243.2 9.4 %collective-permute-done.17.refs_3_.refs_5_ = bf16[256,2048]{1,0:T(8,128)(2,1)S(1)} collective-permute-done((bf16[256,2048]{1,0:T(8,128)(2,1)}, bf16[256,2048]{1,0:T(8,128)(2,1)S(1)}, u32[]{:S(2)}, u32[]{:S(2)}) %collective-permute-start.17) | collective-permute-done | bytes 1048608 | tf_op jit(solution)/shard_map/ppermute | solution.py:143
  255.9 20.1 %collective-permute-done.16.refs_1_.refs_3_ = bf16[256,2048]{1,0:T(8,128)(2,1)S(1)} collective-permute-done((bf16[256,2048]{1,0:T(8,128)(2,1)}, bf16[256,2048]{1,0:T(8,128)(2,1)S(1)}, u32[]{:S(2)}, u32[]{:S(2)}) %collective-permute-start.16) | collective-permute-done | bytes 1048608 | tf_op jit(solution)/shard_map/ppermute | solution.py:146
  278.0 18.9 %gate_up.4 = (bf16[1024,1536]{1,0:T(8,128)(2,1)}, bf16[1024,1536]{1,0:T(8,128)(2,1)}, bf16[1024,1536]{1,0:T(8,128)(2,1)}) custom-call(s32[12]{0:T(128)} %copy-done.32, bf16[256,2048]{1,0:T(8,128)(2,1)} %copy-done.45, bf16[256,2048]{1,0:T(8,128)(2,1)} %copy-done.44, bf16[256,2048]{1,0:T(8,128)(2,1)} %copy-done.43, bf16[256,2048]{1,0:T(8,128)(2,1)} %copy-done.46, ...), custom_call_target="tpu_custom_call" | custom-call | flops 1000000 | bytes 1000000 | tf_op jit(solution)/shard_map/gate_up/pallas_call | solution.py:298
  300.8 12.9 %gate_up.5 = (bf16[512,1536]{1,0:T(8,128)(2,1)}, bf16[512,1536]{1,0:T(8,128)(2,1)}, bf16[512,1536]{1,0:T(8,128)(2,1)}) custom-call(s32[12]{0:T(128)} %copy-done.32, bf16[256,2048]{1,0:T(8,128)(2,1)} %copy-done.48, bf16[256,2048]{1,0:T(8,128)(2,1)} %copy-done.47, bf16[2048,3072]{1,0:T(8,128)(2,1)} %all-gather.9.cloned.1.call-done.refs_3_.refs_4_.refs_5_.refs_6_.refs_8_, ...), custom_call_target="tpu_custom_call" | custom-call | flops 1000000 | bytes 1000000 | tf_op jit(solution)/shard_map/gate_up/pallas_call | solution.py:298
  317.2 31.2 %gate_up_grad.3 = (bf16[1024,3072]{1,0:T(8,128)(2,1)}, bf16[256,2048]{1,0:T(8,128)(2,1)}, bf16[256,2048]{1,0:T(8,128)(2,1)}, bf16[256,2048]{1,0:T(8,128)(2,1)}, bf16[256,2048]{1,0:T(8,128)(2,1)}) custom-call(s32[12]{0:T(128)} %copy-done.32, bf16[256,2048]{1,0:T(8,128)(2,1)} %collective-permute-done.8.refs_1_.refs_11_, ...), custom_call_target="tpu_custom_call" | custom-call | flops 1000000 | bytes 1000000 | tf_op jit(solution)/shard_map/gate_up_grad/pallas_call | solution.py:298
  348.4 20.1 %weight_grad.5 = bf16[1536,2048]{1,0:T(8,128)(2,1)} custom-call(s32[12]{0:T(128)} %copy-done.32, bf16[512,1536]{1,0:T(8,128)(2,1)} %get-tuple-element.343.refs_1_.refs_2_, bf16[512,1536]{1,0:T(8,128)(2,1)} %get-tuple-element.343.refs_1_.refs_2_, bf16[1024,1536]{1,0:T(8,128)(2,1)} %get-tuple-element.338.refs_3_.refs_4_.refs_5_.refs_6_.refs_1_, ...), custom_call_target="tpu_custom_call" | custom-call | flops 1000000 | bytes 1000000 | tf_op jit(solution)/shard_map/weight_grad/pallas_call | solution.py:298
  371.7 20.0 %gate_up_grad.4 = (bf16[512,3072]{1,0:T(8,128)(2,1)}, bf16[256,2048]{1,0:T(8,128)(2,1)}, bf16[256,2048]{1,0:T(8,128)(2,1)}) custom-call(s32[12]{0:T(128)} %copy-done.32, bf16[256,2048]{1,0:T(8,128)(2,1)} %copy-done.56, bf16[256,2048]{1,0:T(8,128)(2,1)} %collective-permute-done.23.refs_16_.refs_2_, ...), custom_call_target="tpu_custom_call" | custom-call | flops 1000000 | bytes 1000000 | tf_op jit(solution)/shard_map/gate_up_grad/pallas_call | solution.py:298
  393.9 20.2 %gate_up_grad.5 = (bf16[512,3072]{1,0:T(8,128)(2,1)}, bf16[512,2048]{1,0:T(8,128)(2,1)}) custom-call(s32[12]{0:T(128)} %copy-done.32, bf16[256,2048]{1,0:T(8,128)(2,1)} %copy-done.52, bf16[256,2048]{1,0:T(8,128)(2,1)} %copy-done.51, bf16[1536,2048]{1,0:T(8,128)(2,1)} %all-gather.11.cloned.1.call-done.refs_5_.refs_3_.refs_2_, ...), custom_call_target="tpu_custom_call" | custom-call | flops 1000000 | bytes 1000000 | tf_op jit(solution)/shard_map/gate_up_grad/pallas_call | solution.py:298
  421.8 19.9 %weight_grad.6 = bf16[2048,1536]{1,0:T(8,128)(2,1)} custom-call(s32[12]{0:T(128)} %copy-done.32, bf16[256,2048]{1,0:T(8,128)(2,1)} %get-tuple-element.352.refs_1_, bf16[256,2048]{1,0:T(8,128)(2,1)} %get-tuple-element.279.refs_2_, bf16[256,2048]{1,0:T(8,128)(2,1)} %copy-done.45, bf16[256,2048]{1,0:T(8,128)(2,1)} %copy-done.44, bf16[256,2048]{1,0:T(8,128)(2,1)} %copy-done.43, ...), custom_call_target="tpu_custom_call" | custom-call | flops 1000000 | bytes 1000000 | tf_op jit(solution)/shard_map/weight_grad/pallas_call | solution.py:298
  443.2 9.5 %norm_gradient.2 = (bf16[256,2048]{1,0:T(8,128)(2,1)}, bf16[256,2048]{1,0:T(8,128)(2,1)}, bf16[512,2048]{1,0:T(8,128)(2,1)}, f32[1,2048]{1,0:T(1,128)}) custom-call(bf16[512,2048]{1,0:T(8,128)(2,1)} %refs_0_.5, f32[512,2048]{1,0:T(8,128)} %get-tuple-element.280.refs_1_.refs_0_, bf16[512,2048]{1,0:T(8,128)(2,1)} %get-tuple-element.315.refs_2_, ...), custom_call_target="tpu_custom_call" | custom-call | flops 1000000 | bytes 1000000 | tf_op jit(solution)/shard_map/norm_gradient/pallas_call | solution.py:528
  472.3 8.5 %block_product.17 = (bf16[256,2048]{1,0:T(8,128)(2,1)S(1)}, bf16[256,2048]{1,0:T(8,128)(2,1)S(1)}, bf16[256,2048]{1,0:T(8,128)(2,1)S(1)}, bf16[256,2048]{1,0:T(8,128)(2,1)S(1)}) custom-call(s32[12]{0:T(128)S(1)} %copy-done.33, bf16[1024,1536]{1,0:T(8,128)(2,1)S(1)} %copy-done.7, bf16[1536,2048]{1,0:T(8,128)(2,1)S(1)} %copy-done.6), custom_call_target="tpu_custom_call" | custom-call | flops 1000000 | bytes 1000000 | tf_op jit(solution)/shard_map/block_product/pallas_call | solution.py:298
  507.1 19.9 %weight_grad.7 = bf16[2048,1536]{1,0:T(8,128)(2,1)} custom-call(s32[12]{0:T(128)} %copy-done.32, bf16[256,2048]{1,0:T(8,128)(2,1)} %get-tuple-element.352.refs_1_, bf16[256,2048]{1,0:T(8,128)(2,1)} %get-tuple-element.279.refs_2_, bf16[256,2048]{1,0:T(8,128)(2,1)} %copy-done.45, bf16[256,2048]{1,0:T(8,128)(2,1)} %copy-done.44, bf16[256,2048]{1,0:T(8,128)(2,1)} %copy-done.43, ...), custom_call_target="tpu_custom_call" | custom-call | flops 1000000 | bytes 1000000 | tf_op jit(solution)/shard_map/weight_grad/pallas_call | solution.py:298
  538.0 10.6 %weight_grad.8 = bf16[512,2048]{1,0:T(8,128)(2,1)} custom-call(s32[12]{0:T(128)} %copy-done.32, bf16[2048,512]{1,0:T(8,128)(2,1)} %get-tuple-element.358.refs_1_.refs_2_.refs_3_.refs_4_.refs_5_.refs_6_.refs_7_.refs_8_, bf16[2048,512]{1,0:T(8,128)(2,1)} %get-tuple-element.358.refs_1_.refs_2_.refs_3_.refs_4_.refs_5_.refs_6_.refs_7_.refs_8_, ...), custom_call_target="tpu_custom_call" | custom-call | flops 1000000 | bytes 1000000 | tf_op jit(solution)/shard_map/weight_grad/pallas_call | solution.py:298
  548.5 24.6 %attend_back.2 = (bf16[2048,1024]{1,0:T(8,128)(2,1)}, f32[2,128]{1,0:T(2,128)}) custom-call(s32[4]{0:T(128)} %compare_select_fusion.5.refs_0_, bf16[2048,512]{1,0:T(8,128)(2,1)} %get-tuple-element.368.refs_0_.refs_1_, bf16[2048,256]{1,0:T(8,128)(2,1)} %get-tuple-element.248.refs_1_.refs_2_, bf16[2048,256]{1,0:T(8,128)(2,1)} %get-tuple-element.249.refs_2_.refs_3_, ...), custom_call_target="tpu_custom_call" | custom-call | flops 1000000 | bytes 1000000 | tf_op jit(solution)/shard_map/attend_back/pallas_call | solution.py:857
  579.6 24.7 %attend_back.3 = (bf16[2048,1024]{1,0:T(8,128)(2,1)}, f32[2,128]{1,0:T(2,128)}) custom-call(s32[4]{0:T(128)} %compare_select_fusion.5.refs_0_, bf16[2048,512]{1,0:T(8,128)(2,1)} %get-tuple-element.368.refs_0_.refs_1_, bf16[2048,256]{1,0:T(8,128)(2,1)} %get-tuple-element.248.refs_1_.refs_2_, ...), custom_call_target="tpu_custom_call", output_to_operand_aliasing={{0}: (12, {})} | custom-call | flops 1000000 | bytes 1000000 | tf_op jit(solution)/shard_map/attend_back/pallas_call | solution.py:857
  626.6 16.8 %weight_grad.9 = (bf16[2048,1024]{1,0:T(8,128)(2,1)}, f32[1,2048]{1,0:T(1,128)}) custom-call(s32[12]{0:T(128)} %copy-done.32, bf16[256,2048]{1,0:T(8,128)(2,1)} %copy-done.50, bf16[256,2048]{1,0:T(8,128)(2,1)} %copy-done.49, bf16[256,2048]{1,0:T(8,128)(2,1)} %collective-permute-done.4.refs_1_.refs_3_, bf16[256,2048]{1,0:T(8,128)(2,1)} %copy-done.54, ...), custom_call_target="tpu_custom_call" | custom-call | flops 1000000 | bytes 1000000 | tf_op jit(solution)/shard_map/weight_grad/pallas_call | solution.py:298
  681.5 10.3 %adamw.2 = (f32[256,2,1536]{2,1,0:T(2,128)}, f32[256,2,1536]{2,1,0:T(2,128)}, f32[256,2,1536]{2,1,0:T(2,128)}) custom-call(f32[256,2,1536]{2,1,0:T(2,128)} %refs_0_.6, f32[256,2,1536]{2,1,0:T(2,128)} %refs_1_.3, f32[256,2,1536]{2,1,0:T(2,128)} %refs_2_.2, bf16[256,1536]{1,0:T(8,128)(2,1)} %reduce-scatter.8.cloned.1.call-done.refs_3_, ...), custom_call_target="tpu_custom_call" | custom-call | flops 1000000 | bytes 1000000 | tf_op jit(solution)/shard_map/adamw/pallas_call | solution.py:92
  (365 shorter events, 278.6 us)
Async XLA Ops:
  7.2 52.9 %all-gather.5.cloned.1.call-start = ((), (), s32[]{:S(2)}) async-start(), calls=%async_computation.5 | async-start | bytes 4718592 | tf_op jit(solution)/shard_map/all_gather | solution.py:969
  9.9 118.0 %all-gather.7.cloned.1.call-start = ((), (), s32[]{:S(2)}) async-start(), calls=%async_computation.6 | async-start | bytes 2359296 | tf_op jit(solution)/shard_map/all_gather | solution.py:970
  11.7 205.7 %all-gather.9.cloned.1.call-start = ((), (), s32[]{:S(2)}) async-start(), calls=%async_computation.7 | async-start | bytes 14155776 | tf_op jit(solution)/shard_map/all_gather | solution.py:971
  14.3 302.9 %all-gather.11.cloned.1.call-start = ((), (), s32[]{:S(2)}) async-start(), calls=%async_computation.8 | async-start | bytes 7077888 | tf_op jit(solution)/shard_map/all_gather | solution.py:972
  16.9 474.3 %reduce-scatter.6.cloned.1.call-start = ((), (), s32[]{:S(2)}) async-start(), calls=%async_computation.9 | async-start | bytes 7077888 | tf_op jit(solution)/shard_map/reduce_scatter | solution.py:1043
  18.9 48.8 %collective-permute-start.1 = (bf16[256,2048]{1,0:T(8,128)(2,1)S(1)}, bf16[256,2048]{1,0:T(8,128)(2,1)S(1)}, u32[]{:S(2)}, u32[]{:S(2)}) collective-permute-start(bf16[256,2048]{1,0:T(8,128)(2,1)S(1)} %get-tuple-element.433.refs_2_), channel_id=1, source_target_pairs={{1,0},{3,1},{2,3},{0,2},{5,4},{7,5},{6,7},{4,6},{9,8},{11,9},{10,1... | collective-permute-start | bytes 3145736 | tf_op jit(solution)/shard_map/ppermute | solution.py:144
  22.0 45.8 %collective-permute-start = (bf16[256,2048]{1,0:T(8,128)(2,1)S(1)}, bf16[256,2048]{1,0:T(8,128)(2,1)}, u32[]{:S(2)}, u32[]{:S(2)}) collective-permute-start(bf16[256,2048]{1,0:T(8,128)(2,1)S(1)} %get-tuple-element.379.refs_1_), channel_id=1, source_target_pairs={{0,1},{1,3},{3,2},{2,0},{4,5},{5,7},{7,6},{6,4},{8,9},{9,11},{11,1... | collective-permute-start | bytes 3145736 | tf_op jit(solution)/shard_map/ppermute | solution.py:143
  22.0 48.1 %collective-permute-start.5 = (bf16[256,2048]{1,0:T(8,128)(2,1)S(1)}, bf16[256,2048]{1,0:T(8,128)(2,1)}, u32[]{:S(2)}, u32[]{:S(2)}) collective-permute-start(bf16[256,2048]{1,0:T(8,128)(2,1)S(1)} %get-tuple-element.433.refs_2_), channel_id=1, source_target_pairs={{0,1},{1,3},{3,2},{2,0},{4,5},{5,7},{7,6},{6,4},{8,9},{9,11},{11,1... | collective-permute-start | bytes 3145736 | tf_op jit(solution)/shard_map/ppermute | solution.py:145
  24.0 46.1 %collective-permute-start.4 = (bf16[256,2048]{1,0:T(8,128)(2,1)S(1)}, bf16[256,2048]{1,0:T(8,128)(2,1)}, u32[]{:S(2)}, u32[]{:S(2)}) collective-permute-start(bf16[256,2048]{1,0:T(8,128)(2,1)S(1)} %get-tuple-element.379.refs_1_), channel_id=1, source_target_pairs={{1,0},{3,1},{2,3},{0,2},{5,4},{7,5},{6,7},{4,6},{9,8},{11,9},{10,1... | collective-permute-start | bytes 3145736 | tf_op jit(solution)/shard_map/ppermute | solution.py:146
  94.8 46.2 %collective-permute-start.11 = (bf16[256,2048]{1,0:T(8,128)(2,1)S(1)}, bf16[256,2048]{1,0:T(8,128)(2,1)S(1)}, u32[]{:S(2)}, u32[]{:S(2)}) collective-permute-start(bf16[256,2048]{1,0:T(8,128)(2,1)S(1)} %get-tuple-element.431.refs_10_.refs_2_), channel_id=1, source_target_pairs={{0,1},{1,3},{3,2},{2,0},{4,5},{5,7},{7,6},{6,4},{8,9},{9,11},{11,1... | collective-permute-start | bytes 3145736 | tf_op jit(solution)/shard_map/ppermute | solution.py:145
  96.4 45.2 %collective-permute-start.10 = (bf16[256,2048]{1,0:T(8,128)(2,1)S(1)}, bf16[256,2048]{1,0:T(8,128)(2,1)}, u32[]{:S(2)}, u32[]{:S(2)}) collective-permute-start(bf16[256,2048]{1,0:T(8,128)(2,1)S(1)} %get-tuple-element.431.refs_10_.refs_2_), channel_id=1, source_target_pairs={{1,0},{3,1},{2,3},{0,2},{5,4},{7,5},{6,7},{4,6},{9,8},{11,9},{10,1... | collective-permute-start | bytes 3145736 | tf_op jit(solution)/shard_map/ppermute | solution.py:144
  96.9 46.6 %collective-permute-start.9 = (bf16[256,2048]{1,0:T(8,128)(2,1)S(1)}, bf16[256,2048]{1,0:T(8,128)(2,1)}, u32[]{:S(2)}, u32[]{:S(2)}) collective-permute-start(bf16[256,2048]{1,0:T(8,128)(2,1)S(1)} %get-tuple-element.314.refs_9_.refs_1_), channel_id=1, source_target_pairs={{0,1},{1,3},{3,2},{2,0},{4,5},{5,7},{7,6},{6,4},{8,9},{9,11},{11,1... | collective-permute-start | bytes 3145736 | tf_op jit(solution)/shard_map/ppermute | solution.py:143
  98.5 46.1 %collective-permute-start.8 = (bf16[256,2048]{1,0:T(8,128)(2,1)S(1)}, bf16[256,2048]{1,0:T(8,128)(2,1)}, u32[]{:S(2)}, u32[]{:S(2)}) collective-permute-start(bf16[256,2048]{1,0:T(8,128)(2,1)S(1)} %get-tuple-element.314.refs_9_.refs_1_), channel_id=1, source_target_pairs={{1,0},{3,1},{2,3},{0,2},{5,4},{7,5},{6,7},{4,6},{9,8},{11,9},{10,1... | collective-permute-start | bytes 3145736 | tf_op jit(solution)/shard_map/ppermute | solution.py:146
  141.6 44.9 %collective-permute-start.12 = (bf16[256,2048]{1,0:T(8,128)(2,1)S(1)}, bf16[256,2048]{1,0:T(8,128)(2,1)S(1)}, u32[]{:S(2)}, u32[]{:S(2)}) collective-permute-start(bf16[256,2048]{1,0:T(8,128)(2,1)S(1)} %get-tuple-element.265), channel_id=1, source_target_pairs={{0,1},{1,3},{3,2},{2,0},{4,5},{5,7},{7,6},{6,4},{8,9},{9,11},{11,1... | collective-permute-start | bytes 3145736 | tf_op jit(solution)/shard_map/ppermute | solution.py:199
  228.3 47.7 %collective-permute-start.16 = (bf16[256,2048]{1,0:T(8,128)(2,1)}, bf16[256,2048]{1,0:T(8,128)(2,1)S(1)}, u32[]{:S(2)}, u32[]{:S(2)}) collective-permute-start(bf16[256,2048]{1,0:T(8,128)(2,1)} %get-tuple-element.352.refs_1_), channel_id=1, source_target_pairs={{1,0},{3,1},{2,3},{0,2},{5,4},{7,5},{6,7},{4,6},{9,8},{11,9},{10,1... | collective-permute-start | bytes 3145736 | tf_op jit(solution)/shard_map/ppermute | solution.py:146
  229.7 46.3 %collective-permute-start.19 = (bf16[256,2048]{1,0:T(8,128)(2,1)}, bf16[256,2048]{1,0:T(8,128)(2,1)S(1)}, u32[]{:S(2)}, u32[]{:S(2)}) collective-permute-start(bf16[256,2048]{1,0:T(8,128)(2,1)} %get-tuple-element.279.refs_2_), channel_id=1, source_target_pairs={{0,1},{1,3},{3,2},{2,0},{4,5},{5,7},{7,6},{6,4},{8,9},{9,11},{11,1... | collective-permute-start | bytes 3145736 | tf_op jit(solution)/shard_map/ppermute | solution.py:145
  253.5 45.4 %collective-permute-start.21 = (bf16[256,2048]{1,0:T(8,128)(2,1)S(1)}, bf16[256,2048]{1,0:T(8,128)(2,1)S(1)}, u32[]{:S(2)}, u32[]{:S(2)}) collective-permute-start(bf16[256,2048]{1,0:T(8,128)(2,1)S(1)} %collective-permute-done.18.refs_2_.refs_4_), channel_id=1, source_target_pairs={{1,0},{3,1},{2,3},{0,2},{5,4},{7,5},{6,7},{4,6},{9,8},{11,9},{10,1... | collective-permute-start | bytes 3145736 | tf_op jit(solution)/shard_map/ppermute | solution.py:159
  368.5 235.8 %reduce-scatter.8.cloned.1.call-start = ((), (), s32[]{:S(2)}) async-start(), calls=%async_computation.10 | async-start | bytes 7077888 | tf_op jit(solution)/shard_map/reduce_scatter | solution.py:1062
  443.1 214.7 %reduce-scatter.12.cloned.1.call-start = ((), (), s32[]{:S(2)}) async-start(), calls=%async_computation.12 | async-start | bytes 7077888 | tf_op jit(solution)/shard_map/reduce_scatter | solution.py:1101
  454.7 45.0 %collective-permute-start.34 = (bf16[256,2048]{1,0:T(8,128)(2,1)}, bf16[256,2048]{1,0:T(8,128)(2,1)}, u32[]{:S(2)}, u32[]{:S(2)}) collective-permute-start(bf16[256,2048]{1,0:T(8,128)(2,1)} %get-tuple-element.334.refs_1_.refs_9_), channel_id=1, source_target_pairs={{1,0},{3,1},{2,3},{0,2},{5,4},{7,5},{6,7},{4,6},{9,8},{11,9},{10,1... | collective-permute-start | bytes 3145736 | tf_op jit(solution)/shard_map/ppermute | solution.py:146
  527.1 150.1 %reduce-scatter.10.cloned.1.call-start = ((), (), s32[]{:S(2)}) async-start(), calls=%async_computation.11 | async-start | bytes 2359296 | tf_op jit(solution)/shard_map/reduce_scatter | solution.py:1174
  527.2 46.0 %collective-permute-start.38 = (bf16[256,2048]{1,0:T(8,128)(2,1)}, bf16[256,2048]{1,0:T(8,128)(2,1)}, u32[]{:S(2)}, u32[]{:S(2)}) collective-permute-start(bf16[256,2048]{1,0:T(8,128)(2,1)} %copy-done.40), channel_id=1, source_target_pairs={{0,1},{1,3},{3,2},{2,0},{4,5},{5,7},{7,6},{6,4},{8,9},{9,11},{11,1... | collective-permute-start | bytes 3145736 | tf_op jit(solution)/shard_map/ppermute | solution.py:199
  528.1 45.0 %collective-permute-start.39 = (bf16[256,2048]{1,0:T(8,128)(2,1)}, bf16[256,2048]{1,0:T(8,128)(2,1)}, u32[]{:S(2)}, u32[]{:S(2)}) collective-permute-start(bf16[256,2048]{1,0:T(8,128)(2,1)} %copy-done.39), channel_id=1, source_target_pairs={{1,0},{3,1},{2,3},{0,2},{5,4},{7,5},{6,7},{4,6},{9,8},{11,9},{10,1... | collective-permute-start | bytes 3145736 | tf_op jit(solution)/shard_map/ppermute | solution.py:199
  604.4 103.8 %reduce-scatter.14.cloned.1.call-start = ((), (), s32[]{:S(2)}) async-start(), calls=%async_computation.13 | async-start | bytes 4718592 | tf_op jit(solution)/shard_map/reduce_scatter | solution.py:1176
  (131 other events, 1734.0 us)
Sparse Core Ops, SparseCore 0:
  10.2 49.8 all-gather.4
  62.3 29.5 all-gather.6
  94.1 115.7 all-gather.8
  211.3 63.3 all-gather.10
  368.6 68.1 reduce-scatter.5
  443.2 68.3 reduce-scatter.7
  527.2 68.6 reduce-scatter.11
  604.5 34.4 reduce-scatter.9
  658.1 50.0 reduce-scatter.13

commit v6 on v5

--- a/solution.py
+++ b/solution.py
@@ -1147,32 +1147,35 @@
         in_parts[:] = mark(
             *weight_gradient(table, normeds, ordered_finely(mixed_grad), in_matrix)
         )
+
+    def add_outputs():
         own, lows, highs = sent
-        outputs[:] = mark(
-            *row_kernel_call(
-                add_kernel,
-                "add",
-                [hidden, turn(own)],
-                lows,
-                highs,
-                norm_gains[0:1],
-                (jnp.bfloat16,),
-            ),
-            in_parts[0],
-        )[:1]
+        whole = [hidden, turn(own)]
+        (result,) = row_kernel_call(
+            add_kernel, "add", whole, lows, highs, norm_gains[0:1], (jnp.bfloat16,)
+        )
+        outputs.append(mark(result))
 
     got = []
-    own, lows, highs = ring_scatter(size, normed_group, order, between=in_gradient, got=got)
+    came = []
+    own, lows, highs = ring_scatter(
+        size,
+        normed_group,
+        order,
+        between=in_gradient,
+        after=add_outputs,
+        got=got,
+        came=came,
+        eager=False,
+    )
     if not in_parts:
         in_gradient()
     rows_of_gains = jnp.concatenate([in_parts[1] / norm_gains[0:1], mlp_gain_grad], axis=0)
     gain_sums = jnp.concatenate([rows_of_gains, qknorm_part], axis=1)
     (outputs,) = outputs
-    gain_sums = tie((gain_sums, own, *got))[0]
-    gain_sums = sum_over(gain_sums, "tensor")
     out_part, gate_weight_grad = tie((out_part, gate_weight_grad, sent, mixed_grad))[:2]
     out_grad = lax.psum_scatter(out_part, "dp", scatter_dimension=1, tiled=True)
-    in_part, up_weight_grad = tie((in_parts[0], up_weight_grad, *got))[:2]
+    in_part, up_weight_grad = tie((in_parts[0], up_weight_grad, *came))[:2]
     in_grad = lax.psum_scatter(in_part, "dp", scatter_dimension=0, tiled=True)
     out_grad, gate_weight_grad = tie((out_grad, gate_weight_grad, *got))[:2]
     out_grad = out_grad.astype(jnp.float32)
@@ -1222,7 +1225,8 @@
         input_second_moment,
         MODEL_WIDTH ** (-0.5),
     )
-    gain_sums = sum_over(tie((gain_sums, *lows, *highs))[0], "dp", (input_grad, in_new))
+    gain_sums = sum_over(tie((gain_sums, *lows, *highs))[0], "tensor", (input_grad,))
+    gain_sums = sum_over(gain_sums, "dp", (in_new,))
     norm_grad, qknorm_grad = gain_sums[:, :MODEL_WIDTH], gain_sums[:, MODEL_WIDTH:]
     norm_new, norm_second = adamw(norm_gains, norm_grad, norm_mean, norm_square, gain_rate)
     qknorm_new, qknorm_second = adamw(

time: 731 us -> 724 us (level)
    unnamed x184 -> x182, local copies, waits for them, and re-layouts: 53.3 us -> 50.5 us
  transfers between devices with their start and end apart: 64 -> 64, of which waited for: 22 -> 20; matrix products, arithmetic and copies ran while one was open for 3% -> 3% of each run, Pallas kernels for 50% -> 51%
where the time goes in v6:
time: 724 us; the launch traced here: 714 us
  Pallas kernels  420 us (58%)
  waiting for transfers between devices  142 us (20%)
  starting transfers between devices  59.3 us (8%)
  local copies, waits for them, and re-layouts  51.6 us (7%)
  other arithmetic  25.3 us (3%)
  between operations  15.4 us (2%)
    pallas_call x23, Pallas kernels, row_call(): pl.pallas_call(kernel, grid_spec=pltpu.PrefetchScalarGridSpec(num_scalar_...  254 us
    ppermute x24, waiting for transfers between devices, ring_scatter(): send = lambda value, pairs: lax.ppermute(value, 'tensor', pairs)  63.4 us
    unnamed x182, local copies, waits for them, and re-layouts  50.5 us
    pallas_call x2, Pallas kernels, attention_backward(): pl.pallas_call(lambda *refs: attend_back_kernel(HEAD_WIDTH ** (-0.5), *re...  49.3 us
    pallas_call x4, Pallas kernels, row_kernel_call(): pl.pallas_call(lambda *refs: kernel(split, len(lows), *refs), grid=(2 * s...  32.2 us
    pallas_call x4, Pallas kernels, project(): pl.pallas_call(lambda *refs: project_kernel(len(blocks), *refs), grid_spe...  31.7 us
    all_gather x1, waiting for transfers between devices, local(): in_matrix = lax.all_gather(in_low, 'dp', axis=0, tiled=True)  30.3 us
    ppermute x24, starting transfers between devices, ring_scatter(): send = lambda value, pairs: lax.ppermute(value, 'tensor', pairs)  25.2 us
  transfers between devices with their start and end apart: 64, of which 20 were waited for; matrix products, arithmetic and copies ran while one was open for 3% of the time, Pallas kernels for 51%

profile of v6, /device:TPU:0, one launch (start us, length us, event | category | flops | bytes accessed | tf_op | source)
XLA Modules:
  0.0 714.3 jit_solution(12383539516414257656)
XLA Ops:
  29.7 30.3 %all-gather.5.cloned.1.call-done.refs_3_.refs_2_.refs_17_ = bf16[2048,1024]{1,0:T(8,128)(2,1)} async-done(((bf16[256,1024]{1,0:T(8,128)(2,1)}), bf16[2048,1024]{1,0:T(8,128)(2,1)}) %all-gather.5.cloned.1.call-update) | async-done | bytes 4194320 | tf_op jit(solution)/shard_map/all_gather | solution.py:969
  99.0 8.3 %project.7 = (bf16[2048,512]{1,0:T(8,128)(2,1)}, bf16[2048,256]{1,0:T(8,128)(2,1)}, bf16[2048,256]{1,0:T(8,128)(2,1)}, f32[2048,512]{1,0:T(8,128)}, f32[2048,256]{1,0:T(8,128)}) custom-call(s32[1]{0:T(128)} %bitcast.3.refs_0_, ...), custom_call_target="tpu_custom_call", output_to_operand_aliasing={{0}: (7, {}), {1}: (8, {}), {2}: (9, {}), {3}: (10, {}), {4... | custom-call | flops 1000000 | bytes 1000000 | tf_op jit(solution)/shard_map/project/pallas_call | solution.py:628
  107.3 20.5 %attend.1 = (bf16[2048,512]{1,0:T(8,128)(2,1)}, f32[2,4,2,512]{3,2,1,0:T(2,128)}) custom-call(bf16[2048,512]{1,0:T(8,128)(2,1)} %get-tuple-element.367.refs_0_.refs_1_, bf16[2048,256]{1,0:T(8,128)(2,1)} %get-tuple-element.247.refs_1_.refs_2_, bf16[2048,256]{1,0:T(8,128)(2,1)} %get-tuple-element.248.refs_2_.refs_3_), custom_call_target="tpu_custom_call" | custom-call | flops 1000000 | bytes 1000000 | tf_op jit(solution)/shard_map/attend/pallas_call | solution.py:720
  144.6 21.3 %collective-permute-done.6.refs_2_ = bf16[256,2048]{1,0:T(8,128)(2,1)S(1)} collective-permute-done((bf16[256,2048]{1,0:T(8,128)(2,1)S(1)}, bf16[256,2048]{1,0:T(8,128)(2,1)S(1)}, u32[]{:S(2)}, u32[]{:S(2)}) %collective-permute-start.6) | collective-permute-done | bytes 1048608 | tf_op jit(solution)/shard_map/ppermute | solution.py:199
  167.1 19.3 %collective-permute-done.12.refs_4_ = bf16[256,2048]{1,0:T(8,128)(2,1)S(1)} collective-permute-done((bf16[256,2048]{1,0:T(8,128)(2,1)S(1)}, bf16[256,2048]{1,0:T(8,128)(2,1)S(1)}, u32[]{:S(2)}, u32[]{:S(2)}) %collective-permute-start.12) | collective-permute-done | bytes 1048608 | tf_op jit(solution)/shard_map/ppermute | solution.py:199
  199.3 17.6 %collective-permute-done.14.refs_2_ = bf16[256,2048]{1,0:T(8,128)(2,1)S(1)} collective-permute-done((bf16[256,2048]{1,0:T(8,128)(2,1)}, bf16[256,2048]{1,0:T(8,128)(2,1)S(1)}, u32[]{:S(2)}, u32[]{:S(2)}) %collective-permute-start.14) | collective-permute-done | bytes 1048608 | tf_op jit(solution)/shard_map/ppermute | solution.py:199
  230.3 12.9 %gate_up.3 = (bf16[512,1536]{1,0:T(8,128)(2,1)}, bf16[512,1536]{1,0:T(8,128)(2,1)}, bf16[512,1536]{1,0:T(8,128)(2,1)}) custom-call(s32[12]{0:T(128)} %copy-done.32, bf16[256,2048]{1,0:T(8,128)(2,1)} %get-tuple-element.351.refs_1_, bf16[256,2048]{1,0:T(8,128)(2,1)} %get-tuple-element.278.refs_2_, ...), custom_call_target="tpu_custom_call" | custom-call | flops 1000000 | bytes 1000000 | tf_op jit(solution)/shard_map/gate_up/pallas_call | solution.py:298
  243.2 9.4 %collective-permute-done.17.refs_3_.refs_5_ = bf16[256,2048]{1,0:T(8,128)(2,1)S(1)} collective-permute-done((bf16[256,2048]{1,0:T(8,128)(2,1)}, bf16[256,2048]{1,0:T(8,128)(2,1)S(1)}, u32[]{:S(2)}, u32[]{:S(2)}) %collective-permute-start.17) | collective-permute-done | bytes 1048608 | tf_op jit(solution)/shard_map/ppermute | solution.py:143
  255.9 20.1 %collective-permute-done.16.refs_1_.refs_3_ = bf16[256,2048]{1,0:T(8,128)(2,1)S(1)} collective-permute-done((bf16[256,2048]{1,0:T(8,128)(2,1)}, bf16[256,2048]{1,0:T(8,128)(2,1)S(1)}, u32[]{:S(2)}, u32[]{:S(2)}) %collective-permute-start.16) | collective-permute-done | bytes 1048608 | tf_op jit(solution)/shard_map/ppermute | solution.py:146
  277.9 18.9 %gate_up.4 = (bf16[1024,1536]{1,0:T(8,128)(2,1)}, bf16[1024,1536]{1,0:T(8,128)(2,1)}, bf16[1024,1536]{1,0:T(8,128)(2,1)}) custom-call(s32[12]{0:T(128)} %copy-done.32, bf16[256,2048]{1,0:T(8,128)(2,1)} %copy-done.45, bf16[256,2048]{1,0:T(8,128)(2,1)} %copy-done.44, bf16[256,2048]{1,0:T(8,128)(2,1)} %copy-done.43, bf16[256,2048]{1,0:T(8,128)(2,1)} %copy-done.46, ...), custom_call_target="tpu_custom_call" | custom-call | flops 1000000 | bytes 1000000 | tf_op jit(solution)/shard_map/gate_up/pallas_call | solution.py:298
  300.8 12.9 %gate_up.5 = (bf16[512,1536]{1,0:T(8,128)(2,1)}, bf16[512,1536]{1,0:T(8,128)(2,1)}, bf16[512,1536]{1,0:T(8,128)(2,1)}) custom-call(s32[12]{0:T(128)} %copy-done.32, bf16[256,2048]{1,0:T(8,128)(2,1)} %copy-done.48, bf16[256,2048]{1,0:T(8,128)(2,1)} %copy-done.47, bf16[2048,3072]{1,0:T(8,128)(2,1)} %all-gather.9.cloned.1.call-done.refs_3_.refs_4_.refs_5_.refs_6_.refs_8_, ...), custom_call_target="tpu_custom_call" | custom-call | flops 1000000 | bytes 1000000 | tf_op jit(solution)/shard_map/gate_up/pallas_call | solution.py:298
  317.2 31.2 %gate_up_grad.3 = (bf16[1024,3072]{1,0:T(8,128)(2,1)}, bf16[256,2048]{1,0:T(8,128)(2,1)}, bf16[256,2048]{1,0:T(8,128)(2,1)}, bf16[256,2048]{1,0:T(8,128)(2,1)}, bf16[256,2048]{1,0:T(8,128)(2,1)}) custom-call(s32[12]{0:T(128)} %copy-done.32, bf16[256,2048]{1,0:T(8,128)(2,1)} %collective-permute-done.8.refs_1_.refs_11_, ...), custom_call_target="tpu_custom_call" | custom-call | flops 1000000 | bytes 1000000 | tf_op jit(solution)/shard_map/gate_up_grad/pallas_call | solution.py:298
  348.4 20.0 %weight_grad.5 = bf16[1536,2048]{1,0:T(8,128)(2,1)} custom-call(s32[12]{0:T(128)} %copy-done.32, bf16[512,1536]{1,0:T(8,128)(2,1)} %get-tuple-element.342.refs_1_.refs_2_, bf16[512,1536]{1,0:T(8,128)(2,1)} %get-tuple-element.342.refs_1_.refs_2_, bf16[1024,1536]{1,0:T(8,128)(2,1)} %get-tuple-element.337.refs_3_.refs_4_.refs_5_.refs_6_.refs_1_, ...), custom_call_target="tpu_custom_call" | custom-call | flops 1000000 | bytes 1000000 | tf_op jit(solution)/shard_map/weight_grad/pallas_call | solution.py:298
  371.7 20.0 %gate_up_grad.4 = (bf16[512,3072]{1,0:T(8,128)(2,1)}, bf16[256,2048]{1,0:T(8,128)(2,1)}, bf16[256,2048]{1,0:T(8,128)(2,1)}) custom-call(s32[12]{0:T(128)} %copy-done.32, bf16[256,2048]{1,0:T(8,128)(2,1)} %copy-done.56, bf16[256,2048]{1,0:T(8,128)(2,1)} %collective-permute-done.23.refs_16_.refs_2_, ...), custom_call_target="tpu_custom_call" | custom-call | flops 1000000 | bytes 1000000 | tf_op jit(solution)/shard_map/gate_up_grad/pallas_call | solution.py:298
  393.8 20.3 %gate_up_grad.5 = (bf16[512,3072]{1,0:T(8,128)(2,1)}, bf16[512,2048]{1,0:T(8,128)(2,1)}) custom-call(s32[12]{0:T(128)} %copy-done.32, bf16[256,2048]{1,0:T(8,128)(2,1)} %copy-done.52, bf16[256,2048]{1,0:T(8,128)(2,1)} %copy-done.51, bf16[1536,2048]{1,0:T(8,128)(2,1)} %all-gather.11.cloned.1.call-done.refs_5_.refs_3_.refs_2_, ...), custom_call_target="tpu_custom_call" | custom-call | flops 1000000 | bytes 1000000 | tf_op jit(solution)/shard_map/gate_up_grad/pallas_call | solution.py:298
  421.8 19.9 %weight_grad.6 = bf16[2048,1536]{1,0:T(8,128)(2,1)} custom-call(s32[12]{0:T(128)} %copy-done.32, bf16[256,2048]{1,0:T(8,128)(2,1)} %get-tuple-element.351.refs_1_, bf16[256,2048]{1,0:T(8,128)(2,1)} %get-tuple-element.278.refs_2_, bf16[256,2048]{1,0:T(8,128)(2,1)} %copy-done.45, bf16[256,2048]{1,0:T(8,128)(2,1)} %copy-done.44, bf16[256,2048]{1,0:T(8,128)(2,1)} %copy-done.43, ...), custom_call_target="tpu_custom_call" | custom-call | flops 1000000 | bytes 1000000 | tf_op jit(solution)/shard_map/weight_grad/pallas_call | solution.py:298
  443.2 9.5 %norm_gradient.2 = (bf16[256,2048]{1,0:T(8,128)(2,1)}, bf16[256,2048]{1,0:T(8,128)(2,1)}, bf16[512,2048]{1,0:T(8,128)(2,1)}, f32[1,2048]{1,0:T(1,128)}) custom-call(bf16[512,2048]{1,0:T(8,128)(2,1)} %refs_0_.5, f32[512,2048]{1,0:T(8,128)} %get-tuple-element.279.refs_1_.refs_0_, bf16[512,2048]{1,0:T(8,128)(2,1)} %get-tuple-element.314.refs_2_, ...), custom_call_target="tpu_custom_call" | custom-call | flops 1000000 | bytes 1000000 | tf_op jit(solution)/shard_map/norm_gradient/pallas_call | solution.py:528
  472.2 8.5 %block_product.17 = (bf16[256,2048]{1,0:T(8,128)(2,1)S(1)}, bf16[256,2048]{1,0:T(8,128)(2,1)S(1)}, bf16[256,2048]{1,0:T(8,128)(2,1)S(1)}, bf16[256,2048]{1,0:T(8,128)(2,1)S(1)}) custom-call(s32[12]{0:T(128)S(1)} %copy-done.33, bf16[1024,1536]{1,0:T(8,128)(2,1)S(1)} %copy-done.7, bf16[1536,2048]{1,0:T(8,128)(2,1)S(1)} %copy-done.6), custom_call_target="tpu_custom_call" | custom-call | flops 1000000 | bytes 1000000 | tf_op jit(solution)/shard_map/block_product/pallas_call | solution.py:298
  507.0 19.9 %weight_grad.7 = bf16[2048,1536]{1,0:T(8,128)(2,1)} custom-call(s32[12]{0:T(128)} %copy-done.32, bf16[256,2048]{1,0:T(8,128)(2,1)} %get-tuple-element.351.refs_1_, bf16[256,2048]{1,0:T(8,128)(2,1)} %get-tuple-element.278.refs_2_, bf16[256,2048]{1,0:T(8,128)(2,1)} %copy-done.45, bf16[256,2048]{1,0:T(8,128)(2,1)} %copy-done.44, bf16[256,2048]{1,0:T(8,128)(2,1)} %copy-done.43, ...), custom_call_target="tpu_custom_call" | custom-call | flops 1000000 | bytes 1000000 | tf_op jit(solution)/shard_map/weight_grad/pallas_call | solution.py:298
  537.9 10.6 %weight_grad.8 = bf16[512,2048]{1,0:T(8,128)(2,1)} custom-call(s32[12]{0:T(128)} %copy-done.32, bf16[2048,512]{1,0:T(8,128)(2,1)} %get-tuple-element.357.refs_1_.refs_2_.refs_3_.refs_4_.refs_5_.refs_6_.refs_7_.refs_8_, bf16[2048,512]{1,0:T(8,128)(2,1)} %get-tuple-element.357.refs_1_.refs_2_.refs_3_.refs_4_.refs_5_.refs_6_.refs_7_.refs_8_, ...), custom_call_target="tpu_custom_call" | custom-call | flops 1000000 | bytes 1000000 | tf_op jit(solution)/shard_map/weight_grad/pallas_call | solution.py:298
  548.4 24.6 %attend_back.2 = (bf16[2048,1024]{1,0:T(8,128)(2,1)}, f32[2,128]{1,0:T(2,128)}) custom-call(s32[4]{0:T(128)} %compare_select_fusion.5.refs_0_, bf16[2048,512]{1,0:T(8,128)(2,1)} %get-tuple-element.367.refs_0_.refs_1_, bf16[2048,256]{1,0:T(8,128)(2,1)} %get-tuple-element.247.refs_1_.refs_2_, bf16[2048,256]{1,0:T(8,128)(2,1)} %get-tuple-element.248.refs_2_.refs_3_, ...), custom_call_target="tpu_custom_call" | custom-call | flops 1000000 | bytes 1000000 | tf_op jit(solution)/shard_map/attend_back/pallas_call | solution.py:857
  579.5 24.7 %attend_back.3 = (bf16[2048,1024]{1,0:T(8,128)(2,1)}, f32[2,128]{1,0:T(2,128)}) custom-call(s32[4]{0:T(128)} %compare_select_fusion.5.refs_0_, bf16[2048,512]{1,0:T(8,128)(2,1)} %get-tuple-element.367.refs_0_.refs_1_, bf16[2048,256]{1,0:T(8,128)(2,1)} %get-tuple-element.247.refs_1_.refs_2_, ...), custom_call_target="tpu_custom_call", output_to_operand_aliasing={{0}: (12, {})} | custom-call | flops 1000000 | bytes 1000000 | tf_op jit(solution)/shard_map/attend_back/pallas_call | solution.py:857
  623.2 16.8 %weight_grad.9 = (bf16[2048,1024]{1,0:T(8,128)(2,1)}, f32[1,2048]{1,0:T(1,128)}) custom-call(s32[12]{0:T(128)} %copy-done.32, bf16[256,2048]{1,0:T(8,128)(2,1)} %copy-done.50, bf16[256,2048]{1,0:T(8,128)(2,1)} %copy-done.49, bf16[256,2048]{1,0:T(8,128)(2,1)} %collective-permute-done.4.refs_1_.refs_3_, bf16[256,2048]{1,0:T(8,128)(2,1)} %copy-done.54, ...), custom_call_target="tpu_custom_call" | custom-call | flops 1000000 | bytes 1000000 | tf_op jit(solution)/shard_map/weight_grad/pallas_call | solution.py:298
  668.2 10.3 %adamw.2 = (f32[256,2,1536]{2,1,0:T(2,128)}, f32[256,2,1536]{2,1,0:T(2,128)}, f32[256,2,1536]{2,1,0:T(2,128)}) custom-call(f32[256,2,1536]{2,1,0:T(2,128)} %refs_0_.6, f32[256,2,1536]{2,1,0:T(2,128)} %refs_1_.3, f32[256,2,1536]{2,1,0:T(2,128)} %refs_2_.2, bf16[256,1536]{1,0:T(8,128)(2,1)} %reduce-scatter.8.cloned.1.call-done.refs_3_, ...), custom_call_target="tpu_custom_call" | custom-call | flops 1000000 | bytes 1000000 | tf_op jit(solution)/shard_map/adamw/pallas_call | solution.py:92
  (363 shorter events, 271.3 us)
Async XLA Ops:
  7.2 52.8 %all-gather.5.cloned.1.call-start = ((), (), s32[]{:S(2)}) async-start(), calls=%async_computation.5 | async-start | bytes 4718592 | tf_op jit(solution)/shard_map/all_gather | solution.py:969
  9.9 117.9 %all-gather.7.cloned.1.call-start = ((), (), s32[]{:S(2)}) async-start(), calls=%async_computation.6 | async-start | bytes 2359296 | tf_op jit(solution)/shard_map/all_gather | solution.py:970
  11.7 205.8 %all-gather.9.cloned.1.call-start = ((), (), s32[]{:S(2)}) async-start(), calls=%async_computation.7 | async-start | bytes 14155776 | tf_op jit(solution)/shard_map/all_gather | solution.py:971
  14.3 302.9 %all-gather.11.cloned.1.call-start = ((), (), s32[]{:S(2)}) async-start(), calls=%async_computation.8 | async-start | bytes 7077888 | tf_op jit(solution)/shard_map/all_gather | solution.py:972
  16.9 474.2 %reduce-scatter.6.cloned.1.call-start = ((), (), s32[]{:S(2)}) async-start(), calls=%async_computation.9 | async-start | bytes 7077888 | tf_op jit(solution)/shard_map/reduce_scatter | solution.py:1043
  19.0 48.8 %collective-permute-start.1 = (bf16[256,2048]{1,0:T(8,128)(2,1)S(1)}, bf16[256,2048]{1,0:T(8,128)(2,1)S(1)}, u32[]{:S(2)}, u32[]{:S(2)}) collective-permute-start(bf16[256,2048]{1,0:T(8,128)(2,1)S(1)} %get-tuple-element.431.refs_2_), channel_id=1, source_target_pairs={{1,0},{3,1},{2,3},{0,2},{5,4},{7,5},{6,7},{4,6},{9,8},{11,9},{10,1... | collective-permute-start | bytes 3145736 | tf_op jit(solution)/shard_map/ppermute | solution.py:144
  22.0 45.8 %collective-permute-start = (bf16[256,2048]{1,0:T(8,128)(2,1)S(1)}, bf16[256,2048]{1,0:T(8,128)(2,1)}, u32[]{:S(2)}, u32[]{:S(2)}) collective-permute-start(bf16[256,2048]{1,0:T(8,128)(2,1)S(1)} %get-tuple-element.378.refs_1_), channel_id=1, source_target_pairs={{0,1},{1,3},{3,2},{2,0},{4,5},{5,7},{7,6},{6,4},{8,9},{9,11},{11,1... | collective-permute-start | bytes 3145736 | tf_op jit(solution)/shard_map/ppermute | solution.py:143
  22.0 48.0 %collective-permute-start.5 = (bf16[256,2048]{1,0:T(8,128)(2,1)S(1)}, bf16[256,2048]{1,0:T(8,128)(2,1)}, u32[]{:S(2)}, u32[]{:S(2)}) collective-permute-start(bf16[256,2048]{1,0:T(8,128)(2,1)S(1)} %get-tuple-element.431.refs_2_), channel_id=1, source_target_pairs={{0,1},{1,3},{3,2},{2,0},{4,5},{5,7},{7,6},{6,4},{8,9},{9,11},{11,1... | collective-permute-start | bytes 3145736 | tf_op jit(solution)/shard_map/ppermute | solution.py:145
  24.0 46.1 %collective-permute-start.4 = (bf16[256,2048]{1,0:T(8,128)(2,1)S(1)}, bf16[256,2048]{1,0:T(8,128)(2,1)}, u32[]{:S(2)}, u32[]{:S(2)}) collective-permute-start(bf16[256,2048]{1,0:T(8,128)(2,1)S(1)} %get-tuple-element.378.refs_1_), channel_id=1, source_target_pairs={{1,0},{3,1},{2,3},{0,2},{5,4},{7,5},{6,7},{4,6},{9,8},{11,9},{10,1... | collective-permute-start | bytes 3145736 | tf_op jit(solution)/shard_map/ppermute | solution.py:146
  94.8 46.2 %collective-permute-start.11 = (bf16[256,2048]{1,0:T(8,128)(2,1)S(1)}, bf16[256,2048]{1,0:T(8,128)(2,1)S(1)}, u32[]{:S(2)}, u32[]{:S(2)}) collective-permute-start(bf16[256,2048]{1,0:T(8,128)(2,1)S(1)} %get-tuple-element.429.refs_10_.refs_2_), channel_id=1, source_target_pairs={{0,1},{1,3},{3,2},{2,0},{4,5},{5,7},{7,6},{6,4},{8,9},{9,11},{11,1... | collective-permute-start | bytes 3145736 | tf_op jit(solution)/shard_map/ppermute | solution.py:145
  96.4 45.1 %collective-permute-start.10 = (bf16[256,2048]{1,0:T(8,128)(2,1)S(1)}, bf16[256,2048]{1,0:T(8,128)(2,1)}, u32[]{:S(2)}, u32[]{:S(2)}) collective-permute-start(bf16[256,2048]{1,0:T(8,128)(2,1)S(1)} %get-tuple-element.429.refs_10_.refs_2_), channel_id=1, source_target_pairs={{1,0},{3,1},{2,3},{0,2},{5,4},{7,5},{6,7},{4,6},{9,8},{11,9},{10,1... | collective-permute-start | bytes 3145736 | tf_op jit(solution)/shard_map/ppermute | solution.py:144
  96.8 46.6 %collective-permute-start.9 = (bf16[256,2048]{1,0:T(8,128)(2,1)S(1)}, bf16[256,2048]{1,0:T(8,128)(2,1)}, u32[]{:S(2)}, u32[]{:S(2)}) collective-permute-start(bf16[256,2048]{1,0:T(8,128)(2,1)S(1)} %get-tuple-element.313.refs_9_.refs_1_), channel_id=1, source_target_pairs={{0,1},{1,3},{3,2},{2,0},{4,5},{5,7},{7,6},{6,4},{8,9},{9,11},{11,1... | collective-permute-start | bytes 3145736 | tf_op jit(solution)/shard_map/ppermute | solution.py:143
  98.5 46.1 %collective-permute-start.8 = (bf16[256,2048]{1,0:T(8,128)(2,1)S(1)}, bf16[256,2048]{1,0:T(8,128)(2,1)}, u32[]{:S(2)}, u32[]{:S(2)}) collective-permute-start(bf16[256,2048]{1,0:T(8,128)(2,1)S(1)} %get-tuple-element.313.refs_9_.refs_1_), channel_id=1, source_target_pairs={{1,0},{3,1},{2,3},{0,2},{5,4},{7,5},{6,7},{4,6},{9,8},{11,9},{10,1... | collective-permute-start | bytes 3145736 | tf_op jit(solution)/shard_map/ppermute | solution.py:146
  141.5 44.9 %collective-permute-start.12 = (bf16[256,2048]{1,0:T(8,128)(2,1)S(1)}, bf16[256,2048]{1,0:T(8,128)(2,1)S(1)}, u32[]{:S(2)}, u32[]{:S(2)}) collective-permute-start(bf16[256,2048]{1,0:T(8,128)(2,1)S(1)} %get-tuple-element.264), channel_id=1, source_target_pairs={{0,1},{1,3},{3,2},{2,0},{4,5},{5,7},{7,6},{6,4},{8,9},{9,11},{11,1... | collective-permute-start | bytes 3145736 | tf_op jit(solution)/shard_map/ppermute | solution.py:199
  228.3 47.7 %collective-permute-start.16 = (bf16[256,2048]{1,0:T(8,128)(2,1)}, bf16[256,2048]{1,0:T(8,128)(2,1)S(1)}, u32[]{:S(2)}, u32[]{:S(2)}) collective-permute-start(bf16[256,2048]{1,0:T(8,128)(2,1)} %get-tuple-element.351.refs_1_), channel_id=1, source_target_pairs={{1,0},{3,1},{2,3},{0,2},{5,4},{7,5},{6,7},{4,6},{9,8},{11,9},{10,1... | collective-permute-start | bytes 3145736 | tf_op jit(solution)/shard_map/ppermute | solution.py:146
  229.7 46.3 %collective-permute-start.19 = (bf16[256,2048]{1,0:T(8,128)(2,1)}, bf16[256,2048]{1,0:T(8,128)(2,1)S(1)}, u32[]{:S(2)}, u32[]{:S(2)}) collective-permute-start(bf16[256,2048]{1,0:T(8,128)(2,1)} %get-tuple-element.278.refs_2_), channel_id=1, source_target_pairs={{0,1},{1,3},{3,2},{2,0},{4,5},{5,7},{7,6},{6,4},{8,9},{9,11},{11,1... | collective-permute-start | bytes 3145736 | tf_op jit(solution)/shard_map/ppermute | solution.py:145
  253.5 45.4 %collective-permute-start.21 = (bf16[256,2048]{1,0:T(8,128)(2,1)S(1)}, bf16[256,2048]{1,0:T(8,128)(2,1)S(1)}, u32[]{:S(2)}, u32[]{:S(2)}) collective-permute-start(bf16[256,2048]{1,0:T(8,128)(2,1)S(1)} %collective-permute-done.18.refs_2_.refs_4_), channel_id=1, source_target_pairs={{1,0},{3,1},{2,3},{0,2},{5,4},{7,5},{6,7},{4,6},{9,8},{11,9},{10,1... | collective-permute-start | bytes 3145736 | tf_op jit(solution)/shard_map/ppermute | solution.py:159
  368.5 235.7 %reduce-scatter.8.cloned.1.call-start = ((), (), s32[]{:S(2)}) async-start(), calls=%async_computation.10 | async-start | bytes 7077888 | tf_op jit(solution)/shard_map/reduce_scatter | solution.py:1062
  443.1 197.0 %reduce-scatter.12.cloned.1.call-start = ((), (), s32[]{:S(2)}) async-start(), calls=%async_computation.12 | async-start | bytes 7077888 | tf_op jit(solution)/shard_map/reduce_scatter | solution.py:1101
  454.7 45.0 %collective-permute-start.34 = (bf16[256,2048]{1,0:T(8,128)(2,1)}, bf16[256,2048]{1,0:T(8,128)(2,1)}, u32[]{:S(2)}, u32[]{:S(2)}) collective-permute-start(bf16[256,2048]{1,0:T(8,128)(2,1)} %get-tuple-element.333.refs_1_.refs_9_), channel_id=1, source_target_pairs={{1,0},{3,1},{2,3},{0,2},{5,4},{7,5},{6,7},{4,6},{9,8},{11,9},{10,1... | collective-permute-start | bytes 3145736 | tf_op jit(solution)/shard_map/ppermute | solution.py:146
  527.0 136.9 %reduce-scatter.10.cloned.1.call-start = ((), (), s32[]{:S(2)}) async-start(), calls=%async_computation.11 | async-start | bytes 2359296 | tf_op jit(solution)/shard_map/reduce_scatter | solution.py:1177
  527.1 46.0 %collective-permute-start.38 = (bf16[256,2048]{1,0:T(8,128)(2,1)}, bf16[256,2048]{1,0:T(8,128)(2,1)}, u32[]{:S(2)}, u32[]{:S(2)}) collective-permute-start(bf16[256,2048]{1,0:T(8,128)(2,1)} %copy-done.40), channel_id=1, source_target_pairs={{0,1},{1,3},{3,2},{2,0},{4,5},{5,7},{7,6},{6,4},{8,9},{9,11},{11,1... | collective-permute-start | bytes 3145736 | tf_op jit(solution)/shard_map/ppermute | solution.py:199
  528.0 45.0 %collective-permute-start.39 = (bf16[256,2048]{1,0:T(8,128)(2,1)}, bf16[256,2048]{1,0:T(8,128)(2,1)}, u32[]{:S(2)}, u32[]{:S(2)}) collective-permute-start(bf16[256,2048]{1,0:T(8,128)(2,1)} %copy-done.39), channel_id=1, source_target_pairs={{1,0},{3,1},{2,3},{0,2},{5,4},{7,5},{6,7},{4,6},{9,8},{11,9},{10,1... | collective-permute-start | bytes 3145736 | tf_op jit(solution)/shard_map/ppermute | solution.py:199
  604.3 91.9 %reduce-scatter.14.cloned.1.call-start = ((), (), s32[]{:S(2)}) async-start(), calls=%async_computation.13 | async-start | bytes 4718592 | tf_op jit(solution)/shard_map/reduce_scatter | solution.py:1179
  (130 other events, 1767.2 us)
Sparse Core Ops, SparseCore 0:
  10.2 49.7 all-gather.4
  62.2 29.5 all-gather.6
  94.1 115.7 all-gather.8
  211.3 63.3 all-gather.10
  368.6 68.1 reduce-scatter.5
  443.2 68.3 reduce-scatter.7
  527.1 68.6 reduce-scatter.11
  604.4 34.4 reduce-scatter.9
  641.2 48.7 reduce-scatter.13

commit v7 on v6

--- a/solution.py
+++ b/solution.py
@@ -176,7 +176,7 @@
 
 def relay(terms, got):
     rows, width = terms[0].shape
-    tile = min(rows, 64)
+    tile = min(rows, 128)
     spec = pl.BlockSpec((tile, width), lambda i: (i, 0))
     count = len(terms)
     return pl.pallas_call(
@@ -544,12 +544,12 @@
     gain_ref, sum_ref, low_ref, high_ref = refs[2 * count :]
     values = base_ref[...].astype(jnp.float32) + own_ref[...].astype(jnp.float32)
     values = values + arrived_sum(split, refs[:count], refs[count : 2 * count])
-    sum_ref[...] = values
+    sum_ref[...] = values.astype(sum_ref.dtype)
     put_half(split, low_ref, high_ref, rms_gain(values, gain_ref[...]).astype(jnp.bfloat16))
 
 
 def add_and_norm(base, own, lows, highs, gain):
-    outs = (jnp.float32, "halves")
+    outs = (jnp.bfloat16, "halves")
     return row_kernel_call(add_norm_kernel, "add_norm", [base, own], lows, highs, gain, outs)
 
 

time: 724 us -> 719 us (level)
  no operation moved by 1% of the time
where the time goes in v7:
time: 719 us; the launch traced here: 709 us
  Pallas kernels  415 us (58%)
  waiting for transfers between devices  142 us (20%)
  starting transfers between devices  59.4 us (8%)
  local copies, waits for them, and re-layouts  51.6 us (7%)
  other arithmetic  25.2 us (4%)
  between operations  15.3 us (2%)
    pallas_call x23, Pallas kernels, row_call(): pl.pallas_call(kernel, grid_spec=pltpu.PrefetchScalarGridSpec(num_scalar_...  254 us
    ppermute x24, waiting for transfers between devices, ring_scatter(): send = lambda value, pairs: lax.ppermute(value, 'tensor', pairs)  64 us
    unnamed x182, local copies, waits for them, and re-layouts  50.5 us
    pallas_call x2, Pallas kernels, attention_backward(): pl.pallas_call(lambda *refs: attend_back_kernel(HEAD_WIDTH ** (-0.5), *re...  49.3 us
    pallas_call x4, Pallas kernels, project(): pl.pallas_call(lambda *refs: project_kernel(len(blocks), *refs), grid_spe...  31.7 us
    pallas_call x4, Pallas kernels, row_kernel_call(): pl.pallas_call(lambda *refs: kernel(split, len(lows), *refs), grid=(2 * s...  30.9 us
    all_gather x1, waiting for transfers between devices, local(): in_matrix = lax.all_gather(in_low, 'dp', axis=0, tiled=True)  30.4 us
    ppermute x24, starting transfers between devices, ring_scatter(): send = lambda value, pairs: lax.ppermute(value, 'tensor', pairs)  25.2 us
  transfers between devices with their start and end apart: 64, of which 20 were waited for; matrix products, arithmetic and copies ran while one was open for 3% of the time, Pallas kernels for 51%

profile of v7, /device:TPU:0, one launch (start us, length us, event | category | flops | bytes accessed | tf_op | source)
XLA Modules:
  0.0 709.4 jit_solution(7691793791256934770)
XLA Ops:
  29.7 30.4 %all-gather.5.cloned.1.call-done.refs_3_.refs_2_.refs_17_ = bf16[2048,1024]{1,0:T(8,128)(2,1)} async-done(((bf16[256,1024]{1,0:T(8,128)(2,1)}), bf16[2048,1024]{1,0:T(8,128)(2,1)}) %all-gather.5.cloned.1.call-update) | async-done | bytes 4194320 | tf_op jit(solution)/shard_map/all_gather | solution.py:969
  99.1 8.3 %project.7 = (bf16[2048,512]{1,0:T(8,128)(2,1)}, bf16[2048,256]{1,0:T(8,128)(2,1)}, bf16[2048,256]{1,0:T(8,128)(2,1)}, f32[2048,512]{1,0:T(8,128)}, f32[2048,256]{1,0:T(8,128)}) custom-call(s32[1]{0:T(128)} %bitcast.3.refs_0_, ...), custom_call_target="tpu_custom_call", output_to_operand_aliasing={{0}: (7, {}), {1}: (8, {}), {2}: (9, {}), {3}: (10, {}), {4... | custom-call | flops 1000000 | bytes 1000000 | tf_op jit(solution)/shard_map/project/pallas_call | solution.py:628
  107.4 20.5 %attend.1 = (bf16[2048,512]{1,0:T(8,128)(2,1)}, f32[2,4,2,512]{3,2,1,0:T(2,128)}) custom-call(bf16[2048,512]{1,0:T(8,128)(2,1)} %get-tuple-element.367.refs_0_.refs_1_, bf16[2048,256]{1,0:T(8,128)(2,1)} %get-tuple-element.247.refs_1_.refs_2_, bf16[2048,256]{1,0:T(8,128)(2,1)} %get-tuple-element.248.refs_2_.refs_3_), custom_call_target="tpu_custom_call" | custom-call | flops 1000000 | bytes 1000000 | tf_op jit(solution)/shard_map/attend/pallas_call | solution.py:720
  144.6 21.3 %collective-permute-done.6.refs_2_ = bf16[256,2048]{1,0:T(8,128)(2,1)S(1)} collective-permute-done((bf16[256,2048]{1,0:T(8,128)(2,1)S(1)}, bf16[256,2048]{1,0:T(8,128)(2,1)S(1)}, u32[]{:S(2)}, u32[]{:S(2)}) %collective-permute-start.6) | collective-permute-done | bytes 1048608 | tf_op jit(solution)/shard_map/ppermute | solution.py:199
  167.1 19.4 %collective-permute-done.12.refs_4_ = bf16[256,2048]{1,0:T(8,128)(2,1)S(1)} collective-permute-done((bf16[256,2048]{1,0:T(8,128)(2,1)S(1)}, bf16[256,2048]{1,0:T(8,128)(2,1)S(1)}, u32[]{:S(2)}, u32[]{:S(2)}) %collective-permute-start.12) | collective-permute-done | bytes 1048608 | tf_op jit(solution)/shard_map/ppermute | solution.py:199
  198.1 17.6 %collective-permute-done.14.refs_2_ = bf16[256,2048]{1,0:T(8,128)(2,1)S(1)} collective-permute-done((bf16[256,2048]{1,0:T(8,128)(2,1)}, bf16[256,2048]{1,0:T(8,128)(2,1)S(1)}, u32[]{:S(2)}, u32[]{:S(2)}) %collective-permute-start.14) | collective-permute-done | bytes 1048608 | tf_op jit(solution)/shard_map/ppermute | solution.py:199
  229.0 12.9 %gate_up.3 = (bf16[512,1536]{1,0:T(8,128)(2,1)}, bf16[512,1536]{1,0:T(8,128)(2,1)}, bf16[512,1536]{1,0:T(8,128)(2,1)}) custom-call(s32[12]{0:T(128)} %copy-done.32, bf16[256,2048]{1,0:T(8,128)(2,1)} %get-tuple-element.351.refs_1_, bf16[256,2048]{1,0:T(8,128)(2,1)} %get-tuple-element.278.refs_2_, ...), custom_call_target="tpu_custom_call" | custom-call | flops 1000000 | bytes 1000000 | tf_op jit(solution)/shard_map/gate_up/pallas_call | solution.py:298
  241.9 9.3 %collective-permute-done.17.refs_3_.refs_5_ = bf16[256,2048]{1,0:T(8,128)(2,1)S(1)} collective-permute-done((bf16[256,2048]{1,0:T(8,128)(2,1)}, bf16[256,2048]{1,0:T(8,128)(2,1)S(1)}, u32[]{:S(2)}, u32[]{:S(2)}) %collective-permute-start.17) | collective-permute-done | bytes 1048608 | tf_op jit(solution)/shard_map/ppermute | solution.py:143
  254.3 20.1 %collective-permute-done.16.refs_1_.refs_3_ = bf16[256,2048]{1,0:T(8,128)(2,1)S(1)} collective-permute-done((bf16[256,2048]{1,0:T(8,128)(2,1)}, bf16[256,2048]{1,0:T(8,128)(2,1)S(1)}, u32[]{:S(2)}, u32[]{:S(2)}) %collective-permute-start.16) | collective-permute-done | bytes 1048608 | tf_op jit(solution)/shard_map/ppermute | solution.py:146
  276.3 18.9 %gate_up.4 = (bf16[1024,1536]{1,0:T(8,128)(2,1)}, bf16[1024,1536]{1,0:T(8,128)(2,1)}, bf16[1024,1536]{1,0:T(8,128)(2,1)}) custom-call(s32[12]{0:T(128)} %copy-done.32, bf16[256,2048]{1,0:T(8,128)(2,1)} %copy-done.45, bf16[256,2048]{1,0:T(8,128)(2,1)} %copy-done.44, bf16[256,2048]{1,0:T(8,128)(2,1)} %copy-done.43, bf16[256,2048]{1,0:T(8,128)(2,1)} %copy-done.46, ...), custom_call_target="tpu_custom_call" | custom-call | flops 1000000 | bytes 1000000 | tf_op jit(solution)/shard_map/gate_up/pallas_call | solution.py:298
  299.2 12.9 %gate_up.5 = (bf16[512,1536]{1,0:T(8,128)(2,1)}, bf16[512,1536]{1,0:T(8,128)(2,1)}, bf16[512,1536]{1,0:T(8,128)(2,1)}) custom-call(s32[12]{0:T(128)} %copy-done.32, bf16[256,2048]{1,0:T(8,128)(2,1)} %copy-done.48, bf16[256,2048]{1,0:T(8,128)(2,1)} %copy-done.47, bf16[2048,3072]{1,0:T(8,128)(2,1)} %all-gather.9.cloned.1.call-done.refs_3_.refs_4_.refs_5_.refs_6_.refs_8_, ...), custom_call_target="tpu_custom_call" | custom-call | flops 1000000 | bytes 1000000 | tf_op jit(solution)/shard_map/gate_up/pallas_call | solution.py:298
  315.5 31.2 %gate_up_grad.3 = (bf16[1024,3072]{1,0:T(8,128)(2,1)}, bf16[256,2048]{1,0:T(8,128)(2,1)}, bf16[256,2048]{1,0:T(8,128)(2,1)}, bf16[256,2048]{1,0:T(8,128)(2,1)}, bf16[256,2048]{1,0:T(8,128)(2,1)}) custom-call(s32[12]{0:T(128)} %copy-done.32, bf16[256,2048]{1,0:T(8,128)(2,1)} %collective-permute-done.8.refs_1_.refs_11_, ...), custom_call_target="tpu_custom_call" | custom-call | flops 1000000 | bytes 1000000 | tf_op jit(solution)/shard_map/gate_up_grad/pallas_call | solution.py:298
  346.7 20.1 %weight_grad.5 = bf16[1536,2048]{1,0:T(8,128)(2,1)} custom-call(s32[12]{0:T(128)} %copy-done.32, bf16[512,1536]{1,0:T(8,128)(2,1)} %get-tuple-element.342.refs_1_.refs_2_, bf16[512,1536]{1,0:T(8,128)(2,1)} %get-tuple-element.342.refs_1_.refs_2_, bf16[1024,1536]{1,0:T(8,128)(2,1)} %get-tuple-element.337.refs_3_.refs_4_.refs_5_.refs_6_.refs_1_, ...), custom_call_target="tpu_custom_call" | custom-call | flops 1000000 | bytes 1000000 | tf_op jit(solution)/shard_map/weight_grad/pallas_call | solution.py:298
  370.0 20.0 %gate_up_grad.4 = (bf16[512,3072]{1,0:T(8,128)(2,1)}, bf16[256,2048]{1,0:T(8,128)(2,1)}, bf16[256,2048]{1,0:T(8,128)(2,1)}) custom-call(s32[12]{0:T(128)} %copy-done.32, bf16[256,2048]{1,0:T(8,128)(2,1)} %copy-done.56, bf16[256,2048]{1,0:T(8,128)(2,1)} %collective-permute-done.23.refs_16_.refs_2_, ...), custom_call_target="tpu_custom_call" | custom-call | flops 1000000 | bytes 1000000 | tf_op jit(solution)/shard_map/gate_up_grad/pallas_call | solution.py:298
  392.2 20.2 %gate_up_grad.5 = (bf16[512,3072]{1,0:T(8,128)(2,1)}, bf16[512,2048]{1,0:T(8,128)(2,1)}) custom-call(s32[12]{0:T(128)} %copy-done.32, bf16[256,2048]{1,0:T(8,128)(2,1)} %copy-done.52, bf16[256,2048]{1,0:T(8,128)(2,1)} %copy-done.51, bf16[1536,2048]{1,0:T(8,128)(2,1)} %all-gather.11.cloned.1.call-done.refs_5_.refs_3_.refs_2_, ...), custom_call_target="tpu_custom_call" | custom-call | flops 1000000 | bytes 1000000 | tf_op jit(solution)/shard_map/gate_up_grad/pallas_call | solution.py:298
  419.3 19.9 %weight_grad.6 = bf16[2048,1536]{1,0:T(8,128)(2,1)} custom-call(s32[12]{0:T(128)} %copy-done.32, bf16[256,2048]{1,0:T(8,128)(2,1)} %get-tuple-element.351.refs_1_, bf16[256,2048]{1,0:T(8,128)(2,1)} %get-tuple-element.278.refs_2_, bf16[256,2048]{1,0:T(8,128)(2,1)} %copy-done.45, bf16[256,2048]{1,0:T(8,128)(2,1)} %copy-done.44, bf16[256,2048]{1,0:T(8,128)(2,1)} %copy-done.43, ...), custom_call_target="tpu_custom_call" | custom-call | flops 1000000 | bytes 1000000 | tf_op jit(solution)/shard_map/weight_grad/pallas_call | solution.py:298
  440.6 8.9 %norm_gradient.2 = (bf16[256,2048]{1,0:T(8,128)(2,1)}, bf16[256,2048]{1,0:T(8,128)(2,1)}, bf16[512,2048]{1,0:T(8,128)(2,1)}, f32[1,2048]{1,0:T(1,128)}) custom-call(bf16[512,2048]{1,0:T(8,128)(2,1)} %refs_0_.5, bf16[512,2048]{1,0:T(8,128)(2,1)} %get-tuple-element.279.refs_1_.refs_0_, bf16[512,2048]{1,0:T(8,128)(2,1)} %get-tuple-element.314.refs_2_, ...), custom_call_target="tpu_custom_call" | custom-call | flops 1000000 | bytes 1000000 | tf_op jit(solution)/shard_map/norm_gradient/pallas_call | solution.py:528
  469.1 8.5 %block_product.17 = (bf16[256,2048]{1,0:T(8,128)(2,1)S(1)}, bf16[256,2048]{1,0:T(8,128)(2,1)S(1)}, bf16[256,2048]{1,0:T(8,128)(2,1)S(1)}, bf16[256,2048]{1,0:T(8,128)(2,1)S(1)}) custom-call(s32[12]{0:T(128)S(1)} %copy-done.33, bf16[1024,1536]{1,0:T(8,128)(2,1)S(1)} %copy-done.7, bf16[1536,2048]{1,0:T(8,128)(2,1)S(1)} %copy-done.6), custom_call_target="tpu_custom_call" | custom-call | flops 1000000 | bytes 1000000 | tf_op jit(solution)/shard_map/block_product/pallas_call | solution.py:298
  503.9 19.9 %weight_grad.7 = bf16[2048,1536]{1,0:T(8,128)(2,1)} custom-call(s32[12]{0:T(128)} %copy-done.32, bf16[256,2048]{1,0:T(8,128)(2,1)} %get-tuple-element.351.refs_1_, bf16[256,2048]{1,0:T(8,128)(2,1)} %get-tuple-element.278.refs_2_, bf16[256,2048]{1,0:T(8,128)(2,1)} %copy-done.45, bf16[256,2048]{1,0:T(8,128)(2,1)} %copy-done.44, bf16[256,2048]{1,0:T(8,128)(2,1)} %copy-done.43, ...), custom_call_target="tpu_custom_call" | custom-call | flops 1000000 | bytes 1000000 | tf_op jit(solution)/shard_map/weight_grad/pallas_call | solution.py:298
  534.7 10.6 %weight_grad.8 = bf16[512,2048]{1,0:T(8,128)(2,1)} custom-call(s32[12]{0:T(128)} %copy-done.32, bf16[2048,512]{1,0:T(8,128)(2,1)} %get-tuple-element.357.refs_1_.refs_2_.refs_3_.refs_4_.refs_5_.refs_6_.refs_7_.refs_8_, bf16[2048,512]{1,0:T(8,128)(2,1)} %get-tuple-element.357.refs_1_.refs_2_.refs_3_.refs_4_.refs_5_.refs_6_.refs_7_.refs_8_, ...), custom_call_target="tpu_custom_call" | custom-call | flops 1000000 | bytes 1000000 | tf_op jit(solution)/shard_map/weight_grad/pallas_call | solution.py:298
  545.3 24.6 %attend_back.2 = (bf16[2048,1024]{1,0:T(8,128)(2,1)}, f32[2,128]{1,0:T(2,128)}) custom-call(s32[4]{0:T(128)} %compare_select_fusion.5.refs_0_, bf16[2048,512]{1,0:T(8,128)(2,1)} %get-tuple-element.367.refs_0_.refs_1_, bf16[2048,256]{1,0:T(8,128)(2,1)} %get-tuple-element.247.refs_1_.refs_2_, bf16[2048,256]{1,0:T(8,128)(2,1)} %get-tuple-element.248.refs_2_.refs_3_, ...), custom_call_target="tpu_custom_call" | custom-call | flops 1000000 | bytes 1000000 | tf_op jit(solution)/shard_map/attend_back/pallas_call | solution.py:857
  575.6 24.7 %attend_back.3 = (bf16[2048,1024]{1,0:T(8,128)(2,1)}, f32[2,128]{1,0:T(2,128)}) custom-call(s32[4]{0:T(128)} %compare_select_fusion.5.refs_0_, bf16[2048,512]{1,0:T(8,128)(2,1)} %get-tuple-element.367.refs_0_.refs_1_, bf16[2048,256]{1,0:T(8,128)(2,1)} %get-tuple-element.247.refs_1_.refs_2_, ...), custom_call_target="tpu_custom_call", output_to_operand_aliasing={{0}: (12, {})} | custom-call | flops 1000000 | bytes 1000000 | tf_op jit(solution)/shard_map/attend_back/pallas_call | solution.py:857
  619.2 16.8 %weight_grad.9 = (bf16[2048,1024]{1,0:T(8,128)(2,1)}, f32[1,2048]{1,0:T(1,128)}) custom-call(s32[12]{0:T(128)} %copy-done.32, bf16[256,2048]{1,0:T(8,128)(2,1)} %copy-done.50, bf16[256,2048]{1,0:T(8,128)(2,1)} %copy-done.49, bf16[256,2048]{1,0:T(8,128)(2,1)} %collective-permute-done.4.refs_1_.refs_3_, bf16[256,2048]{1,0:T(8,128)(2,1)} %copy-done.54, ...), custom_call_target="tpu_custom_call" | custom-call | flops 1000000 | bytes 1000000 | tf_op jit(solution)/shard_map/weight_grad/pallas_call | solution.py:298
  662.7 10.3 %adamw.2 = (f32[256,2,1536]{2,1,0:T(2,128)}, f32[256,2,1536]{2,1,0:T(2,128)}, f32[256,2,1536]{2,1,0:T(2,128)}) custom-call(f32[256,2,1536]{2,1,0:T(2,128)} %refs_0_.6, f32[256,2,1536]{2,1,0:T(2,128)} %refs_1_.3, f32[256,2,1536]{2,1,0:T(2,128)} %refs_2_.2, bf16[256,1536]{1,0:T(8,128)(2,1)} %reduce-scatter.8.cloned.1.call-done.refs_3_, ...), custom_call_target="tpu_custom_call" | custom-call | flops 1000000 | bytes 1000000 | tf_op jit(solution)/shard_map/adamw/pallas_call | solution.py:92
  (363 shorter events, 266.7 us)
Async XLA Ops:
  7.2 52.9 %all-gather.5.cloned.1.call-start = ((), (), s32[]{:S(2)}) async-start(), calls=%async_computation.5 | async-start | bytes 4718592 | tf_op jit(solution)/shard_map/all_gather | solution.py:969
  9.9 118.0 %all-gather.7.cloned.1.call-start = ((), (), s32[]{:S(2)}) async-start(), calls=%async_computation.6 | async-start | bytes 2359296 | tf_op jit(solution)/shard_map/all_gather | solution.py:970
  11.7 204.6 %all-gather.9.cloned.1.call-start = ((), (), s32[]{:S(2)}) async-start(), calls=%async_computation.7 | async-start | bytes 14155776 | tf_op jit(solution)/shard_map/all_gather | solution.py:971
  14.3 301.2 %all-gather.11.cloned.1.call-start = ((), (), s32[]{:S(2)}) async-start(), calls=%async_computation.8 | async-start | bytes 7077888 | tf_op jit(solution)/shard_map/all_gather | solution.py:972
  16.9 471.2 %reduce-scatter.6.cloned.1.call-start = ((), (), s32[]{:S(2)}) async-start(), calls=%async_computation.9 | async-start | bytes 7077888 | tf_op jit(solution)/shard_map/reduce_scatter | solution.py:1043
  18.9 48.9 %collective-permute-start.1 = (bf16[256,2048]{1,0:T(8,128)(2,1)S(1)}, bf16[256,2048]{1,0:T(8,128)(2,1)S(1)}, u32[]{:S(2)}, u32[]{:S(2)}) collective-permute-start(bf16[256,2048]{1,0:T(8,128)(2,1)S(1)} %get-tuple-element.431.refs_2_), channel_id=1, source_target_pairs={{1,0},{3,1},{2,3},{0,2},{5,4},{7,5},{6,7},{4,6},{9,8},{11,9},{10,1... | collective-permute-start | bytes 3145736 | tf_op jit(solution)/shard_map/ppermute | solution.py:144
  21.9 45.9 %collective-permute-start = (bf16[256,2048]{1,0:T(8,128)(2,1)S(1)}, bf16[256,2048]{1,0:T(8,128)(2,1)}, u32[]{:S(2)}, u32[]{:S(2)}) collective-permute-start(bf16[256,2048]{1,0:T(8,128)(2,1)S(1)} %get-tuple-element.378.refs_1_), channel_id=1, source_target_pairs={{0,1},{1,3},{3,2},{2,0},{4,5},{5,7},{7,6},{6,4},{8,9},{9,11},{11,1... | collective-permute-start | bytes 3145736 | tf_op jit(solution)/shard_map/ppermute | solution.py:143
  22.0 48.1 %collective-permute-start.5 = (bf16[256,2048]{1,0:T(8,128)(2,1)S(1)}, bf16[256,2048]{1,0:T(8,128)(2,1)}, u32[]{:S(2)}, u32[]{:S(2)}) collective-permute-start(bf16[256,2048]{1,0:T(8,128)(2,1)S(1)} %get-tuple-element.431.refs_2_), channel_id=1, source_target_pairs={{0,1},{1,3},{3,2},{2,0},{4,5},{5,7},{7,6},{6,4},{8,9},{9,11},{11,1... | collective-permute-start | bytes 3145736 | tf_op jit(solution)/shard_map/ppermute | solution.py:145
  23.9 46.2 %collective-permute-start.4 = (bf16[256,2048]{1,0:T(8,128)(2,1)S(1)}, bf16[256,2048]{1,0:T(8,128)(2,1)}, u32[]{:S(2)}, u32[]{:S(2)}) collective-permute-start(bf16[256,2048]{1,0:T(8,128)(2,1)S(1)} %get-tuple-element.378.refs_1_), channel_id=1, source_target_pairs={{1,0},{3,1},{2,3},{0,2},{5,4},{7,5},{6,7},{4,6},{9,8},{11,9},{10,1... | collective-permute-start | bytes 3145736 | tf_op jit(solution)/shard_map/ppermute | solution.py:146
  94.8 46.2 %collective-permute-start.11 = (bf16[256,2048]{1,0:T(8,128)(2,1)S(1)}, bf16[256,2048]{1,0:T(8,128)(2,1)S(1)}, u32[]{:S(2)}, u32[]{:S(2)}) collective-permute-start(bf16[256,2048]{1,0:T(8,128)(2,1)S(1)} %get-tuple-element.429.refs_10_.refs_2_), channel_id=1, source_target_pairs={{0,1},{1,3},{3,2},{2,0},{4,5},{5,7},{7,6},{6,4},{8,9},{9,11},{11,1... | collective-permute-start | bytes 3145736 | tf_op jit(solution)/shard_map/ppermute | solution.py:145
  96.4 45.2 %collective-permute-start.10 = (bf16[256,2048]{1,0:T(8,128)(2,1)S(1)}, bf16[256,2048]{1,0:T(8,128)(2,1)}, u32[]{:S(2)}, u32[]{:S(2)}) collective-permute-start(bf16[256,2048]{1,0:T(8,128)(2,1)S(1)} %get-tuple-element.429.refs_10_.refs_2_), channel_id=1, source_target_pairs={{1,0},{3,1},{2,3},{0,2},{5,4},{7,5},{6,7},{4,6},{9,8},{11,9},{10,1... | collective-permute-start | bytes 3145736 | tf_op jit(solution)/shard_map/ppermute | solution.py:144
  96.9 46.6 %collective-permute-start.9 = (bf16[256,2048]{1,0:T(8,128)(2,1)S(1)}, bf16[256,2048]{1,0:T(8,128)(2,1)}, u32[]{:S(2)}, u32[]{:S(2)}) collective-permute-start(bf16[256,2048]{1,0:T(8,128)(2,1)S(1)} %get-tuple-element.313.refs_9_.refs_1_), channel_id=1, source_target_pairs={{0,1},{1,3},{3,2},{2,0},{4,5},{5,7},{7,6},{6,4},{8,9},{9,11},{11,1... | collective-permute-start | bytes 3145736 | tf_op jit(solution)/shard_map/ppermute | solution.py:143
  98.5 46.1 %collective-permute-start.8 = (bf16[256,2048]{1,0:T(8,128)(2,1)S(1)}, bf16[256,2048]{1,0:T(8,128)(2,1)}, u32[]{:S(2)}, u32[]{:S(2)}) collective-permute-start(bf16[256,2048]{1,0:T(8,128)(2,1)S(1)} %get-tuple-element.313.refs_9_.refs_1_), channel_id=1, source_target_pairs={{1,0},{3,1},{2,3},{0,2},{5,4},{7,5},{6,7},{4,6},{9,8},{11,9},{10,1... | collective-permute-start | bytes 3145736 | tf_op jit(solution)/shard_map/ppermute | solution.py:146
  141.6 44.9 %collective-permute-start.12 = (bf16[256,2048]{1,0:T(8,128)(2,1)S(1)}, bf16[256,2048]{1,0:T(8,128)(2,1)S(1)}, u32[]{:S(2)}, u32[]{:S(2)}) collective-permute-start(bf16[256,2048]{1,0:T(8,128)(2,1)S(1)} %get-tuple-element.264), channel_id=1, source_target_pairs={{0,1},{1,3},{3,2},{2,0},{4,5},{5,7},{7,6},{6,4},{8,9},{9,11},{11,1... | collective-permute-start | bytes 3145736 | tf_op jit(solution)/shard_map/ppermute | solution.py:199
  226.9 47.4 %collective-permute-start.16 = (bf16[256,2048]{1,0:T(8,128)(2,1)}, bf16[256,2048]{1,0:T(8,128)(2,1)S(1)}, u32[]{:S(2)}, u32[]{:S(2)}) collective-permute-start(bf16[256,2048]{1,0:T(8,128)(2,1)} %get-tuple-element.351.refs_1_), channel_id=1, source_target_pairs={{1,0},{3,1},{2,3},{0,2},{5,4},{7,5},{6,7},{4,6},{9,8},{11,9},{10,1... | collective-permute-start | bytes 3145736 | tf_op jit(solution)/shard_map/ppermute | solution.py:146
  228.3 46.1 %collective-permute-start.19 = (bf16[256,2048]{1,0:T(8,128)(2,1)}, bf16[256,2048]{1,0:T(8,128)(2,1)S(1)}, u32[]{:S(2)}, u32[]{:S(2)}) collective-permute-start(bf16[256,2048]{1,0:T(8,128)(2,1)} %get-tuple-element.278.refs_2_), channel_id=1, source_target_pairs={{0,1},{1,3},{3,2},{2,0},{4,5},{5,7},{7,6},{6,4},{8,9},{9,11},{11,1... | collective-permute-start | bytes 3145736 | tf_op jit(solution)/shard_map/ppermute | solution.py:145
  251.8 45.4 %collective-permute-start.21 = (bf16[256,2048]{1,0:T(8,128)(2,1)S(1)}, bf16[256,2048]{1,0:T(8,128)(2,1)S(1)}, u32[]{:S(2)}, u32[]{:S(2)}) collective-permute-start(bf16[256,2048]{1,0:T(8,128)(2,1)S(1)} %collective-permute-done.18.refs_2_.refs_4_), channel_id=1, source_target_pairs={{1,0},{3,1},{2,3},{0,2},{5,4},{7,5},{6,7},{4,6},{9,8},{11,9},{10,1... | collective-permute-start | bytes 3145736 | tf_op jit(solution)/shard_map/ppermute | solution.py:159
  366.8 233.5 %reduce-scatter.8.cloned.1.call-start = ((), (), s32[]{:S(2)}) async-start(), calls=%async_computation.10 | async-start | bytes 7077888 | tf_op jit(solution)/shard_map/reduce_scatter | solution.py:1062
  440.6 195.5 %reduce-scatter.12.cloned.1.call-start = ((), (), s32[]{:S(2)}) async-start(), calls=%async_computation.12 | async-start | bytes 7077888 | tf_op jit(solution)/shard_map/reduce_scatter | solution.py:1101
  451.5 45.0 %collective-permute-start.34 = (bf16[256,2048]{1,0:T(8,128)(2,1)}, bf16[256,2048]{1,0:T(8,128)(2,1)}, u32[]{:S(2)}, u32[]{:S(2)}) collective-permute-start(bf16[256,2048]{1,0:T(8,128)(2,1)} %get-tuple-element.333.refs_1_.refs_9_), channel_id=1, source_target_pairs={{1,0},{3,1},{2,3},{0,2},{5,4},{7,5},{6,7},{4,6},{9,8},{11,9},{10,1... | collective-permute-start | bytes 3145736 | tf_op jit(solution)/shard_map/ppermute | solution.py:146
  523.9 134.6 %reduce-scatter.10.cloned.1.call-start = ((), (), s32[]{:S(2)}) async-start(), calls=%async_computation.11 | async-start | bytes 2359296 | tf_op jit(solution)/shard_map/reduce_scatter | solution.py:1177
  523.9 46.0 %collective-permute-start.38 = (bf16[256,2048]{1,0:T(8,128)(2,1)}, bf16[256,2048]{1,0:T(8,128)(2,1)}, u32[]{:S(2)}, u32[]{:S(2)}) collective-permute-start(bf16[256,2048]{1,0:T(8,128)(2,1)} %copy-done.40), channel_id=1, source_target_pairs={{0,1},{1,3},{3,2},{2,0},{4,5},{5,7},{7,6},{6,4},{8,9},{9,11},{11,1... | collective-permute-start | bytes 3145736 | tf_op jit(solution)/shard_map/ppermute | solution.py:199
  525.1 44.8 %collective-permute-start.39 = (bf16[256,2048]{1,0:T(8,128)(2,1)}, bf16[256,2048]{1,0:T(8,128)(2,1)}, u32[]{:S(2)}, u32[]{:S(2)}) collective-permute-start(bf16[256,2048]{1,0:T(8,128)(2,1)} %copy-done.39), channel_id=1, source_target_pairs={{1,0},{3,1},{2,3},{0,2},{5,4},{7,5},{6,7},{4,6},{9,8},{11,9},{10,1... | collective-permute-start | bytes 3145736 | tf_op jit(solution)/shard_map/ppermute | solution.py:199
  600.3 90.9 %reduce-scatter.14.cloned.1.call-start = ((), (), s32[]{:S(2)}) async-start(), calls=%async_computation.13 | async-start | bytes 4718592 | tf_op jit(solution)/shard_map/reduce_scatter | solution.py:1179
  (130 other events, 1730.6 us)
Sparse Core Ops, SparseCore 0:
  10.2 49.8 all-gather.4
  62.3 29.5 all-gather.6
  94.1 115.7 all-gather.8
  211.3 63.3 all-gather.10
  366.9 68.1 reduce-scatter.5
  440.4 68.3 reduce-scatter.7
  524.0 68.6 reduce-scatter.11
  600.5 34.6 reduce-scatter.9
  637.4 48.6 reduce-scatter.13
